TPU v7x, 32 devices: a whole 2x2x4 slice. The times are simulated.
32 devices in a mesh: dp: 4 (over x, core), blk: 4 (over z), heads: 2 (over y).
Axes of the slice: x: 2, y: 2, z: 4, core: 2. Of those that a mesh axis runs over, the one named last changes fastest.
Arguments:
- hidden_in: bfloat16 [6144, 2048], P(('dp', 'blk')), may hold values from -6 to 6
- memory: bfloat16 [6144, 2048], P(('dp', 'blk')), may hold values from -6 to 6
- lengths: int32 [4, 4], P('dp'), may hold values from 1 to 1344, 1536 in all within a row
- query_weight: bfloat16 [2048, 2048], P(('dp', 'blk'), 'heads'), may hold values from -0.125 to 0.125
- key_weight: bfloat16 [2048, 2048], P(('dp', 'blk'), 'heads'), may hold values from -0.125 to 0.125
- value_weight: bfloat16 [2048, 2048], P(('dp', 'blk'), 'heads'), may hold values from -0.125 to 0.125
- output_weight: bfloat16 [2048, 2048], P(('dp', 'blk'), 'heads'), may hold values from -3 to 3
- gate_weight: bfloat16 [2048, 5504], P(('dp', 'blk'), 'heads'), may hold values from -0.125 to 0.125
- up_weight: bfloat16 [2048, 5504], P(('dp', 'blk'), 'heads'), may hold values from -0.125 to 0.125
- down_weight: bfloat16 [2048, 5504], P(('dp', 'blk'), 'heads'), may hold values from -0.078125 to 0.078125
- attention_gain: bfloat16 [2048], P(('dp', 'blk')), may hold values from 0.099609375 to 1.8984375
- memory_gain: bfloat16 [2048], P(('dp', 'blk')), may hold values from 0.099609375 to 1.8984375
- feedforward_gain: bfloat16 [2048], P(('dp', 'blk')), may hold values from 0.099609375 to 1.8984375
- cotangent: bfloat16 [6144, 2048], P(('dp', 'blk')), may hold values from -6 to 6
Outputs:
- output: bfloat16 [6144, 2048], P(('dp', 'blk'))
- hidden_grad: float32 [6144, 2048], P(('dp', 'blk'))
- memory_grad: float32 [6144, 2048], P(('dp', 'blk'))
- query_weight_grad: float32 [2048, 2048], P(('dp', 'blk'), 'heads')
- key_weight_grad: float32 [2048, 2048], P(('dp', 'blk'), 'heads')
- value_weight_grad: float32 [2048, 2048], P(('dp', 'blk'), 'heads')
- output_weight_grad: float32 [2048, 2048], P(('dp', 'blk'), 'heads')
- gate_weight_grad: float32 [2048, 5504], P(('dp', 'blk'), 'heads')
- up_weight_grad: float32 [2048, 5504], P(('dp', 'blk'), 'heads')
- down_weight_grad: float32 [2048, 5504], P(('dp', 'blk'), 'heads')
- attention_gain_grad: float32 [2048], P(('dp', 'blk'))
- memory_gain_grad: float32 [2048], P(('dp', 'blk'))
- feedforward_gain_grad: float32 [2048], P(('dp', 'blk'))
Inputs may be any that keep to these rules, and one draw needn't show every extreme that they name: Each row of lengths sums to 1536, and its largest entry is exactly 1344.
All inputs are finite; a program needn't handle non-finite values.
Results may differ from a plain program's by a relative error of at most 0.02.
Values may be sent and summed in bfloat16 or wider, within the bound.
A program may use at most 384 MiB of HBM per device.

v0:
```python
import math

import jax
import jax.numpy as jnp
from jax import lax
from jax.sharding import PartitionSpec as P

HEAD = 128


EPSILON = 1e-06
NEGATIVE = -1e30


def rms_scale(values, gain):
    return values * lax.rsqrt(jnp.mean(values * values, axis=-1, keepdims=True) + EPSILON) * gain


def plain_dot(left, right):
    return jnp.dot(left, right, preferred_element_type=jnp.float32)


def dot_rows(left, right):
    return lax.dot_general(
        left, right, (((1,), (1,)), ((), ())), preferred_element_type=jnp.float32
    )


def dot_cols(left, right):
    return lax.dot_general(
        left, right, (((0,), (0,)), ((), ())), preferred_element_type=jnp.float32
    )


def doc_number(positions, doc_ends):
    return jnp.sum((positions[:, None] >= doc_ends[None, :]).astype(jnp.int32), axis=1)


def local(
    hidden_in,
    memory,
    lengths,
    query_weight,
    key_weight,
    value_weight,
    output_weight,
    gate_weight,
    up_weight,
    down_weight,
    attention_gain,
    memory_gain,
    feedforward_gain,
    cotangent,
):
    rows = hidden_in.shape[0]
    blocks = lax.axis_size("blk")
    first_row = lax.axis_index("blk") * rows
    last_row = first_row + rows - 1
    query_pos = first_row + jnp.arange(rows, dtype=jnp.int32)
    doc_ends = jnp.cumsum(lengths[0], dtype=jnp.int32)
    query_doc = doc_number(query_pos, doc_ends)
    factor = 1.0 / math.sqrt(HEAD)
    attn_set = (
        lax.all_gather(query_weight, ("dp", "blk"), axis=0, tiled=True),
        lax.all_gather(key_weight, ("dp", "blk"), axis=0, tiled=True),
        lax.all_gather(value_weight, ("dp", "blk"), axis=0, tiled=True),
        lax.all_gather(output_weight, ("dp", "blk"), axis=0, tiled=True),
        lax.all_gather(attention_gain, ("dp", "blk"), axis=0, tiled=True),
        lax.all_gather(memory_gain, ("dp", "blk"), axis=0, tiled=True),
    )
    full_query, full_key, full_value, full_output = (
        attn_set[0],
        attn_set[1],
        attn_set[2],
        attn_set[3],
    )
    input_gain = attn_set[4].astype(jnp.float32)
    source_gain = attn_set[5].astype(jnp.float32)
    heads_local = full_query.shape[1] // HEAD
    width_local = full_query.shape[1]
    hidden_float = hidden_in.astype(jnp.float32)
    memory_float = memory.astype(jnp.float32)
    memory_low = rms_scale(memory_float, source_gain).astype(jnp.bfloat16)
    key_low = plain_dot(memory_low, full_key).astype(jnp.bfloat16)
    value_low = plain_dot(memory_low, full_value).astype(jnp.bfloat16)
    normed_low = rms_scale(hidden_float, input_gain).astype(jnp.bfloat16)
    query_low = plain_dot(normed_low, full_query).astype(jnp.bfloat16)
    query_heads = query_low.reshape(rows, heads_local, HEAD)

    def score_tile(key_piece):
        span = key_piece.shape[0]
        key_pos = jnp.arange(span, dtype=jnp.int32)
        allowed = (key_pos[None, :] <= query_pos[:, None]) & (
            doc_number(key_pos, doc_ends)[None, :] == query_doc[:, None]
        )
        key_heads = key_piece.reshape(span, heads_local, HEAD)
        scores = (
            jnp.einsum("qhd,khd->hqk", query_heads, key_heads, preferred_element_type=jnp.float32)
            * factor
        )
        return (scores, allowed, key_heads)

    start_state = (
        jnp.full((heads_local, rows), NEGATIVE, jnp.float32),
        jnp.zeros((heads_local, rows), jnp.float32),
        jnp.zeros((rows, heads_local, HEAD), jnp.float32),
    )
    piece = (
        lax.all_gather(key_low, "blk", axis=0, tiled=True),
        lax.all_gather(value_low, "blk", axis=0, tiled=True),
    )

    def forward_compute(state):
        running_max, running_sum, running_acc = state
        scores, allowed, key_heads = score_tile(piece[0])
        span = piece[1].shape[0]
        value_heads = piece[1].reshape(span, heads_local, HEAD)
        masked = jnp.where(allowed[None], scores, NEGATIVE)
        new_max = jnp.maximum(running_max, jnp.max(masked, axis=-1))
        weights = jnp.where(allowed[None], jnp.exp(masked - new_max[..., None]), 0.0)
        rescale = jnp.exp(running_max - new_max)
        new_sum = jnp.sum(weights, axis=-1)
        added = jnp.einsum(
            "hqk,khd->qhd",
            weights.astype(jnp.bfloat16),
            value_heads,
            preferred_element_type=jnp.float32,
        )
        new_acc = running_acc * rescale.T[:, :, None] + added
        return (new_max, new_sum, new_acc)

    final_state = lax.cond(
        jnp.int32(0) > last_row, lambda state: state, forward_compute, start_state
    )
    context = final_state[2] / final_state[1].T[:, :, None]
    log_total = final_state[0] + jnp.log(final_state[1])
    context_low = context.reshape(rows, width_local).astype(jnp.bfloat16)
    attn_part = dot_rows(context_low, full_output)
    attended = hidden_float + lax.psum(attn_part.astype(jnp.bfloat16), "heads").astype(jnp.float32)
    ffn_set = (
        lax.all_gather(gate_weight, ("dp", "blk"), axis=0, tiled=True),
        lax.all_gather(up_weight, ("dp", "blk"), axis=0, tiled=True),
        lax.all_gather(down_weight, ("dp", "blk"), axis=0, tiled=True),
        lax.all_gather(feedforward_gain, ("dp", "blk"), axis=0, tiled=True),
    )
    full_gate, full_up, full_down = (ffn_set[0], ffn_set[1], ffn_set[2])
    mid_gain = ffn_set[3].astype(jnp.float32)
    mid_low = rms_scale(attended, mid_gain).astype(jnp.bfloat16)
    gate = plain_dot(mid_low, full_gate)
    upward = plain_dot(mid_low, full_up)
    sigma = jax.nn.sigmoid(gate)
    silu_gate = gate * sigma
    act_low = (silu_gate * upward).astype(jnp.bfloat16)
    ffn_part = dot_rows(act_low, full_down)
    output = (
        attended + lax.psum(ffn_part.astype(jnp.bfloat16), "heads").astype(jnp.float32)
    ).astype(jnp.bfloat16)
    ffn_back = (
        lax.all_gather(gate_weight, ("dp", "blk"), axis=0, tiled=True),
        lax.all_gather(up_weight, ("dp", "blk"), axis=0, tiled=True),
        lax.all_gather(down_weight, ("dp", "blk"), axis=0, tiled=True),
        lax.all_gather(feedforward_gain, ("dp", "blk"), axis=0, tiled=True),
    )
    back_gate, back_up, back_down = (ffn_back[0], ffn_back[1], ffn_back[2])
    back_mid_gain = ffn_back[3].astype(jnp.float32)
    cot_float = cotangent.astype(jnp.float32)
    down_grad = dot_cols(cotangent, act_low)
    act_grad = plain_dot(cotangent, back_down)
    gate_grad_low = (act_grad * upward * sigma * (1.0 + gate * (1.0 - sigma))).astype(jnp.bfloat16)
    up_grad_low = (act_grad * silu_gate).astype(jnp.bfloat16)
    gate_wgrad = dot_cols(mid_low, gate_grad_low)
    up_wgrad = dot_cols(mid_low, up_grad_low)
    mid_part = dot_rows(gate_grad_low, back_gate) + dot_rows(up_grad_low, back_up)
    mid_grad = lax.psum(mid_part.astype(jnp.bfloat16), "heads").astype(jnp.float32)
    mid_pull = jax.vjp(rms_scale, attended, back_mid_gain)[1]
    attended_norm_grad, mid_gain_grad = mid_pull(mid_grad)
    attended_grad = cot_float + attended_norm_grad
    ffn_shares = (
        lax.psum_scatter(gate_wgrad, ("dp", "blk"), scatter_dimension=0, tiled=True),
        lax.psum_scatter(up_wgrad, ("dp", "blk"), scatter_dimension=0, tiled=True),
        lax.psum_scatter(down_grad, ("dp", "blk"), scatter_dimension=0, tiled=True),
        lax.psum_scatter(mid_gain_grad, ("dp", "blk"), scatter_dimension=0, tiled=True),
    )
    attn_back = (
        lax.all_gather(query_weight, ("dp", "blk"), axis=0, tiled=True),
        lax.all_gather(key_weight, ("dp", "blk"), axis=0, tiled=True),
        lax.all_gather(value_weight, ("dp", "blk"), axis=0, tiled=True),
        lax.all_gather(output_weight, ("dp", "blk"), axis=0, tiled=True),
        lax.all_gather(attention_gain, ("dp", "blk"), axis=0, tiled=True),
        lax.all_gather(memory_gain, ("dp", "blk"), axis=0, tiled=True),
    )
    back_query, back_key, back_value, back_output = (
        attn_back[0],
        attn_back[1],
        attn_back[2],
        attn_back[3],
    )
    back_input_gain = attn_back[4].astype(jnp.float32)
    back_source_gain = attn_back[5].astype(jnp.float32)
    resid_low = attended_grad.astype(jnp.bfloat16)
    output_wgrad = dot_cols(resid_low, context_low)
    context_grad_low = plain_dot(resid_low, back_output).astype(jnp.bfloat16)
    context_grad_heads = context_grad_low.reshape(rows, heads_local, HEAD)
    delta = jnp.sum(context_grad_heads.astype(jnp.float32) * context, axis=-1).T

    def tile_grads(key_piece, value_piece):
        scores, allowed, key_heads = score_tile(key_piece)
        span = value_piece.shape[0]
        value_heads = value_piece.reshape(span, heads_local, HEAD)
        probs = jnp.where(allowed[None], jnp.exp(scores - log_total[..., None]), 0.0)
        probs_low = probs.astype(jnp.bfloat16)
        prob_grad = jnp.einsum(
            "qhd,khd->hqk", context_grad_heads, value_heads, preferred_element_type=jnp.float32
        )
        score_grad = (probs * (prob_grad - delta[..., None])).astype(jnp.bfloat16)
        return (score_grad, probs_low, key_heads)

    def key_value_update(score_grad, probs_low, span):
        key_part = (
            jnp.einsum("hqk,qhd->khd", score_grad, query_heads, preferred_element_type=jnp.float32)
            * factor
        )
        value_part = jnp.einsum(
            "hqk,qhd->khd", probs_low, context_grad_heads, preferred_element_type=jnp.float32
        )
        return jnp.concatenate(
            [key_part.reshape(span, width_local), value_part.reshape(span, width_local)], axis=1
        )

    back_start = (
        jnp.zeros((rows, heads_local, HEAD), jnp.float32),
        jnp.zeros((rows * blocks, 2 * width_local), jnp.float32),
    )
    backward_piece = (
        lax.all_gather(key_low, "blk", axis=0, tiled=True),
        lax.all_gather(value_low, "blk", axis=0, tiled=True),
    )

    def backward_compute(state):
        score_grad, probs_low, key_heads = tile_grads(backward_piece[0], backward_piece[1])
        span = backward_piece[1].shape[0]
        query_acc = (
            jnp.einsum("hqk,khd->qhd", score_grad, key_heads, preferred_element_type=jnp.float32)
            * factor
        )
        update = key_value_update(score_grad, probs_low, span)
        return (query_acc, update)

    back_state = lax.cond(
        jnp.int32(0) > last_row, lambda state: state, backward_compute, back_start
    )
    kv_mine = lax.psum_scatter(
        back_state[1].astype(jnp.bfloat16), "blk", scatter_dimension=0, tiled=True
    ).astype(jnp.float32)
    query_grad_low = back_state[0].reshape(rows, width_local).astype(jnp.bfloat16)
    key_grad_low = kv_mine[:, :width_local].astype(jnp.bfloat16)
    value_grad_low = kv_mine[:, width_local:].astype(jnp.bfloat16)
    query_wgrad = dot_cols(normed_low, query_grad_low)
    key_wgrad = dot_cols(memory_low, key_grad_low)
    value_wgrad = dot_cols(memory_low, value_grad_low)
    normed_part = dot_rows(query_grad_low, back_query)
    memory_part = dot_rows(key_grad_low, back_key) + dot_rows(value_grad_low, back_value)
    normed_grad, memory_in_grad = (
        lax.psum(normed_part.astype(jnp.bfloat16), "heads").astype(jnp.float32),
        lax.psum(memory_part.astype(jnp.bfloat16), "heads").astype(jnp.float32),
    )
    input_pull = jax.vjp(rms_scale, hidden_float, back_input_gain)[1]
    hidden_norm_grad, input_gain_grad = input_pull(normed_grad)
    source_pull = jax.vjp(rms_scale, memory_float, back_source_gain)[1]
    memory_grad, source_gain_grad = source_pull(memory_in_grad)
    hidden_grad = attended_grad + hidden_norm_grad
    attn_shares = (
        lax.psum_scatter(query_wgrad, ("dp", "blk"), scatter_dimension=0, tiled=True),
        lax.psum_scatter(key_wgrad, ("dp", "blk"), scatter_dimension=0, tiled=True),
        lax.psum_scatter(value_wgrad, ("dp", "blk"), scatter_dimension=0, tiled=True),
        lax.psum_scatter(output_wgrad, ("dp", "blk"), scatter_dimension=0, tiled=True),
        lax.psum_scatter(input_gain_grad, ("dp", "blk"), scatter_dimension=0, tiled=True),
        lax.psum_scatter(source_gain_grad, ("dp", "blk"), scatter_dimension=0, tiled=True),
    )
    return (
        output,
        hidden_grad,
        memory_grad,
        attn_shares[0],
        attn_shares[1],
        attn_shares[2],
        attn_shares[3],
        ffn_shares[0],
        ffn_shares[1],
        ffn_shares[2],
        attn_shares[4],
        attn_shares[5],
        ffn_shares[3],
    )


def solution(mesh):
    placed = (
        P(("dp", "blk"), None),
        P(("dp", "blk"), None),
        P("dp", None),
        P(("dp", "blk"), "heads"),
        P(("dp", "blk"), "heads"),
        P(("dp", "blk"), "heads"),
        P(("dp", "blk"), "heads"),
        P(("dp", "blk"), "heads"),
        P(("dp", "blk"), "heads"),
        P(("dp", "blk"), "heads"),
        P(("dp", "blk")),
        P(("dp", "blk")),
        P(("dp", "blk")),
        P(("dp", "blk"), None),
    )
    return jax.shard_map(
        local,
        mesh=mesh,
        in_specs=placed,
        out_specs=(
            P(("dp", "blk"), None),
            P(("dp", "blk"), None),
            P(("dp", "blk"), None),
            P(("dp", "blk"), "heads"),
            P(("dp", "blk"), "heads"),
            P(("dp", "blk"), "heads"),
            P(("dp", "blk"), "heads"),
            P(("dp", "blk"), "heads"),
            P(("dp", "blk"), "heads"),
            P(("dp", "blk"), "heads"),
            P(("dp", "blk")),
            P(("dp", "blk")),
            P(("dp", "blk")),
        ),
        check_vma=False,
    )
```

profile of v0, /device:TPU:0, one launch (start us, length us, event | category | flops | bytes accessed | tf_op | source)
XLA Modules:
  0.0 2217.2 jit_solution(13810460397712391468)
XLA Ops:
  9.4 33.8 %all-gather = bf16[16,1,128]{2,1,0:T(2,128)(2,1)S(1)} all-gather(bf16[1,1,128]{2,1,0:T(2,128)(2,1)} %bitcast.129), channel_id=1, replica_groups=mesh['dp'=4,'blk'=4,'heads'=2] {'dp','blk'}, dimensions={0}, use_global_device_ids=true | all-gather | bytes 4352 | tf_op jit(solution)/shard_map/all_gather | solution.py:69
  45.1 18.4 all-gather.13.cloned.1.call-done
  63.5 5.5 convolution_convert_fusion.6
  69.1 45.8 %all-gather.19.cloned.1.call-done = bf16[2048,1024]{1,0:T(8,128)(2,1)} async-done(((bf16[128,1024]{1,0:T(8,128)(2,1)}), bf16[2048,1024]{1,0:T(8,128)(2,1)}) %all-gather.19.cloned.1.call-update) | async-done | bytes 4194320 | tf_op jit(solution)/shard_map/all_gather | solution.py:66
  115.0 4.9 convolution_convert_fusion.4
  120.7 30.2 %all-gather.1 = bf16[16,1,128]{2,1,0:T(2,128)(2,1)S(1)} all-gather(bf16[1,1,128]{2,1,0:T(2,128)(2,1)S(1)} %bitcast.130), channel_id=1, replica_groups=mesh['dp'=4,'blk'=4,'heads'=2] {'dp','blk'}, dimensions={0}, use_global_device_ids=true | all-gather | bytes 4352 | tf_op jit(solution)/shard_map/all_gather | solution.py:68
  151.5 14.8 all-gather.17.cloned.1.call-done
  166.3 4.0 fusion.51
  171.4 58.9 %all-gather.15.cloned.1.call-done = bf16[1536,1024]{1,0:T(8,128)(2,1)} async-done(((bf16[384,1024]{1,0:T(8,128)(2,1)}), bf16[1536,1024]{1,0:T(8,128)(2,1)}) %all-gather.15.cloned.1.call-update) | async-done | bytes 3145744 | tf_op jit(solution)/shard_map/all_gather | solution.py:109
  230.3 64.2 %all-gather.21.cloned.1.call-done = bf16[1536,1024]{1,0:T(8,128)(2,1)} async-done(((bf16[384,1024]{1,0:T(8,128)(2,1)}), bf16[1536,1024]{1,0:T(8,128)(2,1)}) %all-gather.21.cloned.1.call-update) | async-done | bytes 3145744 | tf_op jit(solution)/shard_map/all_gather | solution.py:110
  294.5 25.3 %conditional.2 = (f32[8,384]{1,0:T(8,128)S(1)}, f32[8,384]{1,0:T(8,128)S(1)}, f32[8,384]{1,0:T(8,128)S(1)}, f32[384,8,128]{0,2,1:T(8,128)S(1)}) conditional(s32[]{:T(128)} %convert_element_type.137, (s32[384]{0:T(512)S(1)}, s32[4]{0:T(128)S(1)}, s32[384]{0:T(512)S(1)}, bf16[1536,1024]{1,0:T(8,128)(2,1)}, bf16[384,8,128]{2,1,0:T(8,128)(2,1)}, ...), branch_computations={%region_4.8_spmd, %region_8.9_spmd} | conditional | flops 2479443456 | bytes 73276496 | solution.py:132
  296.0 5.9 fusion
  302.0 7.6 fusion.2
  309.6 8.3 bitcast_add_fusion
  320.9 25.0 %all-gather.23.cloned.1.call-done = bf16[2048,1024]{1,0:T(8,128)(2,1)} async-done(((bf16[128,1024]{1,0:T(8,128)(2,1)}), bf16[2048,1024]{1,0:T(8,128)(2,1)}) %all-gather.23.cloned.1.call-update) | async-done | bytes 4194320 | tf_op jit(solution)/shard_map/all_gather | solution.py:67
  346.0 5.4 convolution_convert_fusion.2
  353.9 29.9 %all-gather.2 = bf16[16,1,128]{2,1,0:T(2,128)(2,1)S(1)} all-gather(bf16[1,1,128]{2,1,0:T(2,128)(2,1)S(1)} %bitcast.131), channel_id=1, replica_groups=mesh['dp'=4,'blk'=4,'heads'=2] {'dp','blk'}, dimensions={0}, use_global_device_ids=true | all-gather | bytes 4352 | tf_op jit(solution)/shard_map/all_gather | solution.py:144
  383.8 17.7 all-reduce.9.cloned.1.call-done
  405.5 94.0 %all-gather.25.cloned.1.call-done = bf16[2048,2752]{0,1:T(8,128)(2,1)} async-done(((bf16[128,2752]{0,1:T(8,128)(2,1)}), bf16[2048,2752]{0,1:T(8,128)(2,1)}) %all-gather.25.cloned.1.call-update) | async-done | bytes 11272208 | tf_op jit(solution)/shard_map/all_gather | solution.py:141
  499.6 10.7 fusion.77
  510.2 85.6 %all-gather.27.cloned.1.call-done = bf16[2048,2752]{0,1:T(8,128)(2,1)} async-done(((bf16[128,2752]{0,1:T(8,128)(2,1)}), bf16[2048,2752]{0,1:T(8,128)(2,1)}) %all-gather.27.cloned.1.call-update) | async-done | bytes 11272208 | tf_op jit(solution)/shard_map/all_gather | solution.py:142
  595.8 10.6 fusion.78
  606.4 85.4 %all-gather.29.cloned.1.call-done = bf16[2048,2752]{0,1:T(8,128)(2,1)} async-done(((bf16[128,2752]{0,1:T(8,128)(2,1)}), bf16[2048,2752]{0,1:T(8,128)(2,1)}) %all-gather.29.cloned.1.call-update) | async-done | bytes 11272208 | tf_op jit(solution)/shard_map/all_gather | solution.py:143
  691.9 14.0 multiply_convert_fusion.2
  705.8 9.1 fusion.79
  715.0 5.9 add_convert_fusion.1
  721.0 49.8 %all-reduce.11.cloned.1.call-done = bf16[384,2048]{1,0:T(8,128)(2,1)} async-done(((bf16[384,2048]{1,0:T(8,128)(2,1)}), bf16[384,2048]{1,0:T(8,128)(2,1)}) %all-reduce.11.cloned.1.call-update) | async-done | bytes 1572880 | tf_op jit(solution)/shard_map/psum | solution.py:174
  770.7 3.4 fusion.42
  774.2 4.5 fusion.52
  779.7 2.4 copy.70
  784.0 59.0 %conditional.3 = (bf16[1536,2048]{0,1:T(8,128)(2,1)}, bf16[384,1024]{0,1:T(8,128)(2,1)}) conditional(s32[]{:T(128)} %convert_element_type.137, (s32[384]{0:T(512)S(1)}, s32[4]{0:T(128)S(1)}, s32[384]{0:T(512)S(1)}, bf16[1536,1024]{1,0:T(8,128)(2,1)}, bf16[384,8,128]{2,1,0:T(8,128)(2,1)}, /*index=5*/f32[8,384]{1,0:T(8,128)S(1)}, ...), branch_computations={%region_15.17_spmd, %region_17.18_spmd} | conditional | flops 6105288192 | bytes 197680304 | solution.py:249
  784.0 2.4 copy.73
  786.4 2.4 copy.72
  788.9 4.6 copy.71
  793.5 11.3 fusion.76
  805.5 10.1 fusion.21
  815.6 11.1 multiply_convert_fusion
  830.4 5.1 pad_maximum_fusion
  835.5 7.4 multiply_convert_fusion.1
  843.0 8.7 copy.77
  852.2 10.8 convolution_convert_fusion
  863.0 4.2 convolution_convert_fusion.1
  867.2 95.4 %reduce-scatter.25.cloned.1.call-done = bf16[384,2048]{1,0:T(8,128)(2,1)} async-done(((bf16[1536,2048]{1,0:T(8,128)(2,1)}), bf16[384,2048]{1,0:T(8,128)(2,1)}) %reduce-scatter.25.cloned.1.call-update) | async-done | bytes 1572880
  962.6 4.4 fusion.59
  967.0 3.0 add_convert_fusion
  970.7 7.2 fusion.64
  978.2 8.7 fusion.53
  987.5 7.4 fusion.61
  995.1 7.4 fusion.57
  1002.5 12.4 fusion.80
  1015.3 12.4 fusion.81
  1027.8 13.2 convolution_bitcast_fusion
  1042.8 47.8 %all-reduce.13.cloned.1.call-done = (bf16[384,2048]{1,0:T(8,128)(2,1)}, bf16[384,2048]{1,0:T(8,128)(2,1)}, bf16[384,2048]{1,0:T(8,128)(2,1)}) async-done(((bf16[384,2048]{1,0:T(8,128)(2,1)}, bf16[384,2048]{1,0:T(8,128)(2,1)}, bf16[384,2048]{1,0:T(8,128)(2,1)}), (bf16[384,2048]{1,0:T(8,128)(2,1)}, bf16[384,2048]{1,0:T(8,128)(2,1)}, bf16[384,2048]{1,0:T(8,128)(2,1)})) %all-reduce.13.cloned.1.call-update) | async-done | bytes 4718608 | tf_op jit(solution)/shard_map/psum | solution.py:156
  1090.7 2.7 fusion.43
  1094.6 63.6 %all-reduce.3 = (f32[2048]{0:T(1024)S(1)}, f32[2048]{0:T(1024)S(1)}, f32[2048]{0:T(1024)S(1)}) all-reduce(f32[2048]{0:T(1024)S(1)} %get-tuple-element.145, f32[2048]{0:T(1024)S(1)} %get-tuple-element.143, f32[2048]{0:T(1024)S(1)} %copy-done.29), channel_id=10, replica_groups=mesh['dp'=4,'blk'=4,'heads'=2] {'dp','blk'}, use_global_device_ids=true, to_apply=%region_31.32.clone | all-reduce | flops 6144 | bytes 49152
  1160.0 4.6 add_add_fusion
  1164.6 4.5 fusion.46
  1169.1 30.9 %reduce-scatter.11.cloned.1.call-done = f32[128,1024]{1,0:T(8,128)} async-done(((f32[2048,1024]{1,0:T(8,128)}), f32[128,1024]{1,0:T(8,128)}) %reduce-scatter.11.cloned.1.call-update) | async-done | bytes 524304 | tf_op jit(solution)/shard_map/reduce_scatter | solution.py:273
  1200.1 109.5 %reduce-scatter.17.cloned.1.call-done = f32[128,1024]{1,0:T(8,128)} async-done(((f32[2048,1024]{1,0:T(8,128)}), f32[128,1024]{1,0:T(8,128)}) %reduce-scatter.17.cloned.1.call-update) | async-done | bytes 524304 | tf_op jit(solution)/shard_map/reduce_scatter | solution.py:276
  1309.6 109.4 %reduce-scatter.13.cloned.1.call-done = f32[128,1024]{1,0:T(8,128)} async-done(((f32[2048,1024]{1,0:T(8,128)}), f32[128,1024]{1,0:T(8,128)}) %reduce-scatter.13.cloned.1.call-update) | async-done | bytes 524304 | tf_op jit(solution)/shard_map/reduce_scatter | solution.py:274
  1419.0 109.5 %reduce-scatter.15.cloned.1.call-done = f32[128,1024]{1,0:T(8,128)} async-done(((f32[2048,1024]{1,0:T(8,128)}), f32[128,1024]{1,0:T(8,128)}) %reduce-scatter.15.cloned.1.call-update) | async-done | bytes 524304 | tf_op jit(solution)/shard_map/reduce_scatter | solution.py:275
  1528.5 227.6 %reduce-scatter.19.cloned.1.call-done = f32[128,2752]{0,1:T(8,128)} async-done(((f32[2048,2752]{0,1:T(8,128)}), f32[128,2752]{0,1:T(8,128)}) %reduce-scatter.19.cloned.1.call-update) | async-done | bytes 1409040 | tf_op jit(solution)/shard_map/reduce_scatter | solution.py:179
  1756.1 227.1 %reduce-scatter.21.cloned.1.call-done = f32[128,2752]{0,1:T(8,128)} async-done(((f32[2048,2752]{0,1:T(8,128)}), f32[128,2752]{0,1:T(8,128)}) %reduce-scatter.21.cloned.1.call-update) | async-done | bytes 1409040 | tf_op jit(solution)/shard_map/reduce_scatter | solution.py:180
  1983.2 226.9 %reduce-scatter.23.cloned.1.call-done = f32[128,2752]{0,1:T(8,128)} async-done(((f32[2048,2752]{0,1:T(8,128)}), f32[128,2752]{0,1:T(8,128)}) %reduce-scatter.23.cloned.1.call-update) | async-done | bytes 1409040 | tf_op jit(solution)/shard_map/reduce_scatter | solution.py:181
  (156 shorter events, 31.6 us)
Async XLA Ops:
  7.2 56.3 %all-gather.13.cloned.1.call-start = ((), (), s32[]{:S(2)}) async-start(), calls=%async_computation.8 | async-start | bytes 4456448 | tf_op jit(solution)/shard_map/all_gather | solution.py:65
  7.9 107.1 %all-gather.19.cloned.1.call-start = ((), (), s32[]{:S(2)}) async-start(), calls=%async_computation.11 | async-start | bytes 4456448 | tf_op jit(solution)/shard_map/all_gather | solution.py:66
  8.7 157.6 %all-gather.17.cloned.1.call-start = ((), (), s32[]{:S(2)}) async-start(), calls=%async_computation.10 | async-start | bytes 4456448 | tf_op jit(solution)/shard_map/all_gather | solution.py:64
  9.4 220.9 %all-gather.15.cloned.1.call-start = ((), (), s32[]{:S(2)}) async-start(), calls=%async_computation.9 | async-start | bytes 3932160 | tf_op jit(solution)/shard_map/all_gather | solution.py:109
  43.3 71.7 %copy-start.21 = (f32[16,1,128]{2,1,0:T(1,128)}, f32[16,1,128]{2,1,0:T(1,128)S(1)}, u32[]{:S(2)}) copy-start(f32[16,1,128]{2,1,0:T(1,128)S(1)} %convert_element_type.170) | copy-start | bytes 24580
  45.1 23.9 %copy-start.30 = (f32[384]{0:T(512)}, f32[384]{0:T(512)S(1)}, u32[]{:S(2)}) copy-start(f32[384]{0:T(512)S(1)} %fusion.47) | copy-start | bytes 4612
  45.1 69.9 %copy-start.25 = (f32[384]{0:T(512)}, f32[384]{0:T(512)S(1)}, u32[]{:S(2)}) copy-start(f32[384]{0:T(512)S(1)} %fusion.67) | copy-start | bytes 4612
  63.5 51.5 %copy-start.2 = (bf16[384,2048]{1,0:T(8,128)(2,1)S(1)}, bf16[384,2048]{1,0:T(8,128)(2,1)}, u32[]{:S(2)}) copy-start(bf16[384,2048]{1,0:T(8,128)(2,1)} %param.19) | copy-start | bytes 4718596
  69.0 51.5 %copy-start.39 = (s32[1,4]{1,0:T(1,128)S(1)}, s32[1,4]{1,0:T(1,128)}, u32[]{:S(2)}) copy-start(s32[1,4]{1,0:T(1,128)} %param.20) | copy-start | bytes 52
  69.1 51.7 %copy-start.34 = (bf16[128]{0:T(256)(128)(2,1)S(1)}, bf16[128]{0:T(256)(128)(2,1)}, u32[]{:S(2)}) copy-start(bf16[128]{0:T(256)(128)(2,1)} %param.28) | copy-start | bytes 772
  69.1 82.0 %copy-start = (bf16[384,2048]{1,0:T(8,128)(2,1)S(1)}, bf16[384,2048]{1,0:T(8,128)(2,1)}, u32[]{:S(2)}) copy-start(bf16[384,2048]{1,0:T(8,128)(2,1)} %param.18) | copy-start | bytes 4718596
  69.1 225.4 %all-gather.21.cloned.1.call-start = ((), (), s32[]{:S(2)}) async-start(), calls=%async_computation.12 | async-start | bytes 3932160 | tf_op jit(solution)/shard_map/all_gather | solution.py:110
  119.9 226.0 %all-gather.23.cloned.1.call-start = ((), (), s32[]{:S(2)}) async-start(), calls=%async_computation.13 | async-start | bytes 4456448 | tf_op jit(solution)/shard_map/all_gather | solution.py:67
  120.5 281.0 %all-reduce.9.cloned.1.call-start = ((), (), s32[]{:S(2)}) async-start(), calls=%async_computation.14 | async-start | bytes 3145728 | tf_op jit(solution)/shard_map/psum | solution.py:139
  150.9 19.4 copy-start.23
  151.4 18.9 copy-start.32
  151.4 18.9 copy-start.27
  301.9 7.7 copy-start.16
  319.8 31.6 %copy-start.11 = (f32[384,8,128]{0,2,1:T(8,128)}, f32[384,8,128]{0,2,1:T(8,128)S(1)}, u32[]{:S(2)}) copy-start(f32[384,8,128]{0,2,1:T(8,128)S(1)} %get-tuple-element.140) | copy-start | bytes 4718596
  351.4 2.6 copy-start.35
  351.4 148.2 %all-gather.25.cloned.1.call-start = ((), (), s32[]{:S(2)}) async-start(), calls=%async_computation.15 | async-start | bytes 11976704 | tf_op jit(solution)/shard_map/all_gather | solution.py:141
  352.2 243.6 %all-gather.27.cloned.1.call-start = ((), (), s32[]{:S(2)}) async-start(), calls=%async_computation.16 | async-start | bytes 11976704 | tf_op jit(solution)/shard_map/all_gather | solution.py:142
  352.9 339.0 %all-gather.29.cloned.1.call-start = ((), (), s32[]{:S(2)}) async-start(), calls=%async_computation.17 | async-start | bytes 11976704 | tf_op jit(solution)/shard_map/all_gather | solution.py:143
  353.5 417.2 %all-reduce.11.cloned.1.call-start = ((), (), s32[]{:S(2)}) async-start(), calls=%async_computation.18 | async-start | bytes 3145728 | tf_op jit(solution)/shard_map/psum | solution.py:174
  401.5 2.1 copy-start.1
  705.8 9.1 copy-start.17
  705.8 9.1 copy-start.12
  705.8 9.1 copy-start.9
  720.9 241.7 %reduce-scatter.25.cloned.1.call-start = ((), (), s32[]{:S(2)}) async-start(), calls=%async_computation.26 | async-start | bytes 7864320
  770.7 3.4 copy-start.4
  770.7 3.4 copy-start.6
  793.5 12.0 copy-start.20
  805.5 10.1 copy-start.38
  815.6 11.2 copy-start.13
  826.8 3.7 copy-start.10
  830.4 5.1 copy-start.8
  851.7 238.9 %all-reduce.13.cloned.1.call-start = ((), (), s32[]{:S(2)}) async-start(), calls=%async_computation.27 | async-start | bytes 9437184 | tf_op jit(solution)/shard_map/psum | solution.py:156
  852.2 10.9 copy-start.37
  962.6 4.4 copy-start.19
  962.6 4.4 copy-start.36
  970.0 0.7 copy-start.24
  970.0 0.7 copy-start.28
  970.0 230.0 %reduce-scatter.11.cloned.1.call-start = ((), (), s32[]{:S(2)}) async-start(), calls=%async_computation.19 | async-start | bytes 8912896 | tf_op jit(solution)/shard_map/reduce_scatter | solution.py:273
  978.0 331.6 %reduce-scatter.17.cloned.1.call-start = ((), (), s32[]{:S(2)}) async-start(), calls=%async_computation.22 | async-start | bytes 8912896 | tf_op jit(solution)/shard_map/reduce_scatter | solution.py:276
  986.8 0.7 copy-start.22
  986.8 0.7 copy-start.26
  986.9 432.2 %reduce-scatter.13.cloned.1.call-start = ((), (), s32[]{:S(2)}) async-start(), calls=%async_computation.20 | async-start | bytes 8912896 | tf_op jit(solution)/shard_map/reduce_scatter | solution.py:274
  995.0 533.5 %reduce-scatter.15.cloned.1.call-start = ((), (), s32[]{:S(2)}) async-start(), calls=%async_computation.21 | async-start | bytes 8912896 | tf_op jit(solution)/shard_map/reduce_scatter | solution.py:275
  1002.5 753.6 %reduce-scatter.19.cloned.1.call-start = ((), (), s32[]{:S(2)}) async-start(), calls=%async_computation.23 | async-start | bytes 23953408 | tf_op jit(solution)/shard_map/reduce_scatter | solution.py:179
  1015.0 968.2 %reduce-scatter.21.cloned.1.call-start = ((), (), s32[]{:S(2)}) async-start(), calls=%async_computation.24 | async-start | bytes 23953408 | tf_op jit(solution)/shard_map/reduce_scatter | solution.py:180
  1027.7 1182.4 %reduce-scatter.23.cloned.1.call-start = ((), (), s32[]{:S(2)}) async-start(), calls=%async_computation.25 | async-start | bytes 23953408 | tf_op jit(solution)/shard_map/reduce_scatter | solution.py:181
  1040.9 0.7 copy-start.40
  1090.6 2.7 copy-start.3
  1090.6 2.7 copy-start.14
  1090.6 3.9 copy-start.29
  1090.6 69.3 %copy-start.33 = (f32[384]{0:T(512)S(1)}, f32[384]{0:T(512)}, u32[]{:S(2)}) copy-start(f32[384]{0:T(512)} %copy-done.32) | copy-start | bytes 4612
  1090.7 69.3 %copy-start.31 = (f32[384]{0:T(512)S(1)}, f32[384]{0:T(512)}, u32[]{:S(2)}) copy-start(f32[384]{0:T(512)} %copy-done.30) | copy-start | bytes 4612
  1160.0 4.6 copy-start.5
  1160.0 4.6 copy-start.7
  1160.0 4.6 copy-start.15
  1160.0 4.6 copy-start.18
Sparse Core Ops, SparseCore 0:
  10.2 53.2 all-gather.12
  65.7 49.1 all-gather.18
  117.2 49.0 all-gather.16
  168.3 61.9 all-gather.14
  232.3 62.1 all-gather.20
  296.6 49.3 all-gather.22
  351.5 49.9 all-reduce.8
  403.8 95.7 all-gather.24
  501.9 93.8 all-gather.26
  597.9 93.8 all-gather.28
  721.0 49.6 all-reduce.10
  851.8 110.7 reduce-scatter.24
  970.2 120.4 all-reduce.12
  1095.7 104.3 reduce-scatter.10
  1205.1 104.4 reduce-scatter.16
  1314.6 104.3 reduce-scatter.12
  1424.1 104.4 reduce-scatter.14
  1533.8 222.3 reduce-scatter.18
  1761.5 221.6 reduce-scatter.20
  1988.5 221.6 reduce-scatter.22
where the time goes:
time: 2220 us
  waiting for transfers between devices  1750 us (79%)
  matrix products  222 us (10%)
  blocking collectives  157 us (7%)
  other arithmetic  40.9 us (2%)
  local copies, waits for them, and re-layouts  30.8 us (1%)
    reduce_scatter x1, waiting for transfers between devices, local(): lax.psum_scatter(gate_wgrad, ('dp', 'blk'), scatter_dimension=0, tiled=True)  228 us
    reduce_scatter x1, waiting for transfers between devices, local(): lax.psum_scatter(up_wgrad, ('dp', 'blk'), scatter_dimension=0, tiled=True)  227 us
    reduce_scatter x1, waiting for transfers between devices, local(): lax.psum_scatter(down_grad, ('dp', 'blk'), scatter_dimension=0, tiled=True)  227 us
    reduce_scatter x1, waiting for transfers between devices, local(): lax.psum_scatter(output_wgrad, ('dp', 'blk'), scatter_dimension=0, tiled=...  110 us
    reduce_scatter x1, waiting for transfers between devices, local(): lax.psum_scatter(value_wgrad, ('dp', 'blk'), scatter_dimension=0, tiled=T...  109 us
    reduce_scatter x1, waiting for transfers between devices, local(): lax.psum_scatter(key_wgrad, ('dp', 'blk'), scatter_dimension=0, tiled=True)  109 us
    unnamed x21, waiting for transfers between devices  100 us
    all_gather x1, waiting for transfers between devices, local(): lax.all_gather(gate_weight, ('dp', 'blk'), axis=0, tiled=True)  94 us
  transfers between devices with their start and end apart: 20, of which 20 were waited for; matrix products, arithmetic and copies ran while one was open for 8% of the time, Pallas kernels for 0%

commit v1 on v0

v1 whole, which is shorter than its diff:
```python
import math

import jax
import jax.numpy as jnp
from jax import lax
from jax.sharding import PartitionSpec as P

HEAD = 128
LANES = 128
EPSILON = 1e-06
NEGATIVE = -1e30


def rms_scale(values, gain):
    return values * lax.rsqrt(jnp.mean(values * values, axis=-1, keepdims=True) + EPSILON) * gain


def plain_dot(left, right):
    return jnp.dot(left, right, preferred_element_type=jnp.float32)


def dot_rows(left, right):
    return lax.dot_general(
        left, right, (((1,), (1,)), ((), ())), preferred_element_type=jnp.float32
    )


def dot_cols(left, right):
    return lax.dot_general(
        left, right, (((0,), (0,)), ((), ())), preferred_element_type=jnp.float32
    )


def doc_number(positions, doc_ends):
    return jnp.sum((positions[:, None] >= doc_ends[None, :]).astype(jnp.int32), axis=1)


def swap(array, axis, bit):
    size = lax.axis_size(axis)
    return lax.ppermute(array, axis, [(i, i ^ bit) for i in range(size)])


def pair_sum(part):
    low = part.astype(jnp.bfloat16)
    if lax.axis_size("heads") != 2:
        return lax.psum(low, "heads").astype(jnp.float32)
    other = swap(low, "heads", 1)
    return low.astype(jnp.float32) + other.astype(jnp.float32)


def fold_steps():
    steps = []
    for axis in ("dp", "blk"):
        size, bit = lax.axis_size(axis), 1
        while bit < size:
            steps.append((axis, bit))
            bit *= 2
    return steps


def fold_order(width):
    steps = fold_steps()
    shards = 2 ** len(steps)
    part = width // shards
    here = {axis: lax.axis_index(axis) for axis in ("dp", "blk")}
    offsets = []
    for place in range(shards):
        flip = {"dp": 0, "blk": 0}
        for number, (axis, bit) in enumerate(steps):
            if place >> (len(steps) - 1 - number) & 1:
                flip[axis] |= bit
        shard = (here["dp"] ^ flip["dp"]) * lax.axis_size("blk") + (here["blk"] ^ flip["blk"])
        offsets.append(shard * part)
    return offsets, part


def fold_columns(array):
    offsets, part = fold_order(array.shape[1])
    return jnp.concatenate(
        [lax.dynamic_slice_in_dim(array, offset, part, axis=1) for offset in offsets], axis=1
    )


def fold_product(left, right, kind=jnp.bfloat16):
    steps = fold_steps()
    size = left.shape[1]
    pieces = []
    for _ in steps:
        size //= 2
        pieces.append((size, 2 * size))
    pieces.append((0, size))
    arrived = []
    for (axis, bit), (low, high) in zip(steps, pieces):
        part = dot_cols(left[:, low:high], right)
        for earlier in arrived:
            part = part + earlier[low:high].astype(jnp.float32)
        arrived.append(swap(part.astype(kind), axis, bit))
    low, high = pieces[-1]
    part = dot_cols(left[:, low:high], right)
    for earlier in arrived:
        part = part + earlier[low:high].astype(jnp.float32)
    return part


def fold_vector(vector):
    offsets, part = fold_order(vector.shape[-1])
    held = jnp.stack(
        [lax.dynamic_slice_in_dim(vector, offset, part, axis=-1) for offset in offsets], axis=0
    )
    for axis, bit in fold_steps():
        half = held.shape[0] // 2
        held = held[:half] + swap(held[half:], axis, bit)
    return held[0]


def to_heads(pieces, blocks):
    rows, width = pieces[0].shape
    part = width // blocks
    packed = jnp.stack(
        [
            jnp.concatenate([piece[:, i * part : (i + 1) * part] for piece in pieces], axis=1)
            for i in range(blocks)
        ],
        axis=0,
    )
    moved = lax.all_to_all(packed, "blk", 0, 0)
    flat = moved.reshape(rows * blocks, part * len(pieces))
    return [flat[:, i * part : (i + 1) * part] for i in range(len(pieces))]


def to_blocks(pieces, blocks):
    length, part = pieces[0].shape
    rows = length // blocks
    packed = jnp.concatenate(pieces, axis=1).reshape(blocks, rows, part * len(pieces))
    moved = lax.all_to_all(packed, "blk", 0, 0)
    return [
        jnp.concatenate([moved[j, :, i * part : (i + 1) * part] for j in range(blocks)], axis=1)
        for i in range(len(pieces))
    ]


def local(
    hidden_in,
    memory,
    lengths,
    query_weight,
    key_weight,
    value_weight,
    output_weight,
    gate_weight,
    up_weight,
    down_weight,
    attention_gain,
    memory_gain,
    feedforward_gain,
    cotangent,
):
    rows, features = hidden_in.shape
    blocks = lax.axis_size("blk")
    width = query_weight.shape[1]
    hidden_units = gate_weight.shape[1]
    heads_local = width // HEAD
    factor = 1.0 / math.sqrt(HEAD)
    spread = heads_local % blocks == 0
    doc_ends = jnp.cumsum(lengths[0], dtype=jnp.int32)

    gains = jnp.stack([attention_gain, memory_gain, feedforward_gain], axis=1)
    gains = jnp.pad(gains, ((0, 0), (0, LANES - gains.shape[1])))
    attn_mine = jnp.concatenate(
        [query_weight, key_weight, value_weight, output_weight, gains], axis=1
    )
    attn_full = lax.all_gather(attn_mine, ("dp", "blk"), axis=0, tiled=True)
    cuts = 2
    chunk = -(-hidden_units // (cuts * LANES)) * LANES
    spans = [(i * chunk, min(hidden_units, (i + 1) * chunk)) for i in range(cuts)]
    ffn_mine = []
    for start, stop in spans:
        for weight in (gate_weight, up_weight, down_weight):
            ffn_mine.append(
                jnp.pad(weight[:, start:stop], ((0, 0), (0, chunk - (stop - start))))
            )
    ffn_mine = jnp.concatenate(ffn_mine, axis=1)
    ffn_mine, attn_full = lax.optimization_barrier((ffn_mine, attn_full))
    ffn_full = lax.all_gather(ffn_mine, ("dp", "blk"), axis=0, tiled=True)

    full_query = attn_full[:, :width]
    full_key = attn_full[:, width : 2 * width]
    full_value = attn_full[:, 2 * width : 3 * width]
    full_output = attn_full[:, 3 * width : 4 * width]
    full_gains = attn_full[:, 4 * width : 4 * width + 3].astype(jnp.float32).T
    input_gain, source_gain, mid_gain = full_gains[0], full_gains[1], full_gains[2]

    hidden_float = hidden_in.astype(jnp.float32)
    memory_float = memory.astype(jnp.float32)
    memory_low = rms_scale(memory_float, source_gain).astype(jnp.bfloat16)
    normed_low = rms_scale(hidden_float, input_gain).astype(jnp.bfloat16)
    key_low = plain_dot(memory_low, full_key).astype(jnp.bfloat16)
    value_low = plain_dot(memory_low, full_value).astype(jnp.bfloat16)
    query_low = plain_dot(normed_low, full_query).astype(jnp.bfloat16)

    length = rows * blocks
    key_pos = jnp.arange(length, dtype=jnp.int32)
    key_doc = doc_number(key_pos, doc_ends)
    if spread:
        query_all, key_all, value_all = to_heads([query_low, key_low, value_low], blocks)
        query_pos = key_pos
    else:
        query_all = query_low
        key_all = lax.all_gather(key_low, "blk", axis=0, tiled=True)
        value_all = lax.all_gather(value_low, "blk", axis=0, tiled=True)
        query_pos = lax.axis_index("blk") * rows + jnp.arange(rows, dtype=jnp.int32)
    query_doc = doc_number(query_pos, doc_ends)
    allowed = (key_pos[None, :] <= query_pos[:, None]) & (key_doc[None, :] == query_doc[:, None])
    query_heads = query_all.reshape(query_all.shape[0], -1, HEAD)
    key_heads = key_all.reshape(length, -1, HEAD)
    value_heads = value_all.reshape(length, -1, HEAD)

    def scores_of():
        return (
            jnp.einsum("qhd,khd->hqk", query_heads, key_heads, preferred_element_type=jnp.float32)
            * factor
        )

    masked = jnp.where(allowed[None], scores_of(), NEGATIVE)
    top = jnp.max(masked, axis=-1)
    weights = jnp.where(allowed[None], jnp.exp(masked - top[..., None]), 0.0)
    total = jnp.sum(weights, axis=-1)
    added = jnp.einsum(
        "hqk,khd->qhd", weights.astype(jnp.bfloat16), value_heads, preferred_element_type=jnp.float32
    )
    context = added / total.T[:, :, None]
    log_total = top + jnp.log(total)
    context_all = context.reshape(context.shape[0], -1).astype(jnp.bfloat16)
    context_low = to_blocks([context_all], blocks)[0] if spread else context_all

    attended = hidden_float + pair_sum(dot_rows(context_low, full_output))
    mid_low = rms_scale(attended, mid_gain).astype(jnp.bfloat16)

    mid_fold = fold_columns(mid_low)
    cot_fold = fold_columns(cotangent)
    cot_float = cotangent.astype(jnp.float32)
    ffn_part, mid_part = 0.0, 0.0
    ffn_shares = ([], [], [])
    for number, (start, stop) in enumerate(spans):
        own = ffn_full[:, 3 * chunk * number : 3 * chunk * (number + 1)]
        span_gate, span_up, span_down = own[:, :chunk], own[:, chunk : 2 * chunk], own[:, 2 * chunk :]
        gate = plain_dot(mid_low, span_gate)
        upward = plain_dot(mid_low, span_up)
        sigma = jax.nn.sigmoid(gate)
        silu_gate = gate * sigma
        act_low = (silu_gate * upward).astype(jnp.bfloat16)
        act_grad = plain_dot(cotangent, span_down)
        gate_grad_low = (act_grad * upward * sigma * (1.0 + gate * (1.0 - sigma))).astype(
            jnp.bfloat16
        )
        up_grad_low = (act_grad * silu_gate).astype(jnp.bfloat16)
        mid_part = mid_part + dot_rows(gate_grad_low, span_gate) + dot_rows(up_grad_low, span_up)
        ffn_part = ffn_part + dot_rows(act_low, span_down)
        size = stop - start
        ffn_shares[0].append(fold_product(mid_fold, gate_grad_low[:, :size]))
        ffn_shares[1].append(fold_product(mid_fold, up_grad_low[:, :size]))
        ffn_shares[2].append(fold_product(cot_fold, act_low[:, :size]))
    gate_share, up_share, down_share = (jnp.concatenate(parts, axis=1) for parts in ffn_shares)
    mid_grad = pair_sum(mid_part)
    output = (attended + pair_sum(ffn_part)).astype(jnp.bfloat16)
    attended_norm_grad, mid_gain_grad = jax.vjp(rms_scale, attended, mid_gain)[1](mid_grad)
    attended_grad = cot_float + attended_norm_grad

    resid_low = attended_grad.astype(jnp.bfloat16)
    output_share = fold_product(fold_columns(resid_low), context_low)
    context_grad_low = plain_dot(resid_low, full_output).astype(jnp.bfloat16)
    if spread:
        context_grad_all = to_heads([context_grad_low], blocks)[0]
    else:
        context_grad_all = context_grad_low
    context_grad_heads = context_grad_all.reshape(context_grad_all.shape[0], -1, HEAD)
    delta = jnp.sum(context_grad_heads.astype(jnp.float32) * context, axis=-1).T
    probs = jnp.where(allowed[None], jnp.exp(scores_of() - log_total[..., None]), 0.0)
    probs_low = probs.astype(jnp.bfloat16)
    prob_grad = jnp.einsum(
        "qhd,khd->hqk", context_grad_heads, value_heads, preferred_element_type=jnp.float32
    )
    score_grad = (probs * (prob_grad - delta[..., None])).astype(jnp.bfloat16)
    query_grad = (
        jnp.einsum("hqk,khd->qhd", score_grad, key_heads, preferred_element_type=jnp.float32)
        * factor
    )
    key_grad = (
        jnp.einsum("hqk,qhd->khd", score_grad, query_heads, preferred_element_type=jnp.float32)
        * factor
    )
    value_grad = jnp.einsum(
        "hqk,qhd->khd", probs_low, context_grad_heads, preferred_element_type=jnp.float32
    )
    query_grad, key_grad, value_grad = (
        grad.reshape(grad.shape[0], -1).astype(jnp.bfloat16)
        for grad in (query_grad, key_grad, value_grad)
    )
    if spread:
        query_grad_low, key_grad_low, value_grad_low = to_blocks(
            [query_grad, key_grad, value_grad], blocks
        )
    else:
        query_grad_low = query_grad
        mine = lax.psum_scatter(
            jnp.concatenate([key_grad, value_grad], axis=1), "blk", scatter_dimension=0, tiled=True
        )
        key_grad_low, value_grad_low = mine[:, :width], mine[:, width:]

    normed_grad = pair_sum(dot_rows(query_grad_low, full_query))
    memory_in_grad = pair_sum(
        dot_rows(key_grad_low, full_key) + dot_rows(value_grad_low, full_value)
    )
    normed_fold, memory_fold = fold_columns(normed_low), fold_columns(memory_low)
    query_share = fold_product(normed_fold, query_grad_low)
    key_share = fold_product(memory_fold, key_grad_low)
    value_share = fold_product(memory_fold, value_grad_low)
    hidden_norm_grad, input_gain_grad = jax.vjp(rms_scale, hidden_float, input_gain)[1](normed_grad)
    memory_grad, source_gain_grad = jax.vjp(rms_scale, memory_float, source_gain)[1](memory_in_grad)
    hidden_grad = attended_grad + hidden_norm_grad
    gain_shares = fold_vector(jnp.stack([input_gain_grad, source_gain_grad, mid_gain_grad], axis=0))
    return (
        output,
        hidden_grad,
        memory_grad,
        query_share,
        key_share,
        value_share,
        output_share,
        gate_share,
        up_share,
        down_share,
        gain_shares[0],
        gain_shares[1],
        gain_shares[2],
    )


def solution(mesh):
    tokens = P(("dp", "blk"), None)
    weight = P(("dp", "blk"), "heads")
    gain = P(("dp", "blk"))
    return jax.shard_map(
        local,
        mesh=mesh,
        in_specs=(tokens, tokens, P("dp", None)) + (weight,) * 7 + (gain,) * 3 + (tokens,),
        out_specs=(tokens,) * 3 + (weight,) * 7 + (gain,) * 3,
        check_vma=False,
    )
```

time: 2220 us -> 1170 us (0.53)
  waiting for transfers between devices: 1750 us -> 614 us
  blocking collectives: 157 us -> 0 us
  local copies, waits for them, and re-layouts: 30.8 us -> 134 us
  starting transfers between devices: 2 us -> 80.1 us
  matrix products: 222 us -> 257 us
    reduce_scatter x7 -> x0, waiting for transfers between devices: 1040 us -> none  [the longest x1 228 us: local(): lax.psum_scatter(gate_wgrad, ('dp', 'blk'), scatter_dimension=0, tiled=True)]
    ppermute x0 -> x49, waiting for transfers between devices: none -> 393 us  [swap(): return lax.ppermute(array, axis, [(i, i ^ bit) for i in range(size)])]
    all_gather x9 -> x2, waiting for transfers between devices: 492 us -> 140 us  [the longest x1 94.1 us: local(): attn_full = lax.all_gather(attn_mine, ('dp', 'blk'), axis=0, tiled=True)]
    psum x3 -> x0, waiting for transfers between devices: 115 us -> none  [the longest x1 49.8 us: local(): lax.psum(mid_part.astype(jnp.bfloat16), 'heads').astype(jnp.float32)]
    unnamed x21 -> x2, waiting for transfers between devices: 100 us -> 0.03 us
    all_gather x3 -> x0, blocking collectives: 93.9 us -> none  [the longest x1 33.8 us: local(): lax.all_gather(memory_gain, ('dp', 'blk'), axis=0, tiled=True)]
    all_to_all x0 -> x4, waiting for transfers between devices: none -> 81 us  [the longest x2 66.2 us: to_heads(): moved = lax.all_to_all(packed, 'blk', 0, 0)]
    unnamed x77 -> x359, local copies, waits for them, and re-layouts: 15.2 us -> 81.9 us
  transfers between devices with their start and end apart: 20 -> 55, of which waited for: 20 -> 30; matrix products, arithmetic and copies ran while one was open for 8% -> 30% of each run, Pallas kernels for 0% -> 0%
where the time goes in v1:
time: 1170 us; the launch traced here: 1160 us
  waiting for transfers between devices  614 us (52%)
  matrix products  257 us (22%)
  local copies, waits for them, and re-layouts  134 us (11%)
  starting transfers between devices  80.1 us (7%)
  other arithmetic  60.8 us (5%)
  between operations  16.8 us (1%)
    ppermute x49, waiting for transfers between devices, swap(): return lax.ppermute(array, axis, [(i, i ^ bit) for i in range(size)])  393 us
    dot_general x50, matrix products, dot_cols(): lax.dot_general(left, right, (((0,), (0,)), ((), ())), preferred_element_...  114 us
    all_gather x1, waiting for transfers between devices, local(): attn_full = lax.all_gather(attn_mine, ('dp', 'blk'), axis=0, tiled=True)  94.1 us
    unnamed x359, local copies, waits for them, and re-layouts  81.9 us
    all_to_all x2, waiting for transfers between devices, to_heads(): moved = lax.all_to_all(packed, 'blk', 0, 0)  66.2 us
    ppermute x49, starting transfers between devices, swap(): return lax.ppermute(array, axis, [(i, i ^ bit) for i in range(size)])  57.6 us
    dot_general x10, matrix products, plain_dot(): return jnp.dot(left, right, preferred_element_type=jnp.float32)  51.6 us
    dot_general x10, matrix products, dot_rows(): lax.dot_general(left, right, (((1,), (1,)), ((), ())), preferred_element_...  47.2 us
  transfers between devices with their start and end apart: 55, of which 30 were waited for; matrix products, arithmetic and copies ran while one was open for 30% of the time, Pallas kernels for 0%

profile of v1, /device:TPU:0, one launch (start us, length us, event | category | flops | bytes accessed | tf_op | source)
XLA Modules:
  0.0 1163.1 jit_solution(5886494857645004367)
XLA Ops:
  17.2 94.1 %all-gather.3.cloned.1.call-done = bf16[2048,4224]{1,0:T(8,128)(2,1)} async-done(((bf16[128,4224]{1,0:T(8,128)(2,1)}), bf16[2048,4224]{1,0:T(8,128)(2,1)}) %all-gather.3.cloned.1.call-update) | async-done | bytes 17301520 | tf_op jit(solution)/shard_map/all_gather | solution.py:172
  116.0 5.1 fusion.106
  121.2 4.0 fusion.109
  125.3 4.0 fusion.103
  131.3 4.9 all-to-all-start
  142.1 61.7 %all-to-all-done = bf16[4,384,768]{2,1,0:T(8,128)(2,1)} async-done(((bf16[4,384,768]{2,1,0:T(8,128)(2,1)}), bf16[4,384,768]{2,1,0:T(8,128)(2,1)}, u32[]{:S(2)}, u32[]{:S(2)}) %all-to-all-start) | async-done | bytes 2359328 | tf_op jit(solution)/shard_map/all_to_all | solution.py:126
  212.5 6.0 select_reduce_fusion
  218.5 7.3 fusion.1
  225.9 9.0 fusion.314
  238.0 3.9 all-to-all-start.1
  251.2 14.9 %all-to-all-done.1 = bf16[4,384,256]{2,1,0:T(8,128)(2,1)S(1)} async-done(((bf16[4,384,256]{2,1,0:T(8,128)(2,1)}), bf16[4,384,256]{2,1,0:T(8,128)(2,1)S(1)}, u32[]{:S(2)}, u32[]{:S(2)}) %all-to-all-start.1) | async-done | bytes 786464 | tf_op jit(solution)/shard_map/all_to_all | solution.py:135
  266.2 4.3 fusion.82
  275.5 29.8 %collective-permute-done = bf16[384,2048]{1,0:T(8,128)(2,1)S(1)} collective-permute-done((bf16[384,2048]{1,0:T(8,128)(2,1)S(1)}, bf16[384,2048]{1,0:T(8,128)(2,1)S(1)}, u32[]{:S(2)}, u32[]{:S(2)}) %collective-permute-start) | collective-permute-done | bytes 1572896 | tf_op jit(solution)/shard_map/ppermute | solution.py:40
  312.4 46.3 %all-gather.5.cloned.1.call-done = bf16[2048,8448]{0,1:T(8,128)(2,1)} async-done(((bf16[128,8448]{0,1:T(8,128)(2,1)}), bf16[2048,8448]{0,1:T(8,128)(2,1)}) %all-gather.5.cloned.1.call-update) | async-done | bytes 34603024 | tf_op jit(solution)/shard_map/all_gather | solution.py:184
  358.7 5.8 fusion.28
  364.5 5.4 fusion.64
  369.9 6.2 multiply_convert_fusion.5
  376.1 5.1 convolution_convert_fusion.1
  382.6 5.3 fusion.16
  387.9 5.3 fusion.67
  393.1 6.0 multiply_convert_fusion.3
  399.2 4.9 convolution_convert_fusion
  408.0 4.5 convolution_convert_fusion.3
  412.5 4.4 convolution_convert_fusion.2
  419.5 4.5 convolution_convert_fusion.5
  425.2 4.3 convolution_convert_fusion.4
  430.8 4.6 fusion.26
  435.4 4.6 fusion.18
  440.0 5.0 fusion.14
  445.1 5.3 add_convert_fusion.1
  454.2 4.6 fusion.12
  458.9 6.4 add_convert_fusion.3
  465.3 17.3 %collective-permute-done.2 = bf16[384,2048]{1,0:T(8,128)(2,1)S(1)} collective-permute-done((bf16[384,2048]{1,0:T(8,128)(2,1)S(1)}, bf16[384,2048]{1,0:T(8,128)(2,1)S(1)}, u32[]{:S(2)}, u32[]{:S(2)}) %collective-permute-start.2) | collective-permute-done | bytes 1572896 | tf_op jit(solution)/shard_map/ppermute | solution.py:40
  484.9 4.6 fusion.112
  491.2 8.5 all-to-all-start.2
  516.1 4.4 all-to-all-done.2
  528.7 12.7 %multiply_convert_fusion = bf16[2,1536,1536]{1,2,0:T(8,128)(2,1)} fusion(bf16[1536,2,128]{0,2,1:T(8,128)(2,1)} %copy.208, bf16[1536,2,128]{0,2,1:T(8,128)(2,1)} %bitcast.212, f32[2,1536,1536]{1,2,0:T(8,128)} %copy-done.6, f32[2,1536]{1,0:T(2,128)S(1)} %bitcast.217, f32[2,1536]{1,0:T(2,128)S(1)} %log_add_fusion, pred[1536,1536]{0,1:T(8,128)(4,1)S(1)} %copy-done.15), kind=kOutput, calls=%fused_computation | convolution fusion | flops 1236271104 | bytes 32268288 | tf_op jit(solution)/shard_map/qhd,khd->hqk/dot_general | solution.py:280
  541.4 10.2 fusion.95
  553.9 4.0 fusion.93
  574.9 5.1 all-to-all-start.3
  580.1 3.7 add_convert_fusion.8
  610.5 4.0 add_convert_fusion.4
  630.8 23.8 %collective-permute-done.26 = bf16[512,1344]{0,1:T(8,128)(2,1)S(1)} collective-permute-done((bf16[512,1344]{0,1:T(8,128)(2,1)S(1)}, bf16[512,1344]{0,1:T(8,128)(2,1)S(1)}, u32[]{:S(2)}, u32[]{:S(2)}) %collective-permute-start.26) | collective-permute-done | bytes 1376288 | tf_op jit(solution)/shard_map/ppermute | solution.py:40
  663.1 21.0 %collective-permute-done.42 = bf16[512,1344]{0,1:T(8,128)(2,1)S(1)} collective-permute-done((bf16[512,1344]{0,1:T(8,128)(2,1)S(1)}, bf16[512,1344]{0,1:T(8,128)(2,1)S(1)}, u32[]{:S(2)}, u32[]{:S(2)}) %collective-permute-start.42) | collective-permute-done | bytes 1376288 | tf_op jit(solution)/shard_map/ppermute | solution.py:40
  700.9 14.1 %collective-permute-done.38 = bf16[512,1408]{1,0:T(8,128)(2,1)} collective-permute-done((bf16[512,1408]{1,0:T(8,128)(2,1)}, bf16[512,1408]{1,0:T(8,128)(2,1)}, u32[]{:S(2)}, u32[]{:S(2)}) %collective-permute-start.38) | collective-permute-done | bytes 1441824 | tf_op jit(solution)/shard_map/ppermute | solution.py:40
  720.2 25.7 %collective-permute-done.30 = bf16[512,1408]{1,0:T(8,128)(2,1)} collective-permute-done((bf16[512,1408]{1,0:T(8,128)(2,1)}, bf16[512,1408]{1,0:T(8,128)(2,1)}, u32[]{:S(2)}, u32[]{:S(2)}) %collective-permute-start.30) | collective-permute-done | bytes 1441824 | tf_op jit(solution)/shard_map/ppermute | solution.py:40
  750.9 25.9 %collective-permute-done.22 = bf16[512,1408]{1,0:T(8,128)(2,1)} collective-permute-done((bf16[512,1408]{1,0:T(8,128)(2,1)}, bf16[512,1408]{1,0:T(8,128)(2,1)}, u32[]{:S(2)}, u32[]{:S(2)}) %collective-permute-start.22) | collective-permute-done | bytes 1441824 | tf_op jit(solution)/shard_map/ppermute | solution.py:40
  781.6 17.1 %collective-permute-done.18 = bf16[512,1024]{1,0:T(8,128)(2,1)} collective-permute-done((bf16[512,1024]{1,0:T(8,128)(2,1)}, bf16[512,1024]{1,0:T(8,128)(2,1)}, u32[]{:S(2)}, u32[]{:S(2)}) %collective-permute-start.18) | collective-permute-done | bytes 1048608 | tf_op jit(solution)/shard_map/ppermute | solution.py:40
  833.3 11.8 %collective-permute-done.31 = bf16[256,1408]{1,0:T(8,128)(2,1)} collective-permute-done((bf16[256,1408]{1,0:T(8,128)(2,1)}, bf16[256,1408]{1,0:T(8,128)(2,1)}, u32[]{:S(2)}, u32[]{:S(2)}) %collective-permute-start.31) | collective-permute-done | bytes 720928 | tf_op jit(solution)/shard_map/ppermute | solution.py:40
  849.4 15.0 %collective-permute-done.23 = bf16[256,1408]{1,0:T(8,128)(2,1)} collective-permute-done((bf16[256,1408]{1,0:T(8,128)(2,1)}, bf16[256,1408]{1,0:T(8,128)(2,1)}, u32[]{:S(2)}, u32[]{:S(2)}) %collective-permute-start.23) | collective-permute-done | bytes 720928 | tf_op jit(solution)/shard_map/ppermute | solution.py:40
  871.0 4.0 collective-permute-done.36
  879.6 27.7 %collective-permute-done.28 = bf16[128,1344]{1,0:T(8,128)(2,1)S(1)} collective-permute-done((bf16[128,1344]{1,0:T(8,128)(2,1)S(1)}, bf16[128,1344]{1,0:T(8,128)(2,1)S(1)}, u32[]{:S(2)}, u32[]{:S(2)}) %collective-permute-start.28) | collective-permute-done | bytes 344096 | tf_op jit(solution)/shard_map/ppermute | solution.py:40
  913.6 14.7 %collective-permute-done.40 = bf16[128,1408]{1,0:T(8,128)(2,1)S(1)} collective-permute-done((bf16[128,1408]{1,0:T(8,128)(2,1)S(1)}, bf16[128,1408]{1,0:T(8,128)(2,1)S(1)}, u32[]{:S(2)}, u32[]{:S(2)}) %collective-permute-start.40) | collective-permute-done | bytes 360480 | tf_op jit(solution)/shard_map/ppermute | solution.py:40
  953.8 4.0 fusion.42
  957.9 4.1 add_convert_fusion
  963.7 4.1 fusion.79
  978.0 21.3 %collective-permute-done.4 = bf16[384,2048]{1,0:T(8,128)(2,1)S(1)} collective-permute-done((bf16[384,2048]{1,0:T(8,128)(2,1)S(1)}, bf16[384,2048]{1,0:T(8,128)(2,1)S(1)}, u32[]{:S(2)}, u32[]{:S(2)}) %collective-permute-start.4) | collective-permute-done | bytes 1572896 | tf_op jit(solution)/shard_map/ppermute | solution.py:40
  1000.6 31.4 %collective-permute-done.3 = bf16[384,2048]{1,0:T(8,128)(2,1)S(1)} collective-permute-done((bf16[384,2048]{1,0:T(8,128)(2,1)S(1)}, bf16[384,2048]{1,0:T(8,128)(2,1)S(1)}, u32[]{:S(2)}, u32[]{:S(2)}) %collective-permute-start.3) | collective-permute-done | bytes 1572896 | tf_op jit(solution)/shard_map/ppermute | solution.py:40
  1036.3 6.6 fusion.59
  1054.3 19.2 %collective-permute-done.14 = bf16[512,1024]{1,0:T(8,128)(2,1)S(1)} collective-permute-done((bf16[512,1024]{1,0:T(8,128)(2,1)S(1)}, bf16[512,1024]{1,0:T(8,128)(2,1)S(1)}, u32[]{:S(2)}, u32[]{:S(2)}) %collective-permute-start.14) | collective-permute-done | bytes 1048608 | tf_op jit(solution)/shard_map/ppermute | solution.py:40
  1076.2 19.9 %collective-permute-done.10 = bf16[512,1024]{1,0:T(8,128)(2,1)S(1)} collective-permute-done((bf16[512,1024]{1,0:T(8,128)(2,1)S(1)}, bf16[512,1024]{1,0:T(8,128)(2,1)S(1)}, u32[]{:S(2)}, u32[]{:S(2)}) %collective-permute-start.10) | collective-permute-done | bytes 1048608 | tf_op jit(solution)/shard_map/ppermute | solution.py:40
  1098.6 17.6 %collective-permute-done.6 = bf16[512,1024]{1,0:T(8,128)(2,1)S(1)} collective-permute-done((bf16[512,1024]{1,0:T(8,128)(2,1)S(1)}, bf16[512,1024]{1,0:T(8,128)(2,1)S(1)}, u32[]{:S(2)}, u32[]{:S(2)}) %collective-permute-start.6) | collective-permute-done | bytes 1048608 | tf_op jit(solution)/shard_map/ppermute | solution.py:40
  1124.6 12.9 %collective-permute-done.7 = bf16[256,1024]{1,0:T(8,128)(2,1)S(1)} collective-permute-done((bf16[256,1024]{1,0:T(8,128)(2,1)S(1)}, bf16[256,1024]{1,0:T(8,128)(2,1)S(1)}, u32[]{:S(2)}, u32[]{:S(2)}) %collective-permute-start.7) | collective-permute-done | bytes 524320 | tf_op jit(solution)/shard_map/ppermute | solution.py:40
  1139.9 11.4 collective-permute-done.12
  (582 shorter events, 331.2 us)
Async XLA Ops:
  7.2 104.1 %all-gather.3.cloned.1.call-start = ((), (), s32[]{:S(2)}) async-start(), calls=%async_computation.4 | async-start | bytes 18382848 | tf_op jit(solution)/shard_map/all_gather | solution.py:172
  12.1 346.5 %all-gather.5.cloned.1.call-start = ((), (), s32[]{:S(2)}) async-start(), calls=%async_computation.5 | async-start | bytes 36765696 | tf_op jit(solution)/shard_map/all_gather | solution.py:184
  16.4 94.9 %copy-start.1 = (bf16[384,2048]{1,0:T(8,128)(2,1)S(1)}, bf16[384,2048]{1,0:T(8,128)(2,1)}, u32[]{:S(2)}) copy-start(bf16[384,2048]{1,0:T(8,128)(2,1)} %param.14) | copy-start | bytes 4718596
  17.2 94.5 %copy-start.4 = (bf16[384,2048]{1,0:T(8,128)(2,1)S(1)}, bf16[384,2048]{1,0:T(8,128)(2,1)}, u32[]{:S(2)}) copy-start(bf16[384,2048]{1,0:T(8,128)(2,1)} %param.15) | copy-start | bytes 4718596
  131.3 72.5 %all-to-all-start = ((bf16[4,384,768]{2,1,0:T(8,128)(2,1)}), bf16[4,384,768]{2,1,0:T(8,128)(2,1)}, u32[]{:S(2)}, u32[]{:S(2)}) async-start(bf16[4,384,768]{2,1,0:T(8,128)(2,1)} %pad_maximum_fusion), calls=%async_computation | async-start | bytes 4718592 | tf_op jit(solution)/shard_map/all_to_all | solution.py:126
  238.0 28.0 %all-to-all-start.1 = ((bf16[4,384,256]{2,1,0:T(8,128)(2,1)}), bf16[4,384,256]{2,1,0:T(8,128)(2,1)S(1)}, u32[]{:S(2)}, u32[]{:S(2)}) async-start(bf16[4,384,256]{2,1,0:T(8,128)(2,1)} %copy.163), calls=%async_computation.1 | async-start | bytes 1572864 | tf_op jit(solution)/shard_map/all_to_all | solution.py:135
  266.1 247.4 %copy-start.64 = (bf16[384,256]{1,0:T(8,128)(2,1)}, bf16[384,256]{1,0:T(8,128)(2,1)S(1)}, u32[]{:S(2)}) copy-start(bf16[384,256]{1,0:T(8,128)(2,1)S(1)} %get-tuple-element.154) | copy-start | bytes 589828
  270.5 34.7 %collective-permute-start = (bf16[384,2048]{1,0:T(8,128)(2,1)S(1)}, bf16[384,2048]{1,0:T(8,128)(2,1)S(1)}, u32[]{:S(2)}, u32[]{:S(2)}) collective-permute-start(bf16[384,2048]{1,0:T(8,128)(2,1)S(1)} %fusion.82), channel_id=1, source_target_pairs={{0,1},{1,0},{2,3},{3,2},{4,5},{5,4},{6,7},{7,6},{8,9},{9,8},{10,11... | collective-permute-start | bytes 4718600 | tf_op jit(solution)/shard_map/ppermute | solution.py:40
  312.4 267.7 %copy-start.109 = (bf16[384,128]{1,0:T(8,128)(2,1)}, bf16[384,128]{1,0:T(8,128)(2,1)S(1)}, u32[]{:S(2)}) copy-start(bf16[384,128]{1,0:T(8,128)(2,1)S(1)} %get-tuple-element.118) | copy-start | bytes 294916
  376.1 54.7 %copy-start.35 = (bf16[384,1408]{1,0:T(8,128)(2,1)}, bf16[384,1408]{1,0:T(8,128)(2,1)S(1)}, u32[]{:S(2)}) copy-start(bf16[384,1408]{1,0:T(8,128)(2,1)S(1)} %get-tuple-element.81) | copy-start | bytes 3244036
  376.1 68.9 %copy-start.31 = (bf16[384,1408]{1,0:T(8,128)(2,1)}, bf16[384,1408]{1,0:T(8,128)(2,1)S(1)}, u32[]{:S(2)}) copy-start(bf16[384,1408]{1,0:T(8,128)(2,1)S(1)} %get-tuple-element.80) | copy-start | bytes 3244036
  376.1 82.7 %copy-start.39 = (bf16[384,1408]{1,0:T(8,128)(2,1)}, bf16[384,1408]{1,0:T(8,128)(2,1)S(1)}, u32[]{:S(2)}) copy-start(bf16[384,1408]{1,0:T(8,128)(2,1)S(1)} %get-tuple-element.82) | copy-start | bytes 3244036
  399.2 55.1 %copy-start.23 = (bf16[384,1408]{1,0:T(8,128)(2,1)}, bf16[384,1408]{1,0:T(8,128)(2,1)S(1)}, u32[]{:S(2)}) copy-start(bf16[384,1408]{1,0:T(8,128)(2,1)S(1)} %get-tuple-element.85) | copy-start | bytes 3244036
  450.4 32.2 %collective-permute-start.2 = (bf16[384,2048]{1,0:T(8,128)(2,1)S(1)}, bf16[384,2048]{1,0:T(8,128)(2,1)S(1)}, u32[]{:S(2)}, u32[]{:S(2)}) collective-permute-start(bf16[384,2048]{1,0:T(8,128)(2,1)S(1)} %add_convert_fusion.1), channel_id=1, source_target_pairs={{0,1},{1,0},{2,3},{3,2},{4,5},{5,4},{6,7},{7,6},{8,9},{9,8},{10,11... | collective-permute-start | bytes 4718600 | tf_op jit(solution)/shard_map/ppermute | solution.py:40
  453.2 155.7 %collective-permute-start.37 = (bf16[1024,1408]{1,0:T(8,128)(2,1)}, bf16[1024,1408]{1,0:T(8,128)(2,1)}, u32[]{:S(2)}, u32[]{:S(2)}) collective-permute-start(bf16[1024,1408]{1,0:T(8,128)(2,1)} %convolution_convert_fusion.1), channel_id=1, source_target_pairs={{0,8},{8,0},{16,24},{24,16},{1,9},{9,1},{17,25},{25,17},{2,10},{10... | collective-permute-start | bytes 8650760 | tf_op jit(solution)/shard_map/ppermute | solution.py:40
  453.2 138.6 %collective-permute-start.41 = (bf16[1024,1344]{0,1:T(8,128)(2,1)}, bf16[1024,1344]{0,1:T(8,128)(2,1)}, u32[]{:S(2)}, u32[]{:S(2)}) collective-permute-start(bf16[1024,1344]{0,1:T(8,128)(2,1)} %convolution_convert_fusion), channel_id=1, source_target_pairs={{0,8},{8,0},{16,24},{24,16},{1,9},{9,1},{17,25},{25,17},{2,10},{10... | collective-permute-start | bytes 8257544 | tf_op jit(solution)/shard_map/ppermute | solution.py:40
  453.7 160.8 %collective-permute-start.29 = (bf16[1024,1408]{1,0:T(8,128)(2,1)}, bf16[1024,1408]{1,0:T(8,128)(2,1)}, u32[]{:S(2)}, u32[]{:S(2)}) collective-permute-start(bf16[1024,1408]{1,0:T(8,128)(2,1)} %convolution_convert_fusion.3), channel_id=1, source_target_pairs={{0,8},{8,0},{16,24},{24,16},{1,9},{9,1},{17,25},{25,17},{2,10},{10... | collective-permute-start | bytes 8650760 | tf_op jit(solution)/shard_map/ppermute | solution.py:40
  453.7 126.3 %collective-permute-start.33 = (bf16[1024,1344]{0,1:T(8,128)(2,1)}, bf16[1024,1344]{0,1:T(8,128)(2,1)}, u32[]{:S(2)}, u32[]{:S(2)}) collective-permute-start(bf16[1024,1344]{0,1:T(8,128)(2,1)} %convolution_convert_fusion.2), channel_id=1, source_target_pairs={{0,8},{8,0},{16,24},{24,16},{1,9},{9,1},{17,25},{25,17},{2,10},{10... | collective-permute-start | bytes 8257544 | tf_op jit(solution)/shard_map/ppermute | solution.py:40
  482.6 103.3 %collective-permute-start.25 = (bf16[1024,1344]{0,1:T(8,128)(2,1)}, bf16[1024,1344]{0,1:T(8,128)(2,1)}, u32[]{:S(2)}, u32[]{:S(2)}) collective-permute-start(bf16[1024,1344]{0,1:T(8,128)(2,1)} %convolution_convert_fusion.4), channel_id=1, source_target_pairs={{0,8},{8,0},{16,24},{24,16},{1,9},{9,1},{17,25},{25,17},{2,10},{10... | collective-permute-start | bytes 8257544 | tf_op jit(solution)/shard_map/ppermute | solution.py:40
  491.2 29.4 %all-to-all-start.2 = ((bf16[4,384,256]{2,1,0:T(8,128)(2,1)}), bf16[4,384,256]{2,1,0:T(8,128)(2,1)}, u32[]{:S(2)}, u32[]{:S(2)}) async-start(bf16[4,384,256]{2,1,0:T(8,128)(2,1)} %pad_maximum_fusion.6), calls=%async_computation.2 | async-start | bytes 1572864 | tf_op jit(solution)/shard_map/all_to_all | solution.py:126
  574.9 377.0 %all-to-all-start.3 = ((bf16[4,384,768]{2,1,0:T(8,128)(2,1)}), bf16[4,384,768]{2,1,0:T(8,128)(2,1)}, u32[]{:S(2)}, u32[]{:S(2)}) async-start(bf16[4,384,768]{2,1,0:T(8,128)(2,1)} %pad_maximum_fusion.1), calls=%async_computation.3 | async-start | bytes 4718592 | tf_op jit(solution)/shard_map/all_to_all | solution.py:135
  580.0 38.3 %collective-permute-start.21 = (bf16[1024,1408]{1,0:T(8,128)(2,1)}, bf16[1024,1408]{1,0:T(8,128)(2,1)}, u32[]{:S(2)}, u32[]{:S(2)}) collective-permute-start(bf16[1024,1408]{1,0:T(8,128)(2,1)} %convolution_convert_fusion.5), channel_id=1, source_target_pairs={{0,8},{8,0},{16,24},{24,16},{1,9},{9,1},{17,25},{25,17},{2,10},{10... | collective-permute-start | bytes 8650760 | tf_op jit(solution)/shard_map/ppermute | solution.py:40
  585.8 37.8 %collective-permute-start.17 = (bf16[1024,1024]{1,0:T(8,128)(2,1)}, bf16[1024,1024]{1,0:T(8,128)(2,1)}, u32[]{:S(2)}, u32[]{:S(2)}) collective-permute-start(bf16[1024,1024]{1,0:T(8,128)(2,1)} %convolution_convert_fusion.6), channel_id=1, source_target_pairs={{0,8},{8,0},{16,24},{24,16},{1,9},{9,1},{17,25},{25,17},{2,10},{10... | collective-permute-start | bytes 6291464 | tf_op jit(solution)/shard_map/ppermute | solution.py:40
  591.8 35.2 %collective-permute-start.34 = (bf16[512,1344]{0,1:T(8,128)(2,1)}, bf16[512,1344]{0,1:T(8,128)(2,1)}, u32[]{:S(2)}, u32[]{:S(2)}) collective-permute-start(bf16[512,1344]{0,1:T(8,128)(2,1)} %add_convert_fusion.8), channel_id=1, source_target_pairs={{0,16},{8,24},{16,0},{24,8},{1,17},{9,25},{17,1},{25,9},{2,18},{10... | collective-permute-start | bytes 4128776 | tf_op jit(solution)/shard_map/ppermute | solution.py:40
  608.9 427.3 %collective-permute-start.1 = (bf16[384,2048]{1,0:T(8,128)(2,1)}, bf16[384,2048]{1,0:T(8,128)(2,1)}, u32[]{:S(2)}, u32[]{:S(2)}) collective-permute-start(bf16[384,2048]{1,0:T(8,128)(2,1)} %add_convert_fusion.3), channel_id=1, source_target_pairs={{0,1},{1,0},{2,3},{3,2},{4,5},{5,4},{6,7},{7,6},{8,9},{9,8},{10,11... | collective-permute-start | bytes 4718600 | tf_op jit(solution)/shard_map/ppermute | solution.py:40
  614.5 40.0 %collective-permute-start.26 = (bf16[512,1344]{0,1:T(8,128)(2,1)S(1)}, bf16[512,1344]{0,1:T(8,128)(2,1)S(1)}, u32[]{:S(2)}, u32[]{:S(2)}) collective-permute-start(bf16[512,1344]{0,1:T(8,128)(2,1)S(1)} %copy-done.140), channel_id=1, source_target_pairs={{0,16},{8,24},{16,0},{24,8},{1,17},{9,25},{17,1},{25,9},{2,18},{10... | collective-permute-start | bytes 4128776 | tf_op jit(solution)/shard_map/ppermute | solution.py:40
  618.3 65.7 %collective-permute-start.42 = (bf16[512,1344]{0,1:T(8,128)(2,1)S(1)}, bf16[512,1344]{0,1:T(8,128)(2,1)S(1)}, u32[]{:S(2)}, u32[]{:S(2)}) collective-permute-start(bf16[512,1344]{0,1:T(8,128)(2,1)S(1)} %copy-done.139), channel_id=1, source_target_pairs={{0,16},{8,24},{16,0},{24,8},{1,17},{9,25},{17,1},{25,9},{2,18},{10... | collective-permute-start | bytes 4128776 | tf_op jit(solution)/shard_map/ppermute | solution.py:40
  623.7 91.3 %collective-permute-start.38 = (bf16[512,1408]{1,0:T(8,128)(2,1)}, bf16[512,1408]{1,0:T(8,128)(2,1)}, u32[]{:S(2)}, u32[]{:S(2)}) collective-permute-start(bf16[512,1408]{1,0:T(8,128)(2,1)} %add_convert_fusion.4), channel_id=1, source_target_pairs={{0,16},{8,24},{16,0},{24,8},{1,17},{9,25},{17,1},{25,9},{2,18},{10... | collective-permute-start | bytes 4325384 | tf_op jit(solution)/shard_map/ppermute | solution.py:40
  627.0 118.9 %collective-permute-start.30 = (bf16[512,1408]{1,0:T(8,128)(2,1)}, bf16[512,1408]{1,0:T(8,128)(2,1)}, u32[]{:S(2)}, u32[]{:S(2)}) collective-permute-start(bf16[512,1408]{1,0:T(8,128)(2,1)} %add_convert_fusion.5), channel_id=1, source_target_pairs={{0,16},{8,24},{16,0},{24,8},{1,17},{9,25},{17,1},{25,9},{2,18},{10... | collective-permute-start | bytes 4325384 | tf_op jit(solution)/shard_map/ppermute | solution.py:40
  654.5 122.3 %collective-permute-start.22 = (bf16[512,1408]{1,0:T(8,128)(2,1)}, bf16[512,1408]{1,0:T(8,128)(2,1)}, u32[]{:S(2)}, u32[]{:S(2)}) collective-permute-start(bf16[512,1408]{1,0:T(8,128)(2,1)} %add_convert_fusion.6), channel_id=1, source_target_pairs={{0,16},{8,24},{16,0},{24,8},{1,17},{9,25},{17,1},{25,9},{2,18},{10... | collective-permute-start | bytes 4325384 | tf_op jit(solution)/shard_map/ppermute | solution.py:40
  684.0 114.6 %collective-permute-start.18 = (bf16[512,1024]{1,0:T(8,128)(2,1)}, bf16[512,1024]{1,0:T(8,128)(2,1)}, u32[]{:S(2)}, u32[]{:S(2)}) collective-permute-start(bf16[512,1024]{1,0:T(8,128)(2,1)} %add_convert_fusion.10), channel_id=1, source_target_pairs={{0,16},{8,24},{16,0},{24,8},{1,17},{9,25},{17,1},{25,9},{2,18},{10... | collective-permute-start | bytes 3145736 | tf_op jit(solution)/shard_map/ppermute | solution.py:40
  715.0 88.1 %collective-permute-start.43 = (bf16[256,1344]{0,1:T(8,128)(2,1)}, bf16[256,1344]{0,1:T(8,128)(2,1)S(1)}, u32[]{:S(2)}, u32[]{:S(2)}) collective-permute-start(bf16[256,1344]{0,1:T(8,128)(2,1)} %add_convert_fusion.17), channel_id=1, source_target_pairs={{0,2},{2,0},{4,6},{6,4},{1,3},{3,1},{5,7},{7,5},{8,10},{10,8},{12,... | collective-permute-start | bytes 2064392 | tf_op jit(solution)/shard_map/ppermute | solution.py:40
  720.2 58.6 %copy-start.33 = (bf16[384,1408]{1,0:T(8,128)(2,1)S(1)}, bf16[384,1408]{1,0:T(8,128)(2,1)}, u32[]{:S(2)}) copy-start(bf16[384,1408]{1,0:T(8,128)(2,1)} %copy-done.31) | copy-start | bytes 3244036
  745.9 62.4 %collective-permute-start.35 = (bf16[256,1344]{0,1:T(8,128)(2,1)}, bf16[256,1344]{0,1:T(8,128)(2,1)}, u32[]{:S(2)}, u32[]{:S(2)}) collective-permute-start(bf16[256,1344]{0,1:T(8,128)(2,1)} %add_convert_fusion.18), channel_id=1, source_target_pairs={{0,2},{2,0},{4,6},{6,4},{1,3},{3,1},{5,7},{7,5},{8,10},{10,8},{12,... | collective-permute-start | bytes 2064392 | tf_op jit(solution)/shard_map/ppermute | solution.py:40
  776.8 39.6 %collective-permute-start.27 = (bf16[256,1344]{0,1:T(8,128)(2,1)}, bf16[256,1344]{0,1:T(8,128)(2,1)}, u32[]{:S(2)}, u32[]{:S(2)}) collective-permute-start(bf16[256,1344]{0,1:T(8,128)(2,1)} %add_convert_fusion.19), channel_id=1, source_target_pairs={{0,2},{2,0},{4,6},{6,4},{1,3},{3,1},{5,7},{7,5},{8,10},{10,8},{12,... | collective-permute-start | bytes 2064392 | tf_op jit(solution)/shard_map/ppermute | solution.py:40
  798.7 29.6 %collective-permute-start.39 = (bf16[256,1408]{1,0:T(8,128)(2,1)}, bf16[256,1408]{1,0:T(8,128)(2,1)}, u32[]{:S(2)}, u32[]{:S(2)}) collective-permute-start(bf16[256,1408]{1,0:T(8,128)(2,1)} %add_convert_fusion.14), channel_id=1, source_target_pairs={{0,2},{2,0},{4,6},{6,4},{1,3},{3,1},{5,7},{7,5},{8,10},{10,8},{12,... | collective-permute-start | bytes 2162696 | tf_op jit(solution)/shard_map/ppermute | solution.py:40
  803.1 41.9 %collective-permute-start.31 = (bf16[256,1408]{1,0:T(8,128)(2,1)}, bf16[256,1408]{1,0:T(8,128)(2,1)}, u32[]{:S(2)}, u32[]{:S(2)}) collective-permute-start(bf16[256,1408]{1,0:T(8,128)(2,1)} %add_convert_fusion.15), channel_id=1, source_target_pairs={{0,2},{2,0},{4,6},{6,4},{1,3},{3,1},{5,7},{7,5},{8,10},{10,8},{12,... | collective-permute-start | bytes 2162696 | tf_op jit(solution)/shard_map/ppermute | solution.py:40
  808.3 56.1 %collective-permute-start.23 = (bf16[256,1408]{1,0:T(8,128)(2,1)}, bf16[256,1408]{1,0:T(8,128)(2,1)}, u32[]{:S(2)}, u32[]{:S(2)}) collective-permute-start(bf16[256,1408]{1,0:T(8,128)(2,1)} %add_convert_fusion.16), channel_id=1, source_target_pairs={{0,2},{2,0},{4,6},{6,4},{1,3},{3,1},{5,7},{7,5},{8,10},{10,8},{12,... | collective-permute-start | bytes 2162696 | tf_op jit(solution)/shard_map/ppermute | solution.py:40
  816.4 91.9 %collective-permute-start.19 = (bf16[256,1024]{1,0:T(8,128)(2,1)}, bf16[256,1024]{1,0:T(8,128)(2,1)}, u32[]{:S(2)}, u32[]{:S(2)}) collective-permute-start(bf16[256,1024]{1,0:T(8,128)(2,1)} %add_convert_fusion.20), channel_id=1, source_target_pairs={{0,2},{2,0},{4,6},{6,4},{1,3},{3,1},{5,7},{7,5},{8,10},{10,8},{12,... | collective-permute-start | bytes 1572872 | tf_op jit(solution)/shard_map/ppermute | solution.py:40
  828.3 40.4 %collective-permute-start.44 = (bf16[128,1344]{1,0:T(8,128)(2,1)}, bf16[128,1344]{1,0:T(8,128)(2,1)S(1)}, u32[]{:S(2)}, u32[]{:S(2)}) collective-permute-start(bf16[128,1344]{1,0:T(8,128)(2,1)} %add_convert_fusion.24), channel_id=1, source_target_pairs={{0,4},{2,6},{4,0},{6,2},{1,5},{3,7},{5,1},{7,3},{8,12},{10,14},{12... | collective-permute-start | bytes 1032200 | tf_op jit(solution)/shard_map/ppermute | solution.py:40
  845.1 30.0 %collective-permute-start.36 = (bf16[128,1344]{1,0:T(8,128)(2,1)S(1)}, bf16[128,1344]{1,0:T(8,128)(2,1)S(1)}, u32[]{:S(2)}, u32[]{:S(2)}) collective-permute-start(bf16[128,1344]{1,0:T(8,128)(2,1)S(1)} %copy-done.61), channel_id=1, source_target_pairs={{0,4},{2,6},{4,0},{6,2},{1,5},{3,7},{5,1},{7,3},{8,12},{10,14},{12... | collective-permute-start | bytes 1032200 | tf_op jit(solution)/shard_map/ppermute | solution.py:40
  864.4 42.9 %collective-permute-start.28 = (bf16[128,1344]{1,0:T(8,128)(2,1)S(1)}, bf16[128,1344]{1,0:T(8,128)(2,1)S(1)}, u32[]{:S(2)}, u32[]{:S(2)}) collective-permute-start(bf16[128,1344]{1,0:T(8,128)(2,1)S(1)} %copy-done.62), channel_id=1, source_target_pairs={{0,4},{2,6},{4,0},{6,2},{1,5},{3,7},{5,1},{7,3},{8,12},{10,14},{12... | collective-permute-start | bytes 1032200 | tf_op jit(solution)/shard_map/ppermute | solution.py:40
  868.7 59.6 %collective-permute-start.40 = (bf16[128,1408]{1,0:T(8,128)(2,1)S(1)}, bf16[128,1408]{1,0:T(8,128)(2,1)S(1)}, u32[]{:S(2)}, u32[]{:S(2)}) collective-permute-start(bf16[128,1408]{1,0:T(8,128)(2,1)S(1)} %add_convert_fusion.25), channel_id=1, source_target_pairs={{0,4},{2,6},{4,0},{6,2},{1,5},{3,7},{5,1},{7,3},{8,12},{10,14},{12... | collective-permute-start | bytes 1081352 | tf_op jit(solution)/shard_map/ppermute | solution.py:40
  875.1 61.1 %collective-permute-start.32 = (bf16[128,1408]{1,0:T(8,128)(2,1)}, bf16[128,1408]{1,0:T(8,128)(2,1)}, u32[]{:S(2)}, u32[]{:S(2)}) collective-permute-start(bf16[128,1408]{1,0:T(8,128)(2,1)} %add_convert_fusion.27), channel_id=1, source_target_pairs={{0,4},{2,6},{4,0},{6,2},{1,5},{3,7},{5,1},{7,3},{8,12},{10,14},{12... | collective-permute-start | bytes 1081352 | tf_op jit(solution)/shard_map/ppermute | solution.py:40
  907.3 36.6 %collective-permute-start.24 = (bf16[128,1408]{1,0:T(8,128)(2,1)}, bf16[128,1408]{1,0:T(8,128)(2,1)}, u32[]{:S(2)}, u32[]{:S(2)}) collective-permute-start(bf16[128,1408]{1,0:T(8,128)(2,1)} %add_convert_fusion.29), channel_id=1, source_target_pairs={{0,4},{2,6},{4,0},{6,2},{1,5},{3,7},{5,1},{7,3},{8,12},{10,14},{12... | collective-permute-start | bytes 1081352 | tf_op jit(solution)/shard_map/ppermute | solution.py:40
  910.7 39.0 %collective-permute-start.20 = (bf16[128,1024]{1,0:T(8,128)(2,1)}, bf16[128,1024]{1,0:T(8,128)(2,1)S(1)}, u32[]{:S(2)}, u32[]{:S(2)}) collective-permute-start(bf16[128,1024]{1,0:T(8,128)(2,1)} %add_convert_fusion.30), channel_id=1, source_target_pairs={{0,4},{2,6},{4,0},{6,2},{1,5},{3,7},{5,1},{7,3},{8,12},{10,14},{12... | collective-permute-start | bytes 786440 | tf_op jit(solution)/shard_map/ppermute | solution.py:40
  961.9 37.3 %collective-permute-start.4 = (bf16[384,2048]{1,0:T(8,128)(2,1)S(1)}, bf16[384,2048]{1,0:T(8,128)(2,1)S(1)}, u32[]{:S(2)}, u32[]{:S(2)}) collective-permute-start(bf16[384,2048]{1,0:T(8,128)(2,1)S(1)} %add_convert_fusion), channel_id=1, source_target_pairs={{0,1},{1,0},{2,3},{3,2},{4,5},{5,4},{6,7},{7,6},{8,9},{9,8},{10,11... | collective-permute-start | bytes 4718600 | tf_op jit(solution)/shard_map/ppermute | solution.py:40
  967.8 64.1 %collective-permute-start.3 = (bf16[384,2048]{1,0:T(8,128)(2,1)S(1)}, bf16[384,2048]{1,0:T(8,128)(2,1)S(1)}, u32[]{:S(2)}, u32[]{:S(2)}) collective-permute-start(bf16[384,2048]{1,0:T(8,128)(2,1)S(1)} %fusion.79), channel_id=1, source_target_pairs={{0,1},{1,0},{2,3},{3,2},{4,5},{5,4},{6,7},{7,6},{8,9},{9,8},{10,11... | collective-permute-start | bytes 4718600 | tf_op jit(solution)/shard_map/ppermute | solution.py:40
  971.0 75.6 %collective-permute-start.13 = (bf16[1024,1024]{1,0:T(8,128)(2,1)}, bf16[1024,1024]{1,0:T(8,128)(2,1)S(1)}, u32[]{:S(2)}, u32[]{:S(2)}) collective-permute-start(bf16[1024,1024]{1,0:T(8,128)(2,1)} %convolution_convert_fusion.7), channel_id=1, source_target_pairs={{0,8},{8,0},{16,24},{24,16},{1,9},{9,1},{17,25},{25,17},{2,10},{10... | collective-permute-start | bytes 6291464 | tf_op jit(solution)/shard_map/ppermute | solution.py:40
  972.3 75.7 %collective-permute-start.9 = (bf16[1024,1024]{1,0:T(8,128)(2,1)S(1)}, bf16[1024,1024]{1,0:T(8,128)(2,1)S(1)}, u32[]{:S(2)}, u32[]{:S(2)}) collective-permute-start(bf16[1024,1024]{1,0:T(8,128)(2,1)S(1)} %convolution_convert_fusion.8), channel_id=1, source_target_pairs={{0,8},{8,0},{16,24},{24,16},{1,9},{9,1},{17,25},{25,17},{2,10},{10... | collective-permute-start | bytes 6291464 | tf_op jit(solution)/shard_map/ppermute | solution.py:40
  999.3 51.0 %collective-permute-start.5 = (bf16[1024,1024]{1,0:T(8,128)(2,1)S(1)}, bf16[1024,1024]{1,0:T(8,128)(2,1)S(1)}, u32[]{:S(2)}, u32[]{:S(2)}) collective-permute-start(bf16[1024,1024]{1,0:T(8,128)(2,1)S(1)} %convolution_convert_fusion.9), channel_id=1, source_target_pairs={{0,8},{8,0},{16,24},{24,16},{1,9},{9,1},{17,25},{25,17},{2,10},{10... | collective-permute-start | bytes 6291464 | tf_op jit(solution)/shard_map/ppermute | solution.py:40
  1033.4 1.2 collective-permute-start.45
  1034.7 8.2 collective-permute-start.46
  1042.9 3.7 collective-permute-start.47
  1046.6 7.8 collective-permute-start.48
  1047.4 26.2 %collective-permute-start.14 = (bf16[512,1024]{1,0:T(8,128)(2,1)S(1)}, bf16[512,1024]{1,0:T(8,128)(2,1)S(1)}, u32[]{:S(2)}, u32[]{:S(2)}) collective-permute-start(bf16[512,1024]{1,0:T(8,128)(2,1)S(1)} %add_convert_fusion.11), channel_id=1, source_target_pairs={{0,16},{8,24},{16,0},{24,8},{1,17},{9,25},{17,1},{25,9},{2,18},{10... | collective-permute-start | bytes 3145736 | tf_op jit(solution)/shard_map/ppermute | solution.py:40
  1048.8 47.3 %collective-permute-start.10 = (bf16[512,1024]{1,0:T(8,128)(2,1)S(1)}, bf16[512,1024]{1,0:T(8,128)(2,1)S(1)}, u32[]{:S(2)}, u32[]{:S(2)}) collective-permute-start(bf16[512,1024]{1,0:T(8,128)(2,1)S(1)} %add_convert_fusion.12), channel_id=1, source_target_pairs={{0,16},{8,24},{16,0},{24,8},{1,17},{9,25},{17,1},{25,9},{2,18},{10... | collective-permute-start | bytes 3145736 | tf_op jit(solution)/shard_map/ppermute | solution.py:40
  1051.1 65.1 %collective-permute-start.6 = (bf16[512,1024]{1,0:T(8,128)(2,1)S(1)}, bf16[512,1024]{1,0:T(8,128)(2,1)S(1)}, u32[]{:S(2)}, u32[]{:S(2)}) collective-permute-start(bf16[512,1024]{1,0:T(8,128)(2,1)S(1)} %add_convert_fusion.13), channel_id=1, source_target_pairs={{0,16},{8,24},{16,0},{24,8},{1,17},{9,25},{17,1},{25,9},{2,18},{10... | collective-permute-start | bytes 3145736 | tf_op jit(solution)/shard_map/ppermute | solution.py:40
  1074.1 44.9 %collective-permute-start.15 = (bf16[256,1024]{1,0:T(8,128)(2,1)S(1)}, bf16[256,1024]{1,0:T(8,128)(2,1)S(1)}, u32[]{:S(2)}, u32[]{:S(2)}) collective-permute-start(bf16[256,1024]{1,0:T(8,128)(2,1)S(1)} %add_convert_fusion.21), channel_id=1, source_target_pairs={{0,2},{2,0},{4,6},{6,4},{1,3},{3,1},{5,7},{7,5},{8,10},{10,8},{12,... | collective-permute-start | bytes 1572872 | tf_op jit(solution)/shard_map/ppermute | solution.py:40
  1096.5 25.0 %collective-permute-start.11 = (bf16[256,1024]{1,0:T(8,128)(2,1)S(1)}, bf16[256,1024]{1,0:T(8,128)(2,1)S(1)}, u32[]{:S(2)}, u32[]{:S(2)}) collective-permute-start(bf16[256,1024]{1,0:T(8,128)(2,1)S(1)} %add_convert_fusion.22), channel_id=1, source_target_pairs={{0,2},{2,0},{4,6},{6,4},{1,3},{3,1},{5,7},{7,5},{8,10},{10,8},{12,... | collective-permute-start | bytes 1572872 | tf_op jit(solution)/shard_map/ppermute | solution.py:40
  1116.7 20.9 %collective-permute-start.7 = (bf16[256,1024]{1,0:T(8,128)(2,1)S(1)}, bf16[256,1024]{1,0:T(8,128)(2,1)S(1)}, u32[]{:S(2)}, u32[]{:S(2)}) collective-permute-start(bf16[256,1024]{1,0:T(8,128)(2,1)S(1)} %add_convert_fusion.23), channel_id=1, source_target_pairs={{0,2},{2,0},{4,6},{6,4},{1,3},{3,1},{5,7},{7,5},{8,10},{10,8},{12,... | collective-permute-start | bytes 1572872 | tf_op jit(solution)/shard_map/ppermute | solution.py:40
  1120.3 18.6 %collective-permute-start.16 = (bf16[128,1024]{1,0:T(8,128)(2,1)S(1)}, bf16[128,1024]{1,0:T(8,128)(2,1)S(1)}, u32[]{:S(2)}, u32[]{:S(2)}) collective-permute-start(bf16[128,1024]{1,0:T(8,128)(2,1)S(1)} %add_convert_fusion.31), channel_id=1, source_target_pairs={{0,4},{2,6},{4,0},{6,2},{1,5},{3,7},{5,1},{7,3},{8,12},{10,14},{12... | collective-permute-start | bytes 786440 | tf_op jit(solution)/shard_map/ppermute | solution.py:40
  1122.8 28.4 %collective-permute-start.12 = (bf16[128,1024]{1,0:T(8,128)(2,1)S(1)}, bf16[128,1024]{1,0:T(8,128)(2,1)S(1)}, u32[]{:S(2)}, u32[]{:S(2)}) collective-permute-start(bf16[128,1024]{1,0:T(8,128)(2,1)S(1)} %add_convert_fusion.32), channel_id=1, source_target_pairs={{0,4},{2,6},{4,0},{6,2},{1,5},{3,7},{5,1},{7,3},{8,12},{10,14},{12... | collective-permute-start | bytes 786440 | tf_op jit(solution)/shard_map/ppermute | solution.py:40
  1138.8 16.0 %collective-permute-start.8 = (bf16[128,1024]{1,0:T(8,128)(2,1)S(1)}, bf16[128,1024]{1,0:T(8,128)(2,1)S(1)}, u32[]{:S(2)}, u32[]{:S(2)}) collective-permute-start(bf16[128,1024]{1,0:T(8,128)(2,1)S(1)} %add_convert_fusion.33), channel_id=1, source_target_pairs={{0,4},{2,6},{4,0},{6,2},{1,5},{3,7},{5,1},{7,3},{8,12},{10,14},{12... | collective-permute-start | bytes 786440 | tf_op jit(solution)/shard_map/ppermute | solution.py:40
  (136 other events, 2180.4 us)
Sparse Core Ops, SparseCore 0:
  12.2 98.9 all-gather.2
  113.3 245.3 all-gather.4

commit v2 on v1

--- a/solution.py
+++ b/solution.py
@@ -1,10 +1,14 @@
+import functools
 import math
 
 import jax
 import jax.numpy as jnp
 from jax import lax
+from jax.experimental import pallas as pl
+from jax.experimental.pallas import tpu as pltpu
 from jax.sharding import PartitionSpec as P
 
+MESH = pl.DeviceIdType.MESH
 HEAD = 128
 LANES = 128
 EPSILON = 1e-06
@@ -62,44 +66,164 @@
     steps = fold_steps()
     shards = 2 ** len(steps)
     part = width // shards
-    here = {axis: lax.axis_index(axis) for axis in ("dp", "blk")}
     offsets = []
     for place in range(shards):
-        flip = {"dp": 0, "blk": 0}
+        at = {axis: lax.axis_index(axis) for axis in ("dp", "blk")}
         for number, (axis, bit) in enumerate(steps):
             if place >> (len(steps) - 1 - number) & 1:
-                flip[axis] |= bit
-        shard = (here["dp"] ^ flip["dp"]) * lax.axis_size("blk") + (here["blk"] ^ flip["blk"])
-        offsets.append(shard * part)
+                at[axis] = flipped(at[axis], bit)
+        offsets.append((at["dp"] * lax.axis_size("blk") + at["blk"]) * part)
     return offsets, part
 
 
-def fold_columns(array):
-    offsets, part = fold_order(array.shape[1])
-    return jnp.concatenate(
-        [lax.dynamic_slice_in_dim(array, offset, part, axis=1) for offset in offsets], axis=1
-    )
-
-
-def fold_product(left, right, kind=jnp.bfloat16):
+def flipped(index, bit):
+    return index + bit * (1 - 2 * ((index // bit) % 2))
+
+
+def fold_kernel(steps, edges, tiles, width, slots, left_ref, right_ref, out_ref, *scratch):
+    count = len(steps)
+    held, load_sem, send_sem, recv_sem, credit = scratch[:5]
+    sent, got = scratch[5 : 5 + count], scratch[5 + count :]
+    lefts, features = held.shape[:2]
+    mesh_axes = ("dp", "blk", "heads")
+    here = {axis: lax.axis_index(axis) for axis in mesh_axes}
+    partners = []
+    for axis, bit in steps:
+        partners.append(
+            tuple(flipped(here[a], bit) if a == axis else here[a] for a in mesh_axes)
+        )
+    offsets, part = fold_order(features)
+    loads = []
+    for number in range(lefts):
+        for place, offset in enumerate(offsets):
+            loads.append(
+                pltpu.make_async_copy(
+                    left_ref.at[number, pl.ds(pl.multiple_of(offset, part), part)],
+                    held.at[number, pl.ds(place * part, part)],
+                    load_sem.at[number, place],
+                )
+            )
+    for load in loads:
+        load.start()
+    barrier = pltpu.get_barrier_semaphore()
+    for partner in partners:
+        pl.semaphore_signal(barrier, inc=1, device_id=partner, device_id_type=MESH)
+    pl.semaphore_wait(barrier, count)
+    for load in loads:
+        load.wait()
+
+    def transfer(step, tile):
+        return pltpu.make_async_remote_copy(
+            src_ref=sent[step].at[lax.rem(tile, 2)],
+            dst_ref=got[step].at[lax.rem(tile, slots)],
+            send_sem=send_sem.at[step, lax.rem(tile, 2)],
+            recv_sem=recv_sem.at[step, lax.rem(tile, slots)],
+            device_id=partners[step],
+            device_id_type=MESH,
+        )
+
+    def stage(number, tile):
+        slot = lax.rem(tile, slots)
+        if number > 0:
+            transfer(number - 1, tile).wait_recv()
+        last = number == count
+        low = 0 if last else features >> (number + 1)
+        high = features >> number
+        group = jnp.int32(0)
+        for edge in edges:
+            group = group + (tile >= edge).astype(jnp.int32)
+        columns = pl.ds(pl.multiple_of(tile * width, width), width)
+        total = jnp.dot(
+            held[group, low:high], right_ref[:, columns], preferred_element_type=jnp.float32
+        )
+        for earlier in range(number):
+            total = total + got[earlier][slot, low:high].astype(jnp.float32)
+        if last:
+            out_ref[:, columns] = total
+
+            @pl.when(tile < tiles - slots)
+            def _():
+                for step, partner in enumerate(partners):
+                    pl.semaphore_signal(
+                        credit.at[step], inc=1, device_id=partner, device_id_type=MESH
+                    )
+
+            return
+
+        @pl.when(tile >= 2)
+        def _():
+            transfer(number, tile).wait_send()
+
+        sent[number][lax.rem(tile, 2)] = total.astype(jnp.bfloat16)
+
+        @pl.when(tile >= slots)
+        def _():
+            pl.semaphore_wait(credit.at[number], 1)
+
+        transfer(number, tile).start()
+
+    def turn(index, carry):
+        for number in range(count + 1):
+            tile = index - number
+
+            @pl.when((tile >= 0) & (tile < tiles))
+            def _(number=number, tile=tile):
+                stage(number, tile)
+
+        return carry
+
+    lax.fori_loop(0, tiles + count, turn, 0)
+    for step in range(count):
+        for tile in range(max(0, tiles - 2), tiles):
+            transfer(step, jnp.int32(tile)).wait_send()
+
+
+def fold_products(groups, call, width=128, slots=8):
     steps = fold_steps()
-    size = left.shape[1]
-    pieces = []
-    for _ in steps:
-        size //= 2
-        pieces.append((size, 2 * size))
-    pieces.append((0, size))
-    arrived = []
-    for (axis, bit), (low, high) in zip(steps, pieces):
-        part = dot_cols(left[:, low:high], right)
-        for earlier in arrived:
-            part = part + earlier[low:high].astype(jnp.float32)
-        arrived.append(swap(part.astype(kind), axis, bit))
-    low, high = pieces[-1]
-    part = dot_cols(left[:, low:high], right)
-    for earlier in arrived:
-        part = part + earlier[low:high].astype(jnp.float32)
-    return part
+    count = len(steps)
+    lefts = jnp.stack([left.T for left, _ in groups], axis=0)
+    rights = jnp.concatenate([right for _, many in groups for right in many], axis=1)
+    edges, tiles = [], 0
+    for _, many in groups:
+        tiles += sum(right.shape[1] for right in many) // width
+        edges.append(tiles)
+    slots = min(slots, tiles)
+    number, features, rows = lefts.shape
+    sizes = [features >> (step + 1) for step in range(count)]
+    buffers = [pltpu.VMEM((2, size, width), jnp.bfloat16) for size in sizes]
+    buffers += [pltpu.VMEM((slots, size, width), jnp.bfloat16) for size in sizes]
+    folded = pl.pallas_call(
+        functools.partial(fold_kernel, steps, edges[:-1], tiles, width, slots),
+        out_shape=jax.ShapeDtypeStruct((features >> count, tiles * width), jnp.float32),
+        in_specs=[
+            pl.BlockSpec(memory_space=pl.ANY),
+            pl.BlockSpec(memory_space=pltpu.VMEM),
+        ],
+        out_specs=pl.BlockSpec(memory_space=pltpu.VMEM),
+        scratch_shapes=[
+            pltpu.VMEM((number, features, rows), jnp.bfloat16),
+            pltpu.SemaphoreType.DMA((number, 1 << count)),
+            pltpu.SemaphoreType.DMA((count, 2)),
+            pltpu.SemaphoreType.DMA((count, slots)),
+            pltpu.SemaphoreType.REGULAR((count,)),
+            *buffers,
+        ],
+        compiler_params=pltpu.CompilerParams(
+            collective_id=call, has_side_effects=True, vmem_limit_bytes=60 * 1024 * 1024
+        ),
+        cost_estimate=pl.CostEstimate(
+            flops=2 * features * rows * tiles * width,
+            bytes_accessed=tiles * width * features * 8,
+            transcendentals=0,
+        ),
+    )(lefts, rights)
+    shares, at = [], 0
+    for _, many in groups:
+        shares.append([])
+        for right in many:
+            shares[-1].append(folded[:, at : at + right.shape[1]])
+            at += right.shape[1]
+    return shares
 
 
 def fold_vector(vector):
@@ -170,15 +294,11 @@
         [query_weight, key_weight, value_weight, output_weight, gains], axis=1
     )
     attn_full = lax.all_gather(attn_mine, ("dp", "blk"), axis=0, tiled=True)
-    cuts = 2
-    chunk = -(-hidden_units // (cuts * LANES)) * LANES
-    spans = [(i * chunk, min(hidden_units, (i + 1) * chunk)) for i in range(cuts)]
-    ffn_mine = []
-    for start, stop in spans:
-        for weight in (gate_weight, up_weight, down_weight):
-            ffn_mine.append(
-                jnp.pad(weight[:, start:stop], ((0, 0), (0, chunk - (stop - start))))
-            )
+    padded = -(-hidden_units // (2 * LANES)) * (2 * LANES)
+    ffn_mine = [
+        jnp.pad(weight, ((0, 0), (0, padded - hidden_units)))
+        for weight in (gate_weight, up_weight, down_weight)
+    ]
     ffn_mine = jnp.concatenate(ffn_mine, axis=1)
     ffn_mine, attn_full = lax.optimization_barrier((ffn_mine, attn_full))
     ffn_full = lax.all_gather(ffn_mine, ("dp", "blk"), axis=0, tiled=True)
@@ -236,38 +356,26 @@
     attended = hidden_float + pair_sum(dot_rows(context_low, full_output))
     mid_low = rms_scale(attended, mid_gain).astype(jnp.bfloat16)
 
-    mid_fold = fold_columns(mid_low)
-    cot_fold = fold_columns(cotangent)
     cot_float = cotangent.astype(jnp.float32)
-    ffn_part, mid_part = 0.0, 0.0
-    ffn_shares = ([], [], [])
-    for number, (start, stop) in enumerate(spans):
-        own = ffn_full[:, 3 * chunk * number : 3 * chunk * (number + 1)]
-        span_gate, span_up, span_down = own[:, :chunk], own[:, chunk : 2 * chunk], own[:, 2 * chunk :]
-        gate = plain_dot(mid_low, span_gate)
-        upward = plain_dot(mid_low, span_up)
-        sigma = jax.nn.sigmoid(gate)
-        silu_gate = gate * sigma
-        act_low = (silu_gate * upward).astype(jnp.bfloat16)
-        act_grad = plain_dot(cotangent, span_down)
-        gate_grad_low = (act_grad * upward * sigma * (1.0 + gate * (1.0 - sigma))).astype(
-            jnp.bfloat16
-        )
-        up_grad_low = (act_grad * silu_gate).astype(jnp.bfloat16)
-        mid_part = mid_part + dot_rows(gate_grad_low, span_gate) + dot_rows(up_grad_low, span_up)
-        ffn_part = ffn_part + dot_rows(act_low, span_down)
-        size = stop - start
-        ffn_shares[0].append(fold_product(mid_fold, gate_grad_low[:, :size]))
-        ffn_shares[1].append(fold_product(mid_fold, up_grad_low[:, :size]))
-        ffn_shares[2].append(fold_product(cot_fold, act_low[:, :size]))
-    gate_share, up_share, down_share = (jnp.concatenate(parts, axis=1) for parts in ffn_shares)
+    full_gate = ffn_full[:, :padded]
+    full_up = ffn_full[:, padded : 2 * padded]
+    full_down = ffn_full[:, 2 * padded :]
+    gate = plain_dot(mid_low, full_gate)
+    upward = plain_dot(mid_low, full_up)
+    sigma = jax.nn.sigmoid(gate)
+    silu_gate = gate * sigma
+    act_low = (silu_gate * upward).astype(jnp.bfloat16)
+    act_grad = plain_dot(cotangent, full_down)
+    gate_grad_low = (act_grad * upward * sigma * (1.0 + gate * (1.0 - sigma))).astype(jnp.bfloat16)
+    up_grad_low = (act_grad * silu_gate).astype(jnp.bfloat16)
+    mid_part = dot_rows(gate_grad_low, full_gate) + dot_rows(up_grad_low, full_up)
+    ffn_part = dot_rows(act_low, full_down)
     mid_grad = pair_sum(mid_part)
     output = (attended + pair_sum(ffn_part)).astype(jnp.bfloat16)
     attended_norm_grad, mid_gain_grad = jax.vjp(rms_scale, attended, mid_gain)[1](mid_grad)
     attended_grad = cot_float + attended_norm_grad
 
     resid_low = attended_grad.astype(jnp.bfloat16)
-    output_share = fold_product(fold_columns(resid_low), context_low)
     context_grad_low = plain_dot(resid_low, full_output).astype(jnp.bfloat16)
     if spread:
         context_grad_all = to_heads([context_grad_low], blocks)[0]
@@ -311,10 +419,22 @@
     memory_in_grad = pair_sum(
         dot_rows(key_grad_low, full_key) + dot_rows(value_grad_low, full_value)
     )
-    normed_fold, memory_fold = fold_columns(normed_low), fold_columns(memory_low)
-    query_share = fold_product(normed_fold, query_grad_low)
-    key_share = fold_product(memory_fold, key_grad_low)
-    value_share = fold_product(memory_fold, value_grad_low)
+    shares = fold_products(
+        [
+            (mid_low, [gate_grad_low, up_grad_low]),
+            (cotangent, [act_low]),
+            (resid_low, [context_low]),
+            (normed_low, [query_grad_low]),
+            (memory_low, [key_grad_low, value_grad_low]),
+        ],
+        0,
+    )
+    gate_share, up_share = shares[0]
+    (down_share,), (output_share,), (query_share,) = shares[1:4]
+    key_share, value_share = shares[4]
+    gate_share, up_share, down_share = (
+        share[:, :hidden_units] for share in (gate_share, up_share, down_share)
+    )
     hidden_norm_grad, input_gain_grad = jax.vjp(rms_scale, hidden_float, input_gain)[1](normed_grad)
     memory_grad, source_gain_grad = jax.vjp(rms_scale, memory_float, source_gain)[1](memory_in_grad)
     hidden_grad = attended_grad + hidden_norm_grad

time: 1170 us -> 1080 us (0.923)
  Pallas kernels: 0 us -> 362 us
  waiting for transfers between devices: 614 us -> 342 us
  matrix products: 257 us -> 144 us
  starting transfers between devices: 80.1 us -> 28 us
  local copies, waits for them, and re-layouts: 134 us -> 89.2 us
  blocking collectives: 0 us -> 27.2 us
    pallas_call x0 -> x1, Pallas kernels: none -> 362 us  [fold_products(): pl.pallas_call(functools.partial(fold_kernel, steps, edges[:-1], tiles, w...]
    ppermute x49 -> x9, waiting for transfers between devices: 393 us -> 77.3 us  [swap(): return lax.ppermute(array, axis, [(i, i ^ bit) for i in range(size)])]
    dot_general x50 -> x0, matrix products: 114 us -> none  [dot_cols(): lax.dot_general(left, right, (((0,), (0,)), ((), ())), preferred_element_...]
    ppermute x49 -> x9, starting transfers between devices: 57.6 us -> 9.48 us  [swap(): return lax.ppermute(array, axis, [(i, i ^ bit) for i in range(size)])]
    all_to_all x2 -> x1, waiting for transfers between devices: 14.9 us -> 44.3 us  [to_blocks(): moved = lax.all_to_all(packed, 'blk', 0, 0)]
    all_to_all x0 -> x1, blocking collectives: none -> 27.2 us  [to_blocks(): moved = lax.all_to_all(packed, 'blk', 0, 0)]
    unnamed x359 -> x109, local copies, waits for them, and re-layouts: 81.9 us -> 59.4 us
    all_to_all x2, waiting for transfers between devices: 66.2 us -> 83.6 us  [to_heads(): moved = lax.all_to_all(packed, 'blk', 0, 0)]
  transfers between devices with their start and end apart: 55 -> 14, of which waited for: 30 -> 10; matrix products, arithmetic and copies ran while one was open for 30% -> 16% of each run, Pallas kernels for 0% -> 34%
where the time goes in v2:
time: 1080 us; the launch traced here: 1070 us
  Pallas kernels  362 us (34%)
  waiting for transfers between devices  342 us (32%)
  matrix products  144 us (13%)
  local copies, waits for them, and re-layouts  89.2 us (8%)
  other arithmetic  67 us (6%)
  starting transfers between devices  28 us (3%)
  blocking collectives  27.2 us (3%)
  between operations  15.5 us (1%)
    pallas_call x1, Pallas kernels, fold_products(): pl.pallas_call(functools.partial(fold_kernel, steps, edges[:-1], tiles, w...  362 us
    all_gather x1, waiting for transfers between devices, local(): attn_full = lax.all_gather(attn_mine, ('dp', 'blk'), axis=0, tiled=True)  88 us
    all_to_all x2, waiting for transfers between devices, to_heads(): moved = lax.all_to_all(packed, 'blk', 0, 0)  83.6 us
    ppermute x9, waiting for transfers between devices, swap(): return lax.ppermute(array, axis, [(i, i ^ bit) for i in range(size)])  77.3 us
    unnamed x109, local copies, waits for them, and re-layouts  59.4 us
    dot_general x7, matrix products, dot_rows(): lax.dot_general(left, right, (((1,), (1,)), ((), ())), preferred_element_...  50.1 us
    all_gather x1, waiting for transfers between devices, local(): ffn_full = lax.all_gather(ffn_mine, ('dp', 'blk'), axis=0, tiled=True)  48.4 us
    dot_general x7, matrix products, plain_dot(): return jnp.dot(left, right, preferred_element_type=jnp.float32)  45.1 us
  transfers between devices with their start and end apart: 14, of which 10 were waited for; matrix products, arithmetic and copies ran while one was open for 16% of the time, Pallas kernels for 34%

profile of v2, /device:TPU:0, one launch (start us, length us, event | category | flops | bytes accessed | tf_op | source)
XLA Modules:
  0.0 1074.8 jit_solution(9597674418863149395)
XLA Ops:
  13.2 11.0 %fusion.90 = bf16[128,8448]{0,1:T(8,128)(2,1)} fusion(bf16[128,2752]{0,1:T(8,128)(2,1)S(1)} %copy-done.19, bf16[128,2752]{0,1:T(8,128)(2,1)S(1)} %copy-done.20, bf16[128,2752]{0,1:T(8,128)(2,1)} %param.21), kind=kLoop, calls=%fused_computation.109 | loop fusion | flops 15138816 | bytes 4276224 | tf_op jit(solution)/shard_map/concatenate | solution.py:302
  24.2 88.0 %all-gather.3.cloned.1.call-done = bf16[2048,4224]{1,0:T(8,128)(2,1)} async-done(((bf16[128,4224]{1,0:T(8,128)(2,1)}), bf16[2048,4224]{1,0:T(8,128)(2,1)}) %all-gather.3.cloned.1.call-update) | async-done | bytes 17301520 | tf_op jit(solution)/shard_map/all_gather | solution.py:296
  113.2 2.6 copy.97
  119.8 4.4 fusion.97
  124.3 4.1 fusion.100
  128.5 4.1 fusion.94
  134.6 5.0 all-to-all-start
  139.9 3.5 fusion.19
  143.3 63.8 %all-to-all-done = bf16[4,384,768]{2,1,0:T(8,128)(2,1)} async-done(((bf16[4,384,768]{2,1,0:T(8,128)(2,1)}), bf16[4,384,768]{2,1,0:T(8,128)(2,1)}, u32[]{:S(2)}, u32[]{:S(2)}) %all-to-all-start) | async-done | bytes 2359328 | tf_op jit(solution)/shard_map/all_to_all | solution.py:250
  207.1 2.9 fusion.169
  210.0 2.3 copy.157
  214.6 6.0 select_reduce_fusion
  220.6 7.3 fusion.1
  228.0 8.9 fusion.173
  237.0 1.8 reshape.206
  239.5 27.2 %all_to_all.20 = bf16[4,384,256]{2,1,0:T(8,128)(2,1)S(1)} all-to-all(bf16[4,384,256]{2,1,0:T(8,128)(2,1)S(1)} %copy.150), channel_id=1, replica_groups=mesh['dp'=4,'blk'=4,'heads'=2] {'blk'}, dimensions={0} | all-to-all | bytes 1572864 | tf_op jit(solution)/shard_map/all_to_all | solution.py:259
  267.6 4.6 fusion.73
  273.8 32.9 %collective-permute-done = bf16[384,2048]{0,1:T(8,128)(2,1)S(1)} collective-permute-done((bf16[384,2048]{0,1:T(8,128)(2,1)S(1)}, bf16[384,2048]{0,1:T(8,128)(2,1)S(1)}, u32[]{:S(2)}, u32[]{:S(2)}) %collective-permute-start) | collective-permute-done | bytes 1572896 | tf_op jit(solution)/shard_map/ppermute | solution.py:44
  310.7 48.4 %all-gather.5.cloned.1.call-done = bf16[2048,8448]{0,1:T(8,128)(2,1)} async-done(((bf16[128,8448]{0,1:T(8,128)(2,1)}), bf16[2048,8448]{0,1:T(8,128)(2,1)}) %all-gather.5.cloned.1.call-update) | async-done | bytes 34603024 | tf_op jit(solution)/shard_map/all_gather | solution.py:304
  359.1 8.1 fusion.9
  367.2 8.1 fusion.22
  375.3 11.1 %constant_dynamic-update-slice_fusion.23 = (bf16[384,12544]{1,0:T(8,128)(2,1)}, bf16[384,2816]{1,0:T(8,128)(2,1)}, f32[384,2816]{1,0:T(8,128)S(1)}) fusion(f32[384,2816]{1,0:T(8,128)S(1)} %fusion.22, f32[384,2816]{1,0:T(8,128)S(1)} %fusion.9, bf16[384,2048]{0,1:T(8,128)(2,1)} %copy-done.18, bf16[2048,8448]{0,1:T(8,128)(2,1)} %all-gather.5.cloned.1.call-done), kind=kOutput, calls=%fused_computation.202 | convolution fusion | flops 4439998464 | bytes 30408704 | tf_op jit(solution)/shard_map/dot_general | solution.py:23
  386.4 2.6 constant_dynamic-update-slice_fusion.22
  389.0 2.6 constant_dynamic-update-slice_fusion.21
  391.6 9.9 fusion.67
  403.0 9.2 fusion.7
  412.2 10.2 add_convert_fusion.1
  423.0 1.9 copy.109
  426.2 13.0 %collective-permute-done.1 = bf16[384,2048]{0,1:T(8,128)(2,1)} collective-permute-done((bf16[384,2048]{0,1:T(8,128)(2,1)}, bf16[384,2048]{0,1:T(8,128)(2,1)}, u32[]{:S(2)}, u32[]{:S(2)}) %collective-permute-start.1) | collective-permute-done | bytes 1572896 | tf_op jit(solution)/shard_map/ppermute | solution.py:44
  439.2 28.4 %collective-permute-done.2 = bf16[384,2048]{0,1:T(8,128)(2,1)} collective-permute-done((bf16[384,2048]{0,1:T(8,128)(2,1)}, bf16[384,2048]{0,1:T(8,128)(2,1)}, u32[]{:S(2)}, u32[]{:S(2)}) %collective-permute-start.2) | collective-permute-done | bytes 1572896 | tf_op jit(solution)/shard_map/ppermute | solution.py:44
  467.6 4.5 multiply_reduce_fusion
  472.2 3.5 bitcast_dynamic-update-slice_fusion.2
  475.7 5.2 fusion.103
  482.0 8.5 all-to-all-start.2
  490.5 19.9 %all-to-all-done.2 = bf16[4,384,256]{2,1,0:T(8,128)(2,1)S(1)} async-done(((bf16[4,384,256]{2,1,0:T(8,128)(2,1)}), bf16[4,384,256]{2,1,0:T(8,128)(2,1)S(1)}, u32[]{:S(2)}, u32[]{:S(2)}) %all-to-all-start.2) | async-done | bytes 786464 | tf_op jit(solution)/shard_map/all_to_all | solution.py:250
  511.2 1.9 multiply_reduce_fusion.3
  513.1 14.8 %multiply_convert_fusion = bf16[2,1536,1536]{1,2,0:T(8,128)(2,1)} fusion(bf16[1536,2,128]{0,2,1:T(8,128)(2,1)S(1)} %copy.141, bf16[1536,2,128]{0,2,1:T(8,128)(2,1)} %bitcast.227, f32[2,1536,1536]{1,2,0:T(8,128)} %copy-done.5, f32[2,1536]{1,0:T(2,128)S(1)} %bitcast.232, f32[2,1536]{1,0:T(2,128)S(1)} %log_add_fusion, pred[1536,1536]{0,1:T(8,128)(4,1)} %fusion.19), kind=kOutput, calls=%fused_computation | convolution fusion | flops 1236271104 | bytes 32268288 | tf_op jit(solution)/shard_map/qhd,khd->hqk/dot_general | solution.py:388
  528.0 5.2 fusion.85
  534.5 4.0 fusion.84
  538.5 10.0 fusion.86
  549.4 2.4 reshape.209
  553.4 2.4 reshape.210
  555.8 2.2 copy.156
  558.0 2.7 pad_maximum_fusion.1
  560.7 4.9 all-to-all-start.3
  568.8 2.7 copy.127
  574.6 44.3 %all-to-all-done.3 = bf16[4,384,768]{2,1,0:T(8,128)(2,1)} async-done(((bf16[4,384,768]{2,1,0:T(8,128)(2,1)}), bf16[4,384,768]{2,1,0:T(8,128)(2,1)}, u32[]{:S(2)}, u32[]{:S(2)}) %all-to-all-start.3) | async-done | bytes 2359328 | tf_op jit(solution)/shard_map/all_to_all | solution.py:259
  618.9 1.9 slice_bitcast_fusion.7
  620.8 4.6 fusion.38
  625.4 5.8 add_convert_fusion
  632.8 5.7 fusion.70
  658.8 361.9 %shard_map.237 = f32[128,12544]{1,0:T(8,128)} custom-call(bf16[5,2048,384]{2,1,0:T(8,128)(2,1)} %bitcast_dynamic-update-slice_fusion.left_ref, bf16[384,12544]{1,0:T(8,128)(2,1)} %constant_dynamic-update-slice_fusion.5.right_ref), custom_call_target="tpu_custom_call" | custom-call | flops 19730006016 | bytes 205520896 | tf_op jit(solution)/shard_map/pallas_call | solution.py:195
  1020.7 4.4 fusion.167
  1025.1 2.9 copy.130
  1027.9 2.9 copy.131
  1030.8 2.9 copy.132
  1033.7 2.9 fusion.168
  1036.6 3.3 fusion.53
  1040.0 3.5 fusion.51
  1045.8 4.6 fusion.55
  1052.2 1.9 collective-permute-done.7
  1055.3 4.5 add_add_fusion
  1059.8 3.5 copy.129
  1063.4 3.5 copy.128
  (164 shorter events, 65.2 us)
Async XLA Ops:
  7.2 6.0 copy-start.20
  7.2 6.0 copy-start.19
  7.2 105.1 %all-gather.3.cloned.1.call-start = ((), (), s32[]{:S(2)}) async-start(), calls=%async_computation.4 | async-start | bytes 18382848 | tf_op jit(solution)/shard_map/all_gather | solution.py:296
  12.1 1.0 copy-start.15
  13.1 99.2 %copy-start.16 = (bf16[384,2048]{1,0:T(8,128)(2,1)S(1)}, bf16[384,2048]{1,0:T(8,128)(2,1)}, u32[]{:S(2)}) copy-start(bf16[384,2048]{1,0:T(8,128)(2,1)} %param.15) | copy-start | bytes 4718596
  13.1 346.0 %all-gather.5.cloned.1.call-start = ((), (), s32[]{:S(2)}) async-start(), calls=%async_computation.5 | async-start | bytes 36765696 | tf_op jit(solution)/shard_map/all_gather | solution.py:304
  113.2 11.1 %copy-start.3 = (bf16[384,2048]{0,1:T(8,128)(2,1)}, bf16[384,2048]{0,1:T(8,128)(2,1)S(1)}, u32[]{:S(2)}) copy-start(bf16[384,2048]{0,1:T(8,128)(2,1)S(1)} %copy.99) | copy-start | bytes 4718596
  116.2 0.6 copy-start.29
  116.6 0.6 copy-start.31
  116.6 7.6 copy-start.27
  117.2 11.3 %copy-start.25 = (f32[384]{0:T(512)}, f32[384]{0:T(512)S(1)}, u32[]{:S(2)}) copy-start(f32[384]{0:T(512)S(1)} %fusion.152) | copy-start | bytes 4612
  119.8 4.5 copy-start.21
  119.8 8.7 copy-start.23
  134.6 5.0 copy-start.33
  134.6 72.5 %all-to-all-start = ((bf16[4,384,768]{2,1,0:T(8,128)(2,1)}), bf16[4,384,768]{2,1,0:T(8,128)(2,1)}, u32[]{:S(2)}, u32[]{:S(2)}) async-start(bf16[4,384,768]{2,1,0:T(8,128)(2,1)} %pad_maximum_fusion), calls=%async_computation | async-start | bytes 4718592 | tf_op jit(solution)/shard_map/all_to_all | solution.py:250
  220.6 7.4 copy-start.5
  266.6 0.9 copy-start.10
  272.2 34.4 %collective-permute-start = (bf16[384,2048]{0,1:T(8,128)(2,1)S(1)}, bf16[384,2048]{0,1:T(8,128)(2,1)S(1)}, u32[]{:S(2)}, u32[]{:S(2)}) collective-permute-start(bf16[384,2048]{0,1:T(8,128)(2,1)S(1)} %fusion.73), channel_id=1, source_target_pairs={{0,1},{1,0},{2,3},{3,2},{4,5},{5,4},{6,7},{7,6},{8,9},{9,8},{10,11... | collective-permute-start | bytes 4718600 | tf_op jit(solution)/shard_map/ppermute | solution.py:44
  307.5 1.7 copy-start.1
  310.7 48.4 %copy-start.18 = (bf16[384,2048]{0,1:T(8,128)(2,1)}, bf16[384,2048]{0,1:T(8,128)(2,1)S(1)}, u32[]{:S(2)}) copy-start(bf16[384,2048]{0,1:T(8,128)(2,1)S(1)} %get-tuple-element.74) | copy-start | bytes 4718596
  359.1 8.1 copy-start.17
  401.5 37.7 %collective-permute-start.1 = (bf16[384,2048]{0,1:T(8,128)(2,1)}, bf16[384,2048]{0,1:T(8,128)(2,1)}, u32[]{:S(2)}, u32[]{:S(2)}) collective-permute-start(bf16[384,2048]{0,1:T(8,128)(2,1)} %fusion.67), channel_id=1, source_target_pairs={{0,1},{1,0},{2,3},{3,2},{4,5},{5,4},{6,7},{7,6},{8,9},{9,8},{10,11... | collective-permute-start | bytes 4718600 | tf_op jit(solution)/shard_map/ppermute | solution.py:44
  403.0 9.2 copy-start.34
  422.5 45.1 %collective-permute-start.2 = (bf16[384,2048]{0,1:T(8,128)(2,1)}, bf16[384,2048]{0,1:T(8,128)(2,1)}, u32[]{:S(2)}, u32[]{:S(2)}) collective-permute-start(bf16[384,2048]{0,1:T(8,128)(2,1)} %add_convert_fusion.1), channel_id=1, source_target_pairs={{0,1},{1,0},{2,3},{3,2},{4,5},{5,4},{6,7},{7,6},{8,9},{9,8},{10,11... | collective-permute-start | bytes 4718600 | tf_op jit(solution)/shard_map/ppermute | solution.py:44
  424.9 42.7 %copy-start.2 = (f32[384,2048]{0,1:T(8,128)S(1)}, f32[384,2048]{0,1:T(8,128)}, u32[]{:S(2)}) copy-start(f32[384,2048]{0,1:T(8,128)} %copy-done.1) | copy-start | bytes 9437188
  475.7 5.2 copy-start.7
  482.0 28.4 %all-to-all-start.2 = ((bf16[4,384,256]{2,1,0:T(8,128)(2,1)}), bf16[4,384,256]{2,1,0:T(8,128)(2,1)S(1)}, u32[]{:S(2)}, u32[]{:S(2)}) async-start(bf16[4,384,256]{2,1,0:T(8,128)(2,1)} %pad_maximum_fusion.2), calls=%async_computation.2 | async-start | bytes 1572864 | tf_op jit(solution)/shard_map/all_to_all | solution.py:250
  511.2 1.9 copy-start.12
  513.1 14.9 %copy-start.6 = (bf16[1536,256]{0,1:T(8,128)(2,1)S(1)}, bf16[1536,256]{0,1:T(8,128)(2,1)}, u32[]{:S(2)}) copy-start(bf16[1536,256]{0,1:T(8,128)(2,1)} %copy.158) | copy-start | bytes 2359300
  528.0 6.4 copy-start
  528.0 6.5 copy-start.14
  534.5 4.0 copy-start.9
  534.5 4.0 copy-start.13
  560.7 5.1 copy-start.11
  560.7 58.2 %all-to-all-start.3 = ((bf16[4,384,768]{2,1,0:T(8,128)(2,1)}), bf16[4,384,768]{2,1,0:T(8,128)(2,1)}, u32[]{:S(2)}, u32[]{:S(2)}) async-start(bf16[4,384,768]{2,1,0:T(8,128)(2,1)} %pad_maximum_fusion.1), calls=%async_computation.3 | async-start | bytes 4718592 | tf_op jit(solution)/shard_map/all_to_all | solution.py:259
  565.5 5.9 copy-start.24
  565.6 5.9 copy-start.26
  568.8 4.3 copy-start.4
  568.8 4.3 copy-start.22
  568.8 4.3 copy-start.28
  631.3 405.3 %collective-permute-start.4 = (bf16[384,2048]{0,1:T(8,128)(2,1)}, bf16[384,2048]{0,1:T(8,128)(2,1)}, u32[]{:S(2)}, u32[]{:S(2)}) collective-permute-start(bf16[384,2048]{0,1:T(8,128)(2,1)} %add_convert_fusion), channel_id=1, source_target_pairs={{0,1},{1,0},{2,3},{3,2},{4,5},{5,4},{6,7},{7,6},{8,9},{9,8},{10,11... | collective-permute-start | bytes 4718600 | tf_op jit(solution)/shard_map/ppermute | solution.py:44
  638.5 401.5 %collective-permute-start.3 = (bf16[384,2048]{0,1:T(8,128)(2,1)}, bf16[384,2048]{0,1:T(8,128)(2,1)}, u32[]{:S(2)}, u32[]{:S(2)}) collective-permute-start(bf16[384,2048]{0,1:T(8,128)(2,1)} %fusion.70), channel_id=1, source_target_pairs={{0,1},{1,0},{2,3},{3,2},{4,5},{5,4},{6,7},{7,6},{8,9},{9,8},{10,11... | collective-permute-start | bytes 4718600 | tf_op jit(solution)/shard_map/ppermute | solution.py:44
  1040.0 3.8 copy-start.32
  1040.0 5.9 copy-start.8
  1043.7 1.2 collective-permute-start.5
  1044.9 7.3 copy-start.30
  1044.9 5.5 collective-permute-start.6
  1050.5 3.7 collective-permute-start.7
  1054.2 12.7 %collective-permute-start.8 = (f32[1,3,128]{2,1,0:T(4,128)S(1)}, f32[1,3,128]{2,1,0:T(4,128)S(1)}, u32[]{:S(2)}, u32[]{:S(2)}) collective-permute-start(f32[1,3,128]{2,1,0:T(4,128)S(1)} %slice.307), channel_id=1, source_target_pairs={{0,4},{2,6},{4,0},{6,2},{1,5},{3,7},{5,1},{7,3},{8,12},{10,14},{12... | collective-permute-start | bytes 4616 | tf_op jit(solution)/shard_map/ppermute | solution.py:44
Sparse Core Ops, SparseCore 0:
  13.2 98.9 all-gather.2
  113.7 245.3 all-gather.4

commit v3 on v2

v3 whole, which is shorter than its diff:
```python
import functools
import math

import jax
import jax.numpy as jnp
from jax import lax
from jax.experimental import pallas as pl
from jax.experimental.pallas import tpu as pltpu
from jax.sharding import PartitionSpec as P

MESH = pl.DeviceIdType.MESH
HEAD = 128
LANES = 128
MARKS = (7, 13)
STRIPS = 16
LAST_MARKS = (8, 15)
MESH_AXES = ("dp", "blk", "heads")
EPSILON = 1e-06
NEGATIVE = -1e30


def rms_scale(values, gain):
    return values * lax.rsqrt(jnp.mean(values * values, axis=-1, keepdims=True) + EPSILON) * gain


def plain_dot(left, right):
    return jnp.dot(left, right, preferred_element_type=jnp.float32)


def dot_rows(left, right):
    return lax.dot_general(
        left, right, (((1,), (1,)), ((), ())), preferred_element_type=jnp.float32
    )


def dot_cols(left, right):
    return lax.dot_general(
        left, right, (((0,), (0,)), ((), ())), preferred_element_type=jnp.float32
    )


def swap(array, axis, bit):
    size = lax.axis_size(axis)
    return lax.ppermute(array, axis, [(i, i ^ bit) for i in range(size)])


def heads_other(low):
    if lax.axis_size("heads") == 2:
        return swap(low, "heads", 1)
    return (lax.psum(low.astype(jnp.float32), "heads") - low.astype(jnp.float32)).astype(low.dtype)


def pair_add(low, other):
    return low.astype(jnp.float32) + other.astype(jnp.float32)


def pair_sum(part):
    low = part.astype(jnp.bfloat16)
    return pair_add(low, heads_other(low))


def fold_steps():
    steps = []
    for axis in ("dp", "blk"):
        size, bit = lax.axis_size(axis), 1
        while bit < size:
            steps.append((axis, bit))
            bit *= 2
    return steps


def late_steps(steps):
    first = [step for step in steps if step[0] == "dp"][1:]
    return [step for step in steps if step not in first] + first


def fold_order(width, steps):
    shards = 2 ** len(steps)
    part = width // shards
    offsets = []
    for place in range(shards):
        at = {axis: lax.axis_index(axis) for axis in ("dp", "blk")}
        for number, (axis, bit) in enumerate(steps):
            if place >> (len(steps) - 1 - number) & 1:
                at[axis] = flipped(at[axis], bit)
        offsets.append((at["dp"] * lax.axis_size("blk") + at["blk"]) * part)
    return offsets, part


def flipped(index, bit):
    return index + bit * (1 - 2 * ((index // bit) % 2))


def fold_engine(plans, edges, tiles, width, slots, period, lags, left_refs, right_ref, out_ref, scratch):
    count = len(plans[0])
    held, load_sem, send_sem, recv_sem, credit = scratch[:5]
    sent, got = scratch[5 : 5 + count], scratch[5 + count : 5 + 2 * count]
    lefts, features = held.shape[1:3]
    here = [lax.axis_index(axis) for axis in MESH_AXES]
    partners = [
        [
            tuple(
                flipped(place, bit) if name == axis else place
                for name, place in zip(MESH_AXES, here)
            )
            for axis, bit in steps
        ]
        for steps in plans
    ]
    loads = []
    for plan, steps in enumerate(plans):
        offsets, part = fold_order(features, steps)
        for number in range(lefts):
            for place, offset in enumerate(offsets):
                loads.append(
                    pltpu.make_async_copy(
                        left_refs[number].at[pl.ds(pl.multiple_of(offset, part), part)],
                        held.at[plan, number, pl.ds(place * part, part)],
                        load_sem.at[plan, number, place],
                    )
                )

    def plan_of(tile):
        return jnp.where(lax.rem(tile, period) == period - 1, 1, 0) if len(plans) > 1 else 0

    def partner_of(step, plan):
        if len(plans) == 1:
            return partners[0][step]
        return tuple(
            usual + plan * (other - usual)
            for usual, other in zip(partners[0][step], partners[1][step])
        )

    def transfer(step, tile):
        return pltpu.make_async_remote_copy(
            src_ref=sent[step].at[lax.rem(tile, 2)],
            dst_ref=got[step].at[lax.rem(tile, slots)],
            send_sem=send_sem.at[step, lax.rem(tile, 2)],
            recv_sem=recv_sem.at[step, lax.rem(tile, slots)],
            device_id=partner_of(step, plan_of(tile)),
            device_id_type=MESH,
        )

    def stage(number, tile):
        slot = lax.rem(tile, slots)
        plan = plan_of(tile)
        if number > 0:
            transfer(number - 1, tile).wait_recv()
        last = number == count
        low = 0 if last else features >> (number + 1)
        high = features >> number
        group = jnp.int32(0)
        for edge in edges:
            group = group + (tile >= edge).astype(jnp.int32)
        columns = pl.ds(pl.multiple_of(tile * width, width), width)
        total = jnp.dot(
            held[plan, group, low:high], right_ref[:, columns], preferred_element_type=jnp.float32
        )
        for earlier in range(number):
            total = total + got[earlier][slot, low:high].astype(jnp.float32)
        if last:
            out_ref[:, columns] = total

            @pl.when(tile < tiles - slots)
            def _():
                for step in range(count):
                    pl.semaphore_signal(
                        credit.at[plan, step],
                        inc=1,
                        device_id=partner_of(step, plan),
                        device_id_type=MESH,
                    )

            return

        @pl.when(tile >= 2)
        def _():
            transfer(number, tile - 2).wait_send()

        sent[number][lax.rem(tile, 2)] = total.astype(jnp.bfloat16)

        @pl.when(tile >= slots)
        def _():
            pl.semaphore_wait(credit.at[plan, number], 1)

        transfer(number, tile).start()

    def turn(index):
        for number in range(count + 1):
            tile = index - lags[number]

            @pl.when((tile >= 0) & (tile < tiles))
            def _(number=number, tile=tile):
                stage(number, tile)

    def finish():
        for step in range(count):
            for tile in range(max(0, tiles - 2), tiles):
                transfer(step, jnp.int32(tile)).wait_send()

    return loads, turn, finish, partners[0]


def greet(partners):
    barrier = pltpu.get_barrier_semaphore()
    for partner in partners:
        pl.semaphore_signal(barrier, inc=1, device_id=partner, device_id_type=MESH)
    pl.semaphore_wait(barrier, len(partners))


def fold_kernel(fold, lefts, *refs):
    left_refs, right_ref, out_ref, scratch = refs[:lefts], refs[lefts], refs[lefts + 1], refs[lefts + 2 :]
    loads, turn, finish, partners = fold_engine(*fold, left_refs, right_ref, out_ref, scratch)
    for load in loads:
        load.start()
    greet(partners)
    for load in loads:
        load.wait()

    def body(index, carry):
        turn(index)
        return carry

    lax.fori_loop(0, fold[2] + fold[6][-1], body, 0)
    finish()


def fold_lags(count):
    return (0,) + tuple(range(1, 2 * count, 2))


def fold_scratch(plans, lefts, features, rows, width, slots):
    count = len(plans[0])
    sizes = [features >> (step + 1) for step in range(count)]
    return [
        pltpu.VMEM((len(plans), lefts, features, rows), jnp.bfloat16),
        pltpu.SemaphoreType.DMA((len(plans), lefts, 1 << count)),
        pltpu.SemaphoreType.DMA((count, 2)),
        pltpu.SemaphoreType.DMA((count, slots)),
        pltpu.SemaphoreType.REGULAR((len(plans), count)),
        *[pltpu.VMEM((2, size, width), jnp.bfloat16) for size in sizes],
        *[pltpu.VMEM((slots, size, width), jnp.bfloat16) for size in sizes],
    ]


def fold_setting(groups, width, slots, period):
    steps = fold_steps()
    plans = [steps]
    if lax.axis_size("dp") > 2 and period and slots % period == 0:
        plans.append(late_steps(steps))
    edges, tiles = [], 0
    for _, many in groups:
        tiles += sum(right.shape[1] for right in many) // width
        edges.append(tiles)
    lefts = [left for left, _ in groups]
    rights = [right for _, many in groups for right in many]
    rights = rights[0] if len(rights) == 1 else jnp.concatenate(rights, axis=1)
    fold = (plans, edges[:-1], tiles, width, slots, period, fold_lags(len(steps)))
    features, rows = lefts[0].shape
    shape = jax.ShapeDtypeStruct((features >> len(steps), tiles * width), jnp.float32)
    scratch = fold_scratch(plans, len(lefts), features, rows, width, slots)
    cost = pl.CostEstimate(
        flops=2 * features * rows * tiles * width,
        bytes_accessed=tiles * width * features * 8,
        transcendentals=0,
    )
    return fold, lefts, rights, shape, scratch, cost


def remote_params(call):
    return pltpu.CompilerParams(
        collective_id=call, has_side_effects=True, vmem_limit_bytes=63 * 1024 * 1024
    )


def fold_products(groups, call, width=256, slots=12, period=6):
    fold, lefts, rights, shape, scratch, cost = fold_setting(groups, width, slots, period)
    folded = pl.pallas_call(
        functools.partial(fold_kernel, fold, len(lefts)),
        out_shape=shape,
        in_specs=[pl.BlockSpec(memory_space=pl.ANY)] * len(lefts)
        + [pl.BlockSpec(memory_space=pltpu.VMEM)],
        out_specs=pl.BlockSpec(memory_space=pltpu.VMEM),
        scratch_shapes=scratch,
        compiler_params=remote_params(call),
        cost_estimate=cost,
    )(*lefts, rights)
    return unstacked(groups, folded)


def unstacked(groups, folded):
    shares, at = [], 0
    for _, many in groups:
        shares.append([])
        for right in many:
            shares[-1].append(folded[:, at : at + right.shape[1]])
            at += right.shape[1]
    return shares


def together(*arrays):
    return lax.optimization_barrier(arrays)


def fold_vector(vector):
    steps = fold_steps()
    offsets, part = fold_order(vector.shape[-1], steps)
    held = jnp.stack(
        [lax.dynamic_slice_in_dim(vector, offset, part, axis=-1) for offset in offsets], axis=0
    )
    for axis, bit in steps:
        half = held.shape[0] // 2
        held = held[:half] + swap(held[half:], axis, bit)
    return held[0]


def to_heads(pieces, blocks):
    rows, width = pieces[0].shape
    part = width // blocks
    packed = jnp.stack(
        [
            jnp.concatenate([piece[:, i * part : (i + 1) * part] for piece in pieces], axis=1)
            for i in range(blocks)
        ],
        axis=0,
    )
    moved = lax.all_to_all(packed, "blk", 0, 0)
    return moved.reshape(rows * blocks, part * len(pieces))


def swap_blocks(packed, blocks):
    length, columns = packed.shape
    return lax.all_to_all(packed.reshape(blocks, length // blocks, columns), "blk", 0, 0)


def side_by_side(moved, count):
    part = moved.shape[2] // count
    return [
        jnp.concatenate(
            [moved[j, :, i * part : (i + 1) * part] for j in range(moved.shape[0])], axis=1
        )
        for i in range(count)
    ]


def first_allowed(doc_ends, positions):
    first = jnp.zeros(positions.shape, jnp.int32)
    for number in range(doc_ends.shape[0]):
        end = doc_ends[number]
        first = jnp.maximum(first, jnp.where(end <= positions, end, 0))
    return first


def tile_probs(ends, packed, part, head, start, stop, factor):
    own = slice(head * HEAD, (head + 1) * HEAD)
    keys = packed[:stop, part + own.start : part + own.stop]
    scores = dot_rows(packed[start:stop, own], keys) * factor
    positions = start + lax.broadcasted_iota(jnp.int32, (stop - start, 1), 0)
    first = first_allowed(ends, positions)
    key_pos = lax.broadcasted_iota(jnp.int32, scores.shape, 1)
    allowed = (key_pos >= first) & (key_pos <= positions)
    scores = jnp.where(allowed, scores, NEGATIVE)
    weights = jnp.exp(scores - jnp.max(scores, axis=-1, keepdims=True))
    return weights / jnp.sum(weights, axis=-1, keepdims=True)


def attend_kernel(part, tile, factor, ends, packed, out):
    for head in range(part // HEAD):
        own = slice(head * HEAD, (head + 1) * HEAD)
        for start in range(0, packed.shape[0], tile):
            stop = start + tile
            probs = tile_probs(ends, packed, part, head, start, stop, factor)
            values = packed[:stop, 2 * part + own.start : 2 * part + own.stop]
            out[start:stop, own] = plain_dot(probs.astype(jnp.bfloat16), values).astype(out.dtype)


def attend_back_head(part, tile, factor, head, ends, packed, grads, out, key_sum, value_sum):
    length = packed.shape[0]
    own = slice(head * HEAD, (head + 1) * HEAD)
    key_own = slice(part + own.start, part + own.stop)
    value_own = slice(2 * part + own.start, 2 * part + own.stop)
    for start in reversed(range(0, length, tile)):
        stop = start + tile
        probs = tile_probs(ends, packed, part, head, start, stop, factor)
        grad = grads[start:stop, own]
        prob_grad = dot_rows(grad, packed[:stop, value_own])
        delta = jnp.sum(probs * prob_grad, axis=-1, keepdims=True)
        score_grad = (probs * (prob_grad - delta)).astype(jnp.bfloat16)
        query_grad = plain_dot(score_grad, packed[:stop, key_own]) * factor
        out[start:stop, own] = query_grad.astype(out.dtype)
        key_part = dot_cols(score_grad, packed[start:stop, own])
        value_part = dot_cols(probs.astype(jnp.bfloat16), grad)
        if stop == length:
            key_sum[:stop] = key_part
            value_sum[:stop] = value_part
        else:
            key_sum[:stop] += key_part
            value_sum[:stop] += value_part
    out[:, key_own] = (key_sum[...] * factor).astype(out.dtype)
    out[:, value_own] = value_sum[...].astype(out.dtype)


def attention_tile(length):
    return next(tile for tile in (512, 384, 256, 128, 64, 32, 16) if length % tile == 0)


def attention_call(kernel, doc_ends, arrays, columns, scratch, matmuls):
    length, width = arrays[0].shape
    part = width // 3
    tile = attention_tile(length)
    vmem = pl.BlockSpec(memory_space=pltpu.VMEM)
    return pl.pallas_call(
        functools.partial(kernel, part, tile, 1.0 / math.sqrt(HEAD)),
        out_shape=jax.ShapeDtypeStruct((length, columns), jnp.bfloat16),
        in_specs=[pl.BlockSpec(memory_space=pltpu.SMEM)] + [vmem] * len(arrays),
        out_specs=vmem,
        scratch_shapes=scratch,
        compiler_params=pltpu.CompilerParams(vmem_limit_bytes=48 * 1024 * 1024),
        cost_estimate=pl.CostEstimate(
            flops=2 * matmuls * length * length * part,
            bytes_accessed=10 * length * width,
            transcendentals=length * length * part // HEAD,
        ),
    )(doc_ends, *arrays)


def attend(doc_ends, packed):
    return attention_call(attend_kernel, doc_ends, [packed], packed.shape[1] // 3, [], 2)


def middle_kernel(
    fold, marks, tile, factor, ends, first_left, second_left, right_ref, mid_ref, attended_ref, cot_ref,
    gain_ref, weight_ref, packed_ref, down_ref, out_ref, resid_ref, gain_out, moved, result, *scratch
):
    count = len(fold[0][0])
    attended, cot, weight, packed, load_sem = scratch[:5]
    other, sent_grads, grads, out, key_sum, value_sum = scratch[5:11]
    heads_sem, ctx_sem, out_sem, down, down_sem, ready = scratch[11:17]
    left_refs = (first_left, second_left)
    loads, turn, finish, partners = fold_engine(*fold, left_refs, right_ref, out_ref, scratch[17:])
    rows, features = mid_ref.shape
    blocks, _, part = sent_grads.shape
    dp, blk, heads = (lax.axis_index(axis) for axis in MESH_AXES)

    def away(distance):
        at, bit = blk, 1
        while bit <= distance:
            if distance & bit:
                at = flipped(at, bit)
            bit *= 2
        return at

    mirror = (dp, blk, flipped(heads, 1))
    met = partners + [mirror]
    met += [(dp, away(d), heads) for d in range(1, blocks) if d & (d - 1)]
    loads = loads + [
        pltpu.make_async_copy(source, target, load_sem.at[number])
        for number, (source, target) in enumerate(
            [(attended_ref, attended), (cot_ref, cot), (weight_ref, weight), (packed_ref, packed)]
        )
    ]
    for load in loads:
        load.start()
    greet(met)
    mirrored = pltpu.make_async_remote_copy(
        src_ref=mid_ref,
        dst_ref=other,
        send_sem=heads_sem.at[0],
        recv_sem=heads_sem.at[1],
        device_id=mirror,
        device_id_type=MESH,
    )
    mirrored.start()
    for load in loads:
        load.wait()

    def block(index):
        return pl.ds(pl.multiple_of(index * rows, rows), rows)

    def ctx_copy(distance, landing):
        return pltpu.make_async_remote_copy(
            src_ref=sent_grads.at[away(distance)],
            dst_ref=grads.at[block(landing)],
            send_sem=ctx_sem.at[0, distance],
            recv_sem=ctx_sem.at[1, distance],
            device_id=(dp, away(distance), heads),
            device_id_type=MESH,
        )

    def landing_of(kind, source):
        offset = kind * (part * blocks) + source * part
        return moved.at[:, pl.ds(pl.multiple_of(offset, part), part)]

    def out_copy(kind, distance, landing):
        return pltpu.make_async_remote_copy(
            src_ref=out.at[block(away(distance)), pl.ds(kind * part, part)],
            dst_ref=landing_of(kind, landing),
            send_sem=out_sem.at[0, kind, distance],
            recv_sem=out_sem.at[1, kind, distance],
            device_id=(dp, away(distance), heads),
            device_id_type=MESH,
        )

    step = rows // 3 if rows % 48 == 0 else rows
    starts = list(range(0, rows, step))

    def norm_back(start):
        if start == 0:
            mirrored.wait()
        for start in (start,):
            own = slice(start, start + step)
            values = attended[own]
            mid_grad = pair_add(mid_ref[own], other[own])
            scale = lax.rsqrt(jnp.mean(values * values, axis=-1, keepdims=True) + EPSILON)
            normed = values * scale
            scaled = mid_grad * gain_ref[...]
            inner = jnp.mean(scaled * normed, axis=-1, keepdims=True)
            total = cot[own].astype(jnp.float32) + scale * (scaled - normed * inner)
            resid_ref[own] = total
            gain_part = jnp.sum(mid_grad * normed, axis=0, keepdims=True)
            if start == 0:
                gain_out[...] = gain_part
            else:
                gain_out[...] += gain_part
            low = plain_dot(total.astype(jnp.bfloat16), weight[...]).astype(jnp.bfloat16)
            for number in range(blocks):
                sent_grads[number, own] = low[:, number * part : (number + 1) * part]
        if start != starts[-1]:
            return
        grads[block(blk)] = sent_grads[blk]
        for distance in range(1, blocks):
            ctx_copy(distance, blk).start()

    strip = down.shape[1]
    strips = features // strip
    units = down.shape[2]
    down_at, act_at = down_ref.shape[1] - units, right_ref.shape[1] - units
    second = pltpu.make_async_remote_copy(
        src_ref=cot,
        dst_ref=other,
        send_sem=heads_sem.at[2],
        recv_sem=heads_sem.at[3],
        device_id=mirror,
        device_id_type=MESH,
    )

    def strip_copy(number):
        slot = lax.rem(number, 2)
        return pltpu.make_async_copy(
            down_ref.at[pl.ds(pl.multiple_of(number * strip, strip), strip), pl.ds(down_at, units)],
            down.at[slot],
            down_sem.at[slot],
        )

    def strip_step(number):
        strip_copy(number).wait()

        @pl.when(number + 1 < strips)
        def _():
            strip_copy(number + 1).start()

        columns = pl.ds(pl.multiple_of(number * strip, strip), strip)
        product = dot_rows(right_ref[:, act_at:], down[lax.rem(number, 2)])
        cot[:, columns] = product.astype(jnp.bfloat16)

    def one_head(head):
        attend_back_head(part, tile, factor, head, ends, packed, grads, out, key_sum, value_sum)

    def body(index, carry):
        turn(index)

        for number, start in enumerate(starts):

            @pl.when(index == marks[0] + number)
            def _(start=start):
                norm_back(start)

        done = marks[0] + len(starts) - 1

        @pl.when(index == done)
        def _():
            pl.semaphore_signal(ready, inc=1, device_id=mirror, device_id_type=MESH)
            strip_copy(jnp.int32(0)).start()

        @pl.when((index > done) & (index <= done + strips))
        def _():
            strip_step(index - done - 1)

        @pl.when(index == done + strips)
        def _():
            pl.semaphore_wait(ready, 1)
            second.start()

        @pl.when(index == marks[1])
        def _():
            for distance in range(1, blocks):
                ctx_copy(distance, away(distance)).wait_recv()
                ctx_copy(distance, blk).wait_send()

        for head in range(part // HEAD):

            @pl.when(index == marks[1] + head)
            def _(head=head):
                one_head(head)

        @pl.when(index == marks[1] + part // HEAD - 1)
        def _():
            for kind in range(3):
                offset = pl.multiple_of(kind * (part * blocks) + blk * part, part)
                moved[:, pl.ds(offset, part)] = out[block(blk), kind * part : (kind + 1) * part]

        for number in range(3 * (blocks - 1)):

            @pl.when(index == marks[1] + part // HEAD + 2 * number)
            def _(kind=number // (blocks - 1), distance=number % (blocks - 1) + 1):
                out_copy(kind, distance, blk).start()

        return carry

    lax.fori_loop(0, fold[2] + fold[6][-1], body, 0)
    finish()
    second.wait()
    for start in starts:
        own = slice(start, start + step)
        result[own] = (attended[own] + pair_add(cot[own], other[own])).astype(result.dtype)
    for kind in range(3):
        for distance in range(1, blocks):
            out_copy(kind, distance, away(distance)).wait_recv()
            out_copy(kind, distance, blk).wait_send()


def middle(
    groups, doc_ends, mid, attended, cot, gain, weight, packed, down, call, marks, width=256, slots=10
):
    fold, lefts, rights, shape, scratch, cost = fold_setting(groups, width, slots, 0)
    blocks = lax.axis_size("blk")
    rows, features = mid.shape
    length, columns = packed.shape
    part = columns // 3
    tile = 256 if length % 256 == 0 else attention_tile(length)
    turns = fold[2] + fold[6][-1]
    assert marks[0] + 3 + STRIPS < turns and marks[0] + 3 < marks[1]
    assert marks[1] + part // HEAD + 2 * 3 * (blocks - 1) < turns
    vmem, anywhere = (pl.BlockSpec(memory_space=space) for space in (pltpu.VMEM, pl.ANY))
    low = jnp.bfloat16
    folded, resid, gain_grad, moved, result = pl.pallas_call(
        functools.partial(middle_kernel, fold, marks, tile, 1.0 / math.sqrt(HEAD)),
        out_shape=(
            shape,
            jax.ShapeDtypeStruct(attended.shape, jnp.float32),
            jax.ShapeDtypeStruct((1, features), jnp.float32),
            jax.ShapeDtypeStruct((rows, columns * blocks), low),
            jax.ShapeDtypeStruct((rows, features), low),
        ),
        in_specs=[
            pl.BlockSpec(memory_space=pltpu.SMEM),
            anywhere,
            anywhere,
            vmem,
            vmem,
            anywhere,
            anywhere,
            vmem,
            anywhere,
            anywhere,
            anywhere,
        ],
        out_specs=(vmem,) * 5,
        scratch_shapes=[
            pltpu.VMEM(attended.shape, jnp.float32),
            pltpu.VMEM(cot.shape, low),
            pltpu.VMEM(weight.shape, low),
            pltpu.VMEM(packed.shape, low),
            pltpu.SemaphoreType.DMA((4,)),
            pltpu.VMEM(mid.shape, low),
            pltpu.VMEM((blocks, rows, part), low),
            pltpu.VMEM((length, part), low),
            pltpu.VMEM((length, columns), low),
            pltpu.VMEM((length, HEAD), jnp.float32),
            pltpu.VMEM((length, HEAD), jnp.float32),
            pltpu.SemaphoreType.DMA((4,)),
            pltpu.SemaphoreType.DMA((2, blocks)),
            pltpu.SemaphoreType.DMA((2, 3, blocks)),
            pltpu.VMEM((2, features // STRIPS, groups[-1][1][0].shape[1]), low),
            pltpu.SemaphoreType.DMA((2,)),
            pltpu.SemaphoreType.REGULAR,
            *scratch,
        ],
        compiler_params=remote_params(call),
        cost_estimate=cost,
    )(doc_ends, *lefts, rights, mid, attended, cot, gain[None], weight, packed, down)
    return unstacked(groups, folded), resid, gain_grad[0], moved, result


def last_kernel(
    fold, marks, first_left, second_left, third_left, right_ref, normed_part, memory_part, hidden_ref,
    memory_ref, resid_ref, gains_ref, mid_gain_ref, out_ref, hidden_grad, memory_grad, gain_out, *scratch
):
    steps = fold[0][0]
    count = len(steps)
    normed_other, memory_other, hidden, memory, resid = scratch[:5]
    load_sem, heads_sem, gain_sem, gain_held = scratch[5:9]
    gain_got = scratch[9 : 9 + count]
    left_refs = (first_left, second_left, third_left)
    loads, turn, finish, partners = fold_engine(
        *fold, left_refs, right_ref, out_ref, scratch[9 + count :]
    )
    rows, features = normed_part.shape
    dp, blk, heads = (lax.axis_index(axis) for axis in MESH_AXES)
    mirror = (dp, blk, flipped(heads, 1))
    loads = loads + [
        pltpu.make_async_copy(source, target, load_sem.at[number])
        for number, (source, target) in enumerate(
            [(hidden_ref, hidden), (memory_ref, memory), (resid_ref, resid)]
        )
    ]
    for load in loads:
        load.start()
    greet(partners + [mirror])
    mirrored = [
        pltpu.make_async_remote_copy(
            src_ref=source,
            dst_ref=target,
            send_sem=heads_sem.at[0, number],
            recv_sem=heads_sem.at[1, number],
            device_id=mirror,
            device_id_type=MESH,
        )
        for number, (source, target) in enumerate(
            [(normed_part, normed_other), (memory_part, memory_other)]
        )
    ]
    for copy in mirrored:
        copy.start()
    for load in loads:
        load.wait()
    offsets, part = fold_order(features, steps)

    def keep_gain(number, gain_grad):
        for place, offset in enumerate(offsets):
            columns = pl.ds(pl.multiple_of(offset, part), part)
            gain_held[place, number : number + 1] = gain_grad[:, columns]

    def norm_back(number):
        mirrored[number].wait()
        own, other = ((normed_part, normed_other), (memory_part, memory_other))[number]
        source, target = ((hidden, hidden_grad), (memory, memory_grad))[number]
        step = rows // 3 if rows % 48 == 0 else rows
        gain_total = None
        for start in range(0, rows, step):
            here = slice(start, start + step)
            values = source[here].astype(jnp.float32)
            grad = pair_add(own[here], other[here])
            scale = lax.rsqrt(jnp.mean(values * values, axis=-1, keepdims=True) + EPSILON)
            normed = values * scale
            scaled = grad * gains_ref[number : number + 1]
            inner = jnp.mean(scaled * normed, axis=-1, keepdims=True)
            total = scale * (scaled - normed * inner)
            target[here] = total + resid[here] if number == 0 else total
            gain_part = jnp.sum(grad * normed, axis=0, keepdims=True)
            gain_total = gain_part if gain_total is None else gain_total + gain_part
        gain_sum[...] = gain_total
        keep_gain(number, gain_sum)

    gain_sum = scratch[-1]

    def gain_copy(step):
        half = (1 << count) >> (step + 1)
        return pltpu.make_async_remote_copy(
            src_ref=gain_held.at[pl.ds(half, half)],
            dst_ref=gain_got[step],
            send_sem=gain_sem.at[0, step],
            recv_sem=gain_sem.at[1, step],
            device_id=partners[step],
            device_id_type=MESH,
        )

    def gain_step(step):
        if step > 0:
            gain_copy(step - 1).wait()
            half = (1 << count) >> step
            gain_held[:half] += gain_got[step - 1][...]
        if step < count:
            gain_copy(step).start()

    def body(index, carry):
        turn(index)

        @pl.when(index == marks[0])
        def _():
            gain_held[...] = jnp.zeros_like(gain_held)
            keep_gain(2, mid_gain_ref)
            norm_back(0)

        @pl.when(index == marks[1])
        def _():
            norm_back(1)

        for step in range(count):

            @pl.when(index == marks[1] + step)
            def _(step=step):
                gain_step(step)

        return carry

    lax.fori_loop(0, fold[2] + fold[6][-1], body, 0)
    gain_step(count)
    gain_out[...] = gain_held[0]
    finish()


def last(groups, normed_part, memory_part, hidden, memory, resid, gains, mid_gain_grad, call, marks, width=256, slots=12):
    fold, lefts, rights, shape, scratch, cost = fold_setting(groups, width, slots, 6)
    count = len(fold[0][0])
    marks = tuple(min(mark, fold[2] + fold[6][-1] - count) for mark in marks)
    rows, features = normed_part.shape
    part = features >> count
    vmem, anywhere = (pl.BlockSpec(memory_space=space) for space in (pltpu.VMEM, pl.ANY))
    folded, hidden_grad, memory_grad, gain_grads = pl.pallas_call(
        functools.partial(last_kernel, fold, marks),
        out_shape=(
            shape,
            jax.ShapeDtypeStruct(hidden.shape, jnp.float32),
            jax.ShapeDtypeStruct(hidden.shape, jnp.float32),
            jax.ShapeDtypeStruct((8, part), jnp.float32),
        ),
        in_specs=[anywhere] * 3 + [vmem] * 3 + [anywhere] * 3 + [vmem] * 2,
        out_specs=(vmem,) * 4,
        scratch_shapes=[
            pltpu.VMEM(hidden.shape, jnp.bfloat16),
            pltpu.VMEM(hidden.shape, jnp.bfloat16),
            pltpu.VMEM(hidden.shape, jnp.bfloat16),
            pltpu.VMEM(hidden.shape, jnp.bfloat16),
            pltpu.VMEM(hidden.shape, jnp.float32),
            pltpu.SemaphoreType.DMA((3,)),
            pltpu.SemaphoreType.DMA((2, 2)),
            pltpu.SemaphoreType.DMA((2, count)),
            pltpu.VMEM((1 << count, 8, part), jnp.float32),
            *[pltpu.VMEM(((1 << count) >> (step + 1), 8, part), jnp.float32) for step in range(count)],
            *scratch,
            pltpu.VMEM((1, features), jnp.float32),
        ],
        compiler_params=remote_params(call),
        cost_estimate=cost,
    )(*lefts, rights, normed_part, memory_part, hidden, memory, resid, gains, mid_gain_grad[None])
    return unstacked(groups, folded), hidden_grad, memory_grad, gain_grads


def by_head(array):
    return array.reshape(array.shape[0], -1, HEAD).transpose(1, 0, 2)


def from_heads(array):
    return array.transpose(1, 0, 2).reshape(array.shape[1], -1).astype(jnp.bfloat16)


def plain_probs(doc_ends, query_pos, query, key):
    key_pos = jnp.arange(key.shape[0], dtype=jnp.int32)
    first = first_allowed(doc_ends, query_pos)
    allowed = (key_pos[None, :] >= first[:, None]) & (key_pos[None, :] <= query_pos[:, None])
    scores = dot_rows(query, key) * (1.0 / math.sqrt(HEAD))
    return jax.nn.softmax(jnp.where(allowed, scores, NEGATIVE), axis=-1)


def plain_attend(doc_ends, query_pos, queries, keys, values):
    def one(arrays):
        query, key, value = arrays
        probs = plain_probs(doc_ends, query_pos, query, key)
        return plain_dot(probs.astype(jnp.bfloat16), value)

    return from_heads(lax.map(one, (by_head(queries), by_head(keys), by_head(values))))


def plain_attend_back(doc_ends, query_pos, queries, keys, values, grads):
    factor = 1.0 / math.sqrt(HEAD)

    def one(arrays):
        query, key, value, grad = arrays
        probs = plain_probs(doc_ends, query_pos, query, key)
        prob_grad = dot_rows(grad, value)
        delta = jnp.sum(probs * prob_grad, axis=-1, keepdims=True)
        score_grad = (probs * (prob_grad - delta)).astype(jnp.bfloat16)
        return (
            plain_dot(score_grad, key) * factor,
            dot_cols(score_grad, query) * factor,
            dot_cols(probs.astype(jnp.bfloat16), grad),
        )

    arrays = tuple(by_head(array) for array in (queries, keys, values, grads))
    return tuple(from_heads(grad) for grad in lax.map(one, arrays))


def local(
    hidden_in,
    memory,
    lengths,
    query_weight,
    key_weight,
    value_weight,
    output_weight,
    gate_weight,
    up_weight,
    down_weight,
    attention_gain,
    memory_gain,
    feedforward_gain,
    cotangent,
):
    rows, features = hidden_in.shape
    blocks = lax.axis_size("blk")
    width = query_weight.shape[1]
    hidden_units = gate_weight.shape[1]
    heads_local = width // HEAD
    spread = heads_local % blocks == 0 and lax.axis_size("heads") == 2
    doc_ends = jnp.cumsum(lengths[0], dtype=jnp.int32)

    gains = jnp.stack([attention_gain, memory_gain, feedforward_gain], axis=1)
    gains = jnp.pad(gains, ((0, 0), (0, LANES - gains.shape[1])))
    attn_mine = jnp.concatenate(
        [query_weight, key_weight, value_weight, output_weight, gains], axis=1
    )
    attn_full = lax.all_gather(attn_mine, ("dp", "blk"), axis=0, tiled=True)
    padded = -(-hidden_units // (2 * LANES)) * (2 * LANES)
    ffn_mine = jnp.concatenate(
        [
            jnp.pad(weight, ((0, 0), (0, padded - hidden_units)))
            for weight in (gate_weight, up_weight, down_weight)
        ],
        axis=1,
    )
    ffn_mine, attn_full = together(ffn_mine, attn_full)
    ffn_full = lax.all_gather(ffn_mine, ("dp", "blk"), axis=0, tiled=True)

    full_query = attn_full[:, :width]
    full_key = attn_full[:, width : 2 * width]
    full_value = attn_full[:, 2 * width : 3 * width]
    full_output = attn_full[:, 3 * width : 4 * width]
    full_gains = attn_full[:, 4 * width : 4 * width + 3].astype(jnp.float32).T
    input_gain, source_gain, mid_gain = full_gains[0], full_gains[1], full_gains[2]

    hidden_float = hidden_in.astype(jnp.float32)
    memory_float = memory.astype(jnp.float32)
    memory_low = rms_scale(memory_float, source_gain).astype(jnp.bfloat16)
    normed_low = rms_scale(hidden_float, input_gain).astype(jnp.bfloat16)
    key_low = plain_dot(memory_low, full_key).astype(jnp.bfloat16)
    value_low = plain_dot(memory_low, full_value).astype(jnp.bfloat16)
    query_low = plain_dot(normed_low, full_query).astype(jnp.bfloat16)

    if spread:
        packed = to_heads([query_low, key_low, value_low], blocks)
        context_low = side_by_side(swap_blocks(attend(doc_ends, packed), blocks), 1)[0]
    else:
        query_pos = lax.axis_index("blk") * rows + jnp.arange(rows, dtype=jnp.int32)
        key_all = lax.all_gather(key_low, "blk", axis=0, tiled=True)
        value_all = lax.all_gather(value_low, "blk", axis=0, tiled=True)
        context_low = plain_attend(doc_ends, query_pos, query_low, key_all, value_all)

    attended = hidden_float + pair_sum(dot_rows(context_low, full_output))
    attended, cot_turned, normed_turned, memory_turned = together(
        attended, cotangent.T, normed_low.T, memory_low.T
    )
    mid_low = rms_scale(attended, mid_gain).astype(jnp.bfloat16)

    full_gate = ffn_full[:, :padded]
    full_up = ffn_full[:, padded : 2 * padded]
    full_down = ffn_full[:, 2 * padded :]
    gate = plain_dot(mid_low, full_gate)
    upward = plain_dot(mid_low, full_up)
    sigma = jax.nn.sigmoid(gate)
    silu_gate = gate * sigma
    act_low = (silu_gate * upward).astype(jnp.bfloat16)
    act_grad = plain_dot(cotangent, full_down)
    gate_grad_low = (act_grad * upward * sigma * (1.0 + gate * (1.0 - sigma))).astype(jnp.bfloat16)
    up_grad_low = (act_grad * silu_gate).astype(jnp.bfloat16)
    mid_part = dot_rows(gate_grad_low, full_gate) + dot_rows(up_grad_low, full_up)
    mid_part = mid_part.astype(jnp.bfloat16)
    products = [(mid_low.T, [gate_grad_low, up_grad_low]), (cot_turned, [act_low])]
    if spread:
        shares, attended_grad, mid_gain_grad, moved, output = middle(
            products,
            doc_ends,
            mid_part,
            attended,
            cotangent,
            mid_gain,
            full_output,
            packed,
            ffn_full,
            0,
            MARKS,
        )
        resid_low = attended_grad.astype(jnp.bfloat16)
        query_grad_low, key_grad_low, value_grad_low = (
            moved[:, i * width : (i + 1) * width] for i in range(3)
        )
    else:
        shares = fold_products(products, 0)
        output = (attended + pair_sum(dot_rows(act_low, full_down))).astype(jnp.bfloat16)
        mid_grad = pair_sum(mid_part)
        attended_norm_grad, mid_gain_grad = jax.vjp(rms_scale, attended, mid_gain)[1](mid_grad)
        attended_grad = cotangent.astype(jnp.float32) + attended_norm_grad
        resid_low = attended_grad.astype(jnp.bfloat16)
        context_grad_low = plain_dot(resid_low, full_output).astype(jnp.bfloat16)
        query_grad_low, key_grad, value_grad = plain_attend_back(
            doc_ends, query_pos, query_low, key_all, value_all, context_grad_low
        )
        moved = lax.psum_scatter(
            jnp.concatenate([key_grad, value_grad], axis=1), "blk", scatter_dimension=0, tiled=True
        )
        key_grad_low, value_grad_low = moved[:, :width], moved[:, width:]
    (gate_share, up_share), (down_share,) = shares
    normed_part = dot_rows(query_grad_low, full_query).astype(jnp.bfloat16)
    memory_part = (
        dot_rows(key_grad_low, full_key) + dot_rows(value_grad_low, full_value)
    ).astype(jnp.bfloat16)
    if spread:
        right_sets = ([context_low], [moved[:, :width]], [moved[:, width:]])
    else:
        right_sets = ([context_low], [query_grad_low], [key_grad_low, value_grad_low])
    products = list(zip((resid_low.T, normed_turned, memory_turned), right_sets))
    if spread:
        shares, hidden_grad, memory_grad, gain_shares = last(
            products,
            normed_part,
            memory_part,
            hidden_in,
            memory,
            attended_grad,
            jnp.stack([input_gain, source_gain], axis=0),
            mid_gain_grad,
            1,
            LAST_MARKS,
        )
    else:
        shares = fold_products(products, 1)
        normed_grad = pair_sum(normed_part)
        memory_in_grad = pair_sum(memory_part)
        hidden_norm_grad, input_gain_grad = jax.vjp(rms_scale, hidden_float, input_gain)[1](
            normed_grad
        )
        memory_grad, source_gain_grad = jax.vjp(rms_scale, memory_float, source_gain)[1](
            memory_in_grad
        )
        hidden_grad = attended_grad + hidden_norm_grad
        gain_shares = fold_vector(
            jnp.stack([input_gain_grad, source_gain_grad, mid_gain_grad], axis=0)
        )
    (output_share,), (query_share,), both = shares
    both = jnp.concatenate(both, axis=1)
    key_share, value_share = both[:, :width], both[:, width:]
    gate_share, up_share, down_share = (
        share[:, :hidden_units] for share in (gate_share, up_share, down_share)
    )
    return (
        output,
        hidden_grad,
        memory_grad,
        query_share,
        key_share,
        value_share,
        output_share,
        gate_share,
        up_share,
        down_share,
        gain_shares[0],
        gain_shares[1],
        gain_shares[2],
    )


def solution(mesh):
    tokens = P(("dp", "blk"), None)
    weight = P(("dp", "blk"), "heads")
    gain = P(("dp", "blk"))
    return jax.shard_map(
        local,
        mesh=mesh,
        in_specs=(tokens, tokens, P("dp", None)) + (weight,) * 7 + (gain,) * 3 + (tokens,),
        out_specs=(tokens,) * 3 + (weight,) * 7 + (gain,) * 3,
        check_vma=False,
    )
```

time: 1080 us -> 822 us (0.76)
  waiting for transfers between devices: 342 us -> 238 us
  matrix products: 144 us -> 81 us
  other arithmetic: 67 us -> 15.6 us
  local copies, waits for them, and re-layouts: 89.2 us -> 56.6 us
  starting transfers between devices: 28 us -> 6.6 us
  Pallas kernels: 362 us -> 373 us
    ppermute x9 -> x1, waiting for transfers between devices: 77.3 us -> 15.8 us  [swap(): return lax.ppermute(array, axis, [(i, i ^ bit) for i in range(size)])]
    dot_general x6 -> x0, matrix products: 49 us -> none  [the longest x1 14.8 us: local(): jnp.einsum('qhd,khd->hqk', context_grad_heads, value_heads, preferred_ele...]
    all_to_all x1 -> x0, waiting for transfers between devices: 44.3 us -> none  [to_blocks(): moved = lax.all_to_all(packed, 'blk', 0, 0)]
    unnamed x109 -> x70, local copies, waits for them, and re-layouts: 59.4 us -> 32.3 us
    reduce_sum x6 -> x0, other arithmetic: 20.7 us -> none  [the longest x3 11.4 us: rms_scale(): values * lax.rsqrt(jnp.mean(values * values, axis=-1, keepdims=True) + EP...]
    all_to_all x2 -> x1, waiting for transfers between devices: 83.6 us -> 67.5 us  [to_heads(): moved = lax.all_to_all(packed, 'blk', 0, 0)]
    convert_element_type x8 -> x0, local copies, waits for them, and re-layouts: 11.9 us -> none  [the longest x6 9.43 us: local(): grad.reshape(grad.shape[0], -1).astype(jnp.bfloat16)]
    unnamed x5 -> x0, other arithmetic: 11.8 us -> none
  transfers between devices with their start and end apart: 14 -> 4, of which waited for: 10 -> 4; matrix products, arithmetic and copies ran while one was open for 16% -> 7% of each run, Pallas kernels for 34% -> 1%
where the time goes in v3:
time: 822 us; the launch traced here: 813 us
  Pallas kernels  373 us (45%)
  waiting for transfers between devices  238 us (29%)
  matrix products  81 us (10%)
  local copies, waits for them, and re-layouts  56.6 us (7%)
  blocking collectives  27.7 us (3%)
  other arithmetic  15.6 us (2%)
  between operations  14.9 us (2%)
    pallas_call x1, Pallas kernels, middle(): pl.pallas_call(functools.partial(middle_kernel, fold, marks, tile, 1.0 /...  254 us
    pallas_call x1, Pallas kernels, last(): pl.pallas_call(functools.partial(last_kernel, fold, marks), out_shape=(sh...  111 us
    all_gather x1, waiting for transfers between devices, local(): attn_full = lax.all_gather(attn_mine, ('dp', 'blk'), axis=0, tiled=True)  95.2 us
    all_to_all x1, waiting for transfers between devices, to_heads(): moved = lax.all_to_all(packed, 'blk', 0, 0)  67.5 us
    all_gather x1, waiting for transfers between devices, local(): ffn_full = lax.all_gather(ffn_mine, ('dp', 'blk'), axis=0, tiled=True)  59.8 us
    dot_general x6, matrix products, plain_dot(): return jnp.dot(left, right, preferred_element_type=jnp.float32)  42.6 us
    dot_general x6, matrix products, dot_rows(): lax.dot_general(left, right, (((1,), (1,)), ((), ())), preferred_element_...  38.4 us
    unnamed x70, local copies, waits for them, and re-layouts  32.3 us
  transfers between devices with their start and end apart: 4, of which 4 were waited for; matrix products, arithmetic and copies ran while one was open for 7% of the time, Pallas kernels for 1%

profile of v3, /device:TPU:0, one launch (start us, length us, event | category | flops | bytes accessed | tf_op | source)
XLA Modules:
  0.0 813.4 jit_solution(14912984685807845056)
XLA Ops:
  7.3 1.2 copy.31
  8.5 1.1 copy.32
  9.6 1.1 copy.33
  10.7 1.1 copy.34
  12.1 1.0 copy-done.12
  13.4 1.4 copy.29
  14.8 1.4 copy.30
  16.2 1.5 fusion.44
  17.6 95.2 %all-gather.3.cloned.1.call-done = bf16[2048,4224]{0,1:T(8,128)(2,1)} async-done(((bf16[128,4224]{0,1:T(8,128)(2,1)}), bf16[2048,4224]{0,1:T(8,128)(2,1)}) %all-gather.3.cloned.1.call-update) | async-done | bytes 17301520 | tf_op jit(solution)/shard_map/all_gather | solution.py:923
  112.9 0.9 copy.35
  113.7 2.4 copy.27
  116.2 0.4 fusion.30
  116.6 0.4 fusion.33
  117.1 0.8 convert_bitcast_fusion.1
  117.9 4.4 fusion.48
  122.4 4.6 fusion.51
  127.1 4.6 fusion.45
  131.9 1.7 pad_maximum_fusion.1
  133.6 5.0 all-to-all-start
  138.8 67.5 %all-to-all-done = bf16[4,384,768]{2,1,0:T(8,128)(2,1)S(1)} async-done(((bf16[4,384,768]{2,1,0:T(8,128)(2,1)}), bf16[4,384,768]{2,1,0:T(8,128)(2,1)S(1)}, u32[]{:S(2)}, u32[]{:S(2)}) %all-to-all-start) | async-done | bytes 2359328 | tf_op jit(solution)/shard_map/all_to_all | solution.py:327
  206.3 7.6 shard_map.237
  213.9 27.7 %all_to_all.10 = bf16[4,384,256]{2,1,0:T(8,128)(2,1)S(1)} all-to-all(bf16[4,384,256]{2,1,0:T(8,128)(2,1)S(1)} %bitcast.61), channel_id=1, replica_groups=mesh['dp'=4,'blk'=4,'heads'=2] {'blk'}, dimensions={0} | all-to-all | bytes 1572864 | tf_op jit(solution)/shard_map/all_to_all | solution.py:333
  241.7 6.0 convolution_convert_fusion
  247.7 1.5 collective-permute-start
  249.1 1.6 copy.37
  250.7 4.8 slice.155
  255.6 0.6 stack.40.gains_ref
  256.2 6.5 copy.40.weight_ref
  262.7 1.7 fusion.74.third_left
  264.4 0.7 constant_dynamic-update-slice_fusion.8
  265.1 0.7 constant_dynamic-update-slice_fusion.7
  265.8 0.7 constant_dynamic-update-slice_fusion.6
  266.4 0.7 constant_dynamic-update-slice_fusion.5
  267.1 15.8 %collective-permute-done = bf16[384,2048]{0,1:T(8,128)(2,1)} collective-permute-done((bf16[384,2048]{0,1:T(8,128)(2,1)}, bf16[384,2048]{0,1:T(8,128)(2,1)}, u32[]{:S(2)}, u32[]{:S(2)}) %collective-permute-start) | collective-permute-done | bytes 1572896 | tf_op jit(solution)/shard_map/ppermute | solution.py:44
  282.9 3.9 fusion.64
  286.8 2.4 copy.39.attended_ref
  289.2 0.3 multiply_reduce_fusion
  289.5 1.6 fusion.88.first_left
  291.1 59.8 %all-gather.5.cloned.1.call-done.down_ref = bf16[2048,8448]{1,0:T(8,128)(2,1)} async-done(((bf16[128,8448]{1,0:T(8,128)(2,1)}), bf16[2048,8448]{1,0:T(8,128)(2,1)}) %all-gather.5.cloned.1.call-update) | async-done | bytes 34603024 | tf_op jit(solution)/shard_map/all_gather | solution.py:933
  350.9 8.2 %fusion.8 = f32[384,2816]{1,0:T(8,128)S(1)} fusion(bf16[2048,8448]{1,0:T(8,128)(2,1)} %all-gather.5.cloned.1.call-done.down_ref, f32[384,2048]{0,1:T(8,128)S(1)} %get-tuple-element.29, f32[2048]{0:T(1024)S(1)} %bitcast.67, f32[384]{0:T(512)S(1)} %add_rsqrt_fusion), kind=kOutput, calls=%fused_computation.8 | convolution fusion | flops 4431544320 | bytes 19015168 | tf_op jit(solution)/shard_map/dot_general | solution.py:27
  359.2 9.5 %fusion.10 = f32[384,2816]{1,0:T(8,128)} fusion(bf16[384,2048]{1,0:T(8,128)(2,1)S(1)} %copy-done.7, bf16[2048,8448]{1,0:T(8,128)(2,1)} %all-gather.5.cloned.1.call-done.down_ref), kind=kOutput, calls=%fused_computation.16 | convolution fusion | flops 4429185024 | bytes 17432576 | tf_op jit(solution)/shard_map/dot_general | solution.py:27
  368.6 11.3 %multiply_convert_fusion.2 = (bf16[384,2816]{1,0:T(8,128)(2,1)S(1)}, bf16[384,2816]{1,0:T(8,128)(2,1)S(1)}, bf16[384,2816]{1,0:T(8,128)(2,1)S(1)}) fusion(f32[384,2816]{1,0:T(8,128)} %fusion.10, f32[384,2816]{1,0:T(8,128)S(1)} %fusion.8, bf16[2048,8448]{1,0:T(8,128)(2,1)} %all-gather.5.cloned.1.call-done.down_ref, f32[384,2048]{0,1:T(8,128)S(1)} %get-tuple-element.29, ...), kind=kOutput, calls=%fused_computation.21 | convolution fusion | flops 4447764480 | bytes 29828608 | tf_op jit(solution)/shard_map/dot_general | solution.py:27
  379.9 3.0 pad_maximum_fusion.right_ref
  382.9 7.5 fusion.2
  390.5 10.1 %add_convert_fusion.1.mid_ref = bf16[384,2048]{1,0:T(8,128)(2,1)} fusion(f32[384,2048]{1,0:T(8,128)S(1)} %fusion.2, bf16[384,2816]{1,0:T(8,128)(2,1)S(1)} %get-tuple-element.58, bf16[2048,8448]{1,0:T(8,128)(2,1)} %all-gather.5.cloned.1.call-done.down_ref), kind=kOutput, calls=%fused_computation.49 | convolution fusion | flops 4430757888 | bytes 18415616 | tf_op jit(solution)/shard_map/dot_general | solution.py:31
  400.6 254.1 %shard_map.238 = (f32[128,8448]{1,0:T(8,128)}, f32[384,2048]{1,0:T(8,128)}, f32[1,2048]{1,0:T(1,128)}, bf16[384,3072]{1,0:T(8,128)(2,1)}, bf16[384,2048]{1,0:T(8,128)(2,1)}) custom-call(s32[4]{0:T(128)} %bitcast.63, bf16[2048,384]{1,0:T(8,128)(2,1)} %fusion.88.first_left, bf16[2048,384]{1,0:T(8,128)(2,1)} %bitcast.64, ...), custom_call_target="tpu_custom_call" | custom-call | flops 13287555072 | bytes 138412032 | tf_op jit(solution)/shard_map/pallas_call | solution.py:646
  654.6 4.4 fusion.18
  659.0 5.2 fusion.40.normed_part
  664.2 5.3 add_convert_fusion.memory_part
  669.7 1.7 copy-done.18
  671.4 1.2 copy-done.10
  672.5 1.7 copy.41
  674.2 111.1 %shard_map.239 = (f32[128,4096]{1,0:T(8,128)}, f32[384,2048]{1,0:T(8,128)}, f32[384,2048]{1,0:T(8,128)}, f32[8,128]{1,0:T(8,128)}) custom-call(bf16[2048,384]{1,0:T(8,128)(2,1)} %bitcast.65, bf16[2048,384]{1,0:T(8,128)(2,1)} %get-tuple-element.34.second_left, bf16[2048,384]{1,0:T(8,128)(2,1)} %fusion.74.third_left, bf16[384,4096]{1,0:T(8,128)(2,1)} %copy-done.18, ...), custom_call_target="tpu_custom_call" | custom-call | flops 6442450944 | bytes 67108864 | tf_op jit(solution)/shard_map/pallas_call | solution.py:820
  785.2 2.9 fusion.78
  788.1 1.3 slice_bitcast_fusion.4
  789.4 3.6 fusion.77
  793.1 2.9 copy.42
  796.0 1.5 copy.43
  797.5 1.5 copy.44
  799.0 1.1 copy.58
  800.2 1.3 copy-done.9
  801.5 1.7 copy.59
  803.1 1.4 copy-done.8
  804.5 1.7 copy.60
  (63 shorter events, 1.4 us)
Async XLA Ops:
  7.2 4.8 copy-start.21
  7.2 4.8 copy-start.20
  7.2 4.8 copy-start.19
  7.2 5.9 copy-start.15
  7.2 105.6 %all-gather.3.cloned.1.call-start = ((), (), s32[]{:S(2)}) async-start(), calls=%async_computation.2 | async-start | bytes 18382848 | tf_op jit(solution)/shard_map/all_gather | solution.py:923
  12.0 1.0 copy-start.12
  13.1 337.8 %all-gather.5.cloned.1.call-start = ((), (), s32[]{:S(2)}) async-start(), calls=%async_computation.3 | async-start | bytes 36765696 | tf_op jit(solution)/shard_map/all_gather | solution.py:933
  17.6 95.2 %copy-start.13 = (bf16[384,2048]{1,0:T(8,128)(2,1)S(1)}, bf16[384,2048]{1,0:T(8,128)(2,1)}, u32[]{:S(2)}) copy-start(bf16[384,2048]{1,0:T(8,128)(2,1)} %memory_ref.1) | copy-start | bytes 4718596
  113.7 8.6 %copy-start.2 = (bf16[384,2048]{0,1:T(8,128)(2,1)}, bf16[384,2048]{0,1:T(8,128)(2,1)S(1)}, u32[]{:S(2)}) copy-start(bf16[384,2048]{0,1:T(8,128)(2,1)S(1)} %copy.35) | copy-start | bytes 4718596
  116.2 10.9 %copy-start.4 = (bf16[384,2048]{0,1:T(8,128)(2,1)}, bf16[384,2048]{0,1:T(8,128)(2,1)S(1)}, u32[]{:S(2)}) copy-start(bf16[384,2048]{0,1:T(8,128)(2,1)S(1)} %copy.27) | copy-start | bytes 4718596
  117.8 250.8 %copy-start.16 = (f32[1,2048]{1,0:T(1,128)}, f32[1,2048]{1,0:T(1,128)S(1)}, u32[]{:S(2)}) copy-start(f32[1,2048]{1,0:T(1,128)S(1)} %get-tuple-element.84.gain_ref) | copy-start | bytes 24580
  133.6 5.0 copy-start.22
  133.6 72.7 %all-to-all-start = ((bf16[4,384,768]{2,1,0:T(8,128)(2,1)}), bf16[4,384,768]{2,1,0:T(8,128)(2,1)S(1)}, u32[]{:S(2)}, u32[]{:S(2)}) async-start(bf16[4,384,768]{2,1,0:T(8,128)(2,1)} %pad_maximum_fusion.1), calls=%async_computation | async-start | bytes 4718592 | tf_op jit(solution)/shard_map/all_to_all | solution.py:327
  138.8 75.1 %copy-start.1 = (s32[4,1]{0,1:T(1,128)}, s32[4,1]{0,1:T(1,128)S(1)}, u32[]{:S(2)}) copy-start(s32[4,1]{0,1:T(1,128)S(1)} %reduce-window.9) | copy-start | bytes 52
  206.3 7.6 copy-start
  241.7 7.5 copy-start.6
  247.7 35.2 %collective-permute-start = (bf16[384,2048]{0,1:T(8,128)(2,1)}, bf16[384,2048]{0,1:T(8,128)(2,1)}, u32[]{:S(2)}, u32[]{:S(2)}) collective-permute-start(bf16[384,2048]{0,1:T(8,128)(2,1)} %convolution_convert_fusion), channel_id=1, source_target_pairs={{0,1},{1,0},{2,3},{3,2},{4,5},{5,4},{6,7},{7,6},{8,9},{9,8},{10,11... | collective-permute-start | bytes 4718600 | tf_op jit(solution)/shard_map/ppermute | solution.py:44
  256.2 6.5 copy-start.3
  262.7 20.2 %copy-start.5 = (bf16[384,2048]{0,1:T(8,128)(2,1)S(1)}, bf16[384,2048]{0,1:T(8,128)(2,1)}, u32[]{:S(2)}) copy-start(bf16[384,2048]{0,1:T(8,128)(2,1)} %copy-done.4) | copy-start | bytes 4718596
  350.9 8.3 %copy-start.7 = (bf16[384,2048]{1,0:T(8,128)(2,1)S(1)}, bf16[384,2048]{1,0:T(8,128)(2,1)}, u32[]{:S(2)}) copy-start(bf16[384,2048]{1,0:T(8,128)(2,1)} %cot_ref.1) | copy-start | bytes 4718596
  654.6 4.4 copy-start.11
  664.2 5.3 copy-start.17
  669.5 3.0 copy-start.10
  669.7 1.7 copy-start.18
  797.5 1.5 copy-start.14
  799.0 2.5 copy-start.9
  801.5 3.0 copy-start.8
Sparse Core Ops, SparseCore 0:
  13.2 99.6 all-gather.2
  114.4 236.4 all-gather.4

commit v4 on v3

--- a/solution.py
+++ b/solution.py
@@ -153,8 +153,12 @@
         for edge in edges:
             group = group + (tile >= edge).astype(jnp.int32)
         columns = pl.ds(pl.multiple_of(tile * width, width), width)
+        each = right_ref.shape[2] // width
+        own = pl.ds(pl.multiple_of(lax.rem(tile, each) * width, width), width)
         total = jnp.dot(
-            held[plan, group, low:high], right_ref[:, columns], preferred_element_type=jnp.float32
+            held[plan, group, low:high],
+            right_ref[tile // each, :, own],
+            preferred_element_type=jnp.float32,
         )
         for earlier in range(number):
             total = total + got[earlier][slot, low:high].astype(jnp.float32)
@@ -243,18 +247,15 @@
     ]
 
 
-def fold_setting(groups, width, slots, period):
+def fold_layout(lefts, right_sets, width, slots, period):
     steps = fold_steps()
     plans = [steps]
     if lax.axis_size("dp") > 2 and period and slots % period == 0:
         plans.append(late_steps(steps))
     edges, tiles = [], 0
-    for _, many in groups:
+    for many in right_sets:
         tiles += sum(right.shape[1] for right in many) // width
         edges.append(tiles)
-    lefts = [left for left, _ in groups]
-    rights = [right for _, many in groups for right in many]
-    rights = rights[0] if len(rights) == 1 else jnp.concatenate(rights, axis=1)
     fold = (plans, edges[:-1], tiles, width, slots, period, fold_lags(len(steps)))
     features, rows = lefts[0].shape
     shape = jax.ShapeDtypeStruct((features >> len(steps), tiles * width), jnp.float32)
@@ -264,6 +265,14 @@
         bytes_accessed=tiles * width * features * 8,
         transcendentals=0,
     )
+    return fold, shape, scratch, cost
+
+
+def fold_setting(groups, width, slots, period):
+    lefts = [left for left, _ in groups]
+    right_sets = [many for _, many in groups]
+    rights = jnp.concatenate([right for many in right_sets for right in many], axis=1)[None]
+    fold, shape, scratch, cost = fold_layout(lefts, right_sets, width, slots, period)
     return fold, lefts, rights, shape, scratch, cost
 
 
@@ -429,16 +438,16 @@
 
 
 def middle_kernel(
-    fold, marks, tile, factor, ends, first_left, second_left, right_ref, mid_ref, attended_ref, cot_ref,
-    gain_ref, weight_ref, packed_ref, down_ref, out_ref, resid_ref, gain_out, moved, result, *scratch
+    fold, marks, tile, factor, ends, first_left, second_left, right_ref, attended_ref, cot_ref, gain_ref,
+    weight_ref, packed_ref, mid, feed_ref, out_ref, resid_ref, gain_out, moved, result, *scratch
 ):
     count = len(fold[0][0])
     attended, cot, weight, packed, load_sem = scratch[:5]
     other, sent_grads, grads, out, key_sum, value_sum = scratch[5:11]
-    heads_sem, ctx_sem, out_sem, down, down_sem, ready = scratch[11:17]
+    heads_sem, ctx_sem, out_sem, strip_rows, strip_sem, ready = scratch[11:17]
     left_refs = (first_left, second_left)
     loads, turn, finish, partners = fold_engine(*fold, left_refs, right_ref, out_ref, scratch[17:])
-    rows, features = mid_ref.shape
+    rows, features = mid.shape
     blocks, _, part = sent_grads.shape
     dp, blk, heads = (lax.axis_index(axis) for axis in MESH_AXES)
 
@@ -461,16 +470,42 @@
     ]
     for load in loads:
         load.start()
+    strip = strip_rows.shape[1]
+    strips = features // strip
+    units = right_ref.shape[2]
+
+    def strip_copy(number):
+        slot = lax.rem(number, 2)
+        rows_of = pl.ds(pl.multiple_of(number * strip, strip), strip)
+        return pltpu.make_async_copy(
+            feed_ref.at[rows_of, pl.ds(2 * units, units)], strip_rows.at[slot], strip_sem.at[slot]
+        )
+
+    def strip_step(number):
+        strip_copy(number).wait()
+
+        @pl.when(number + 1 < strips)
+        def _():
+            strip_copy(number + 1).start()
+
+        columns = pl.ds(pl.multiple_of(number * strip, strip), strip)
+        product = dot_rows(right_ref[2], strip_rows[lax.rem(number, 2)])
+        cot[:, columns] = product.astype(jnp.bfloat16)
+
     greet(met)
-    mirrored = pltpu.make_async_remote_copy(
-        src_ref=mid_ref,
-        dst_ref=other,
-        send_sem=heads_sem.at[0],
-        recv_sem=heads_sem.at[1],
-        device_id=mirror,
-        device_id_type=MESH,
-    )
-    mirrored.start()
+
+    def mirrored(source, number):
+        return pltpu.make_async_remote_copy(
+            src_ref=source,
+            dst_ref=other,
+            send_sem=heads_sem.at[0, number],
+            recv_sem=heads_sem.at[1, number],
+            device_id=mirror,
+            device_id_type=MESH,
+        )
+
+    first, second = mirrored(mid, 0), mirrored(cot, 1)
+    first.start()
     for load in loads:
         load.wait()
 
@@ -506,11 +541,11 @@
 
     def norm_back(start):
         if start == 0:
-            mirrored.wait()
+            first.wait()
         for start in (start,):
             own = slice(start, start + step)
             values = attended[own]
-            mid_grad = pair_add(mid_ref[own], other[own])
+            mid_grad = pair_add(mid[own], other[own])
             scale = lax.rsqrt(jnp.mean(values * values, axis=-1, keepdims=True) + EPSILON)
             normed = values * scale
             scaled = mid_grad * gain_ref[...]
@@ -531,38 +566,6 @@
         for distance in range(1, blocks):
             ctx_copy(distance, blk).start()
 
-    strip = down.shape[1]
-    strips = features // strip
-    units = down.shape[2]
-    down_at, act_at = down_ref.shape[1] - units, right_ref.shape[1] - units
-    second = pltpu.make_async_remote_copy(
-        src_ref=cot,
-        dst_ref=other,
-        send_sem=heads_sem.at[2],
-        recv_sem=heads_sem.at[3],
-        device_id=mirror,
-        device_id_type=MESH,
-    )
-
-    def strip_copy(number):
-        slot = lax.rem(number, 2)
-        return pltpu.make_async_copy(
-            down_ref.at[pl.ds(pl.multiple_of(number * strip, strip), strip), pl.ds(down_at, units)],
-            down.at[slot],
-            down_sem.at[slot],
-        )
-
-    def strip_step(number):
-        strip_copy(number).wait()
-
-        @pl.when(number + 1 < strips)
-        def _():
-            strip_copy(number + 1).start()
-
-        columns = pl.ds(pl.multiple_of(number * strip, strip), strip)
-        product = dot_rows(right_ref[:, act_at:], down[lax.rem(number, 2)])
-        cot[:, columns] = product.astype(jnp.bfloat16)
-
     def one_head(head):
         attend_back_head(part, tile, factor, head, ends, packed, grads, out, key_sum, value_sum)
 
@@ -629,17 +632,17 @@
             out_copy(kind, distance, blk).wait_send()
 
 
-def middle(
-    groups, doc_ends, mid, attended, cot, gain, weight, packed, down, call, marks, width=256, slots=10
-):
-    fold, lefts, rights, shape, scratch, cost = fold_setting(groups, width, slots, 0)
+def middle(lefts, rights, doc_ends, attended, cot, gain, weight, packed, mid, feed, call, marks, width=256, slots=10):
+    each = rights.shape[2]
+    sizes = [jax.ShapeDtypeStruct((1, each), jnp.bfloat16)] * 3
+    fold, shape, scratch, cost = fold_layout(lefts, [sizes[:2], sizes[2:]], width, slots, 0)
     blocks = lax.axis_size("blk")
-    rows, features = mid.shape
+    rows, features = attended.shape
     length, columns = packed.shape
     part = columns // 3
     tile = 256 if length % 256 == 0 else attention_tile(length)
     turns = fold[2] + fold[6][-1]
-    assert marks[0] + 3 + STRIPS < turns and marks[0] + 3 < marks[1]
+    assert marks[0] + 3 + STRIPS < turns and marks[0] < marks[1] - 3
     assert marks[1] + part // HEAD + 2 * 3 * (blocks - 1) < turns
     vmem, anywhere = (pl.BlockSpec(memory_space=space) for space in (pltpu.VMEM, pl.ANY))
     low = jnp.bfloat16
@@ -657,12 +660,12 @@
             anywhere,
             anywhere,
             vmem,
-            vmem,
             anywhere,
             anywhere,
             vmem,
             anywhere,
             anywhere,
+            vmem,
             anywhere,
         ],
         out_specs=(vmem,) * 5,
@@ -672,24 +675,25 @@
             pltpu.VMEM(weight.shape, low),
             pltpu.VMEM(packed.shape, low),
             pltpu.SemaphoreType.DMA((4,)),
-            pltpu.VMEM(mid.shape, low),
+            pltpu.VMEM(cot.shape, low),
             pltpu.VMEM((blocks, rows, part), low),
             pltpu.VMEM((length, part), low),
             pltpu.VMEM((length, columns), low),
             pltpu.VMEM((length, HEAD), jnp.float32),
             pltpu.VMEM((length, HEAD), jnp.float32),
-            pltpu.SemaphoreType.DMA((4,)),
+            pltpu.SemaphoreType.DMA((2, 2)),
             pltpu.SemaphoreType.DMA((2, blocks)),
             pltpu.SemaphoreType.DMA((2, 3, blocks)),
-            pltpu.VMEM((2, features // STRIPS, groups[-1][1][0].shape[1]), low),
+            pltpu.VMEM((2, features // STRIPS, each), low),
             pltpu.SemaphoreType.DMA((2,)),
             pltpu.SemaphoreType.REGULAR,
             *scratch,
         ],
         compiler_params=remote_params(call),
         cost_estimate=cost,
-    )(doc_ends, *lefts, rights, mid, attended, cot, gain[None], weight, packed, down)
-    return unstacked(groups, folded), resid, gain_grad[0], moved, result
+    )(doc_ends, *lefts, rights, attended, cot, gain[None], weight, packed, mid, feed)
+    shares = [folded[:, number * each : (number + 1) * each] for number in range(3)]
+    return shares, resid, gain_grad[0], moved, result
 
 
 def last_kernel(
@@ -847,6 +851,42 @@
     return unstacked(groups, folded), hidden_grad, memory_grad, gain_grads
 
 
+def feed_kernel(mid_ref, cot_ref, gate_ref, up_ref, down_ref, out_ref):
+    gate = plain_dot(mid_ref[...], gate_ref[...])
+    upward = plain_dot(mid_ref[...], up_ref[...])
+    act_grad = plain_dot(cot_ref[...], down_ref[...])
+    sigma = jax.nn.sigmoid(gate)
+    silu_gate = gate * sigma
+    gate_grad = act_grad * upward * sigma * (1.0 + gate * (1.0 - sigma))
+    out_ref[0] = gate_grad.astype(jnp.bfloat16)
+    out_ref[1] = (act_grad * silu_gate).astype(jnp.bfloat16)
+    out_ref[2] = (silu_gate * upward).astype(jnp.bfloat16)
+
+
+def feed(mid, cot, full, width=256):
+    rows, features = mid.shape
+    units = full.shape[1] // 3
+    steps = units // width
+    whole = pl.BlockSpec((rows, features), lambda i: (0, 0))
+    return pl.pallas_call(
+        feed_kernel,
+        grid=(steps,),
+        out_shape=jax.ShapeDtypeStruct((3, rows, units), jnp.bfloat16),
+        in_specs=[whole, whole]
+        + [
+            pl.BlockSpec((features, width), lambda i, number=number: (0, number * steps + i))
+            for number in range(3)
+        ],
+        out_specs=pl.BlockSpec((3, rows, width), lambda i: (0, 0, i)),
+        compiler_params=pltpu.CompilerParams(vmem_limit_bytes=40 * 1024 * 1024),
+        cost_estimate=pl.CostEstimate(
+            flops=6 * rows * features * units,
+            bytes_accessed=6 * features * units,
+            transcendentals=rows * units,
+        ),
+    )(mid, cot, full, full, full)
+
+
 def by_head(array):
     return array.reshape(array.shape[0], -1, HEAD).transpose(1, 0, 2)
 
@@ -962,30 +1002,21 @@
     )
     mid_low = rms_scale(attended, mid_gain).astype(jnp.bfloat16)
 
-    full_gate = ffn_full[:, :padded]
-    full_up = ffn_full[:, padded : 2 * padded]
-    full_down = ffn_full[:, 2 * padded :]
-    gate = plain_dot(mid_low, full_gate)
-    upward = plain_dot(mid_low, full_up)
-    sigma = jax.nn.sigmoid(gate)
-    silu_gate = gate * sigma
-    act_low = (silu_gate * upward).astype(jnp.bfloat16)
-    act_grad = plain_dot(cotangent, full_down)
-    gate_grad_low = (act_grad * upward * sigma * (1.0 + gate * (1.0 - sigma))).astype(jnp.bfloat16)
-    up_grad_low = (act_grad * silu_gate).astype(jnp.bfloat16)
-    mid_part = dot_rows(gate_grad_low, full_gate) + dot_rows(up_grad_low, full_up)
+    rights = feed(mid_low, cotangent, ffn_full)
+    full_gate, full_up, full_down = (ffn_full[:, i * padded : (i + 1) * padded] for i in range(3))
+    mid_part = dot_rows(rights[0], full_gate) + dot_rows(rights[1], full_up)
     mid_part = mid_part.astype(jnp.bfloat16)
-    products = [(mid_low.T, [gate_grad_low, up_grad_low]), (cot_turned, [act_low])]
     if spread:
         shares, attended_grad, mid_gain_grad, moved, output = middle(
-            products,
+            (mid_low.T, cot_turned),
+            rights,
             doc_ends,
-            mid_part,
             attended,
             cotangent,
             mid_gain,
             full_output,
             packed,
+            mid_part,
             ffn_full,
             0,
             MARKS,
@@ -995,7 +1026,11 @@
             moved[:, i * width : (i + 1) * width] for i in range(3)
         )
     else:
-        shares = fold_products(products, 0)
+        gate_grad_low, up_grad_low, act_low = rights[0], rights[1], rights[2]
+        shares = fold_products(
+            [(mid_low.T, [gate_grad_low, up_grad_low]), (cot_turned, [act_low])], 0
+        )
+        shares = [*shares[0], *shares[1]]
         output = (attended + pair_sum(dot_rows(act_low, full_down))).astype(jnp.bfloat16)
         mid_grad = pair_sum(mid_part)
         attended_norm_grad, mid_gain_grad = jax.vjp(rms_scale, attended, mid_gain)[1](mid_grad)
@@ -1009,7 +1044,7 @@
             jnp.concatenate([key_grad, value_grad], axis=1), "blk", scatter_dimension=0, tiled=True
         )
         key_grad_low, value_grad_low = moved[:, :width], moved[:, width:]
-    (gate_share, up_share), (down_share,) = shares
+    gate_share, up_share, down_share = shares
     normed_part = dot_rows(query_grad_low, full_query).astype(jnp.bfloat16)
     memory_part = (
         dot_rows(key_grad_low, full_key) + dot_rows(value_grad_low, full_value)

time: 822 us -> 814 us (level)
  matrix products: 81 us -> 54.3 us
  Pallas kernels: 373 us -> 394 us
  waiting for transfers between devices: 238 us -> 227 us
    dot_general x6 -> x3, matrix products: 42.6 us -> 13.6 us  [plain_dot(): return jnp.dot(left, right, preferred_element_type=jnp.float32)]
    pallas_call x0 -> x1, Pallas kernels: none -> 20.5 us  [feed(): pl.pallas_call(feed_kernel, grid=(steps,), out_shape=jax.ShapeDtypeStruct...]
    all_gather x1, waiting for transfers between devices: 59.8 us -> 48.7 us  [local(): ffn_full = lax.all_gather(ffn_mine, ('dp', 'blk'), axis=0, tiled=True)]
    unnamed x70 -> x76, local copies, waits for them, and re-layouts: 32.3 us -> 33.8 us
  transfers between devices with their start and end apart: 4 -> 4, of which waited for: 4 -> 4; matrix products, arithmetic and copies ran while one was open for 7% -> 8% of each run, Pallas kernels for 1% -> 1%
where the time goes in v4:
time: 814 us; the launch traced here: 805 us
  Pallas kernels  394 us (48%)
  waiting for transfers between devices  227 us (28%)
  local copies, waits for them, and re-layouts  61.1 us (8%)
  matrix products  54.3 us (7%)
  blocking collectives  27.9 us (3%)
  other arithmetic  19.1 us (2%)
  between operations  14.9 us (2%)
    pallas_call x1, Pallas kernels, middle(): pl.pallas_call(functools.partial(middle_kernel, fold, marks, tile, 1.0 /...  255 us
    pallas_call x1, Pallas kernels, last(): pl.pallas_call(functools.partial(last_kernel, fold, marks), out_shape=(sh...  112 us
    all_gather x1, waiting for transfers between devices, local(): attn_full = lax.all_gather(attn_mine, ('dp', 'blk'), axis=0, tiled=True)  95.2 us
    all_to_all x1, waiting for transfers between devices, to_heads(): moved = lax.all_to_all(packed, 'blk', 0, 0)  67.5 us
    all_gather x1, waiting for transfers between devices, local(): ffn_full = lax.all_gather(ffn_mine, ('dp', 'blk'), axis=0, tiled=True)  48.7 us
    dot_general x6, matrix products, dot_rows(): lax.dot_general(left, right, (((1,), (1,)), ((), ())), preferred_element_...  40.6 us
    unnamed x76, local copies, waits for them, and re-layouts  33.8 us
    all_to_all x1, blocking collectives, swap_blocks(): lax.all_to_all(packed.reshape(blocks, length // blocks, columns), 'blk',...  27.9 us
  transfers between devices with their start and end apart: 4, of which 4 were waited for; matrix products, arithmetic and copies ran while one was open for 8% of the time, Pallas kernels for 1%

profile of v4, /device:TPU:0, one launch (start us, length us, event | category | flops | bytes accessed | tf_op | source)
XLA Modules:
  0.0 805.2 jit_solution(13899278701506195594)
XLA Ops:
  7.3 1.2 copy.31
  8.5 1.1 copy.32
  9.6 1.1 copy.33
  10.7 1.1 copy.34
  12.1 1.0 copy-done.15
  13.4 1.4 copy.29
  14.8 1.4 copy.30
  16.2 1.5 fusion.34
  17.6 95.2 %all-gather.3.cloned.1.call-done = bf16[2048,4224]{0,1:T(8,128)(2,1)} async-done(((bf16[128,4224]{0,1:T(8,128)(2,1)}), bf16[2048,4224]{0,1:T(8,128)(2,1)}) %all-gather.3.cloned.1.call-update) | async-done | bytes 17301520 | tf_op jit(solution)/shard_map/all_gather | solution.py:963
  112.9 0.9 copy.35
  113.7 2.4 copy.27
  116.2 0.4 fusion.20
  117.1 0.8 convert_bitcast_fusion.1
  117.9 4.4 fusion.38
  122.4 4.6 fusion.41
  127.1 4.6 fusion.35
  131.9 1.7 pad_maximum_fusion
  133.6 5.0 all-to-all-start
  138.8 67.5 %all-to-all-done = bf16[4,384,768]{2,1,0:T(8,128)(2,1)S(1)} async-done(((bf16[4,384,768]{2,1,0:T(8,128)(2,1)}), bf16[4,384,768]{2,1,0:T(8,128)(2,1)S(1)}, u32[]{:S(2)}, u32[]{:S(2)}) %all-to-all-start) | async-done | bytes 2359328 | tf_op jit(solution)/shard_map/all_to_all | solution.py:336
  206.3 7.6 shard_map.237
  213.9 27.9 %all_to_all.10 = bf16[4,384,256]{2,1,0:T(8,128)(2,1)S(1)} all-to-all(bf16[4,384,256]{2,1,0:T(8,128)(2,1)S(1)} %bitcast.61), channel_id=1, replica_groups=mesh['dp'=4,'blk'=4,'heads'=2] {'blk'}, dimensions={0} | all-to-all | bytes 1572864 | tf_op jit(solution)/shard_map/all_to_all | solution.py:342
  241.9 0.8 copy-done.9
  242.7 5.9 convolution_convert_fusion
  248.6 1.5 collective-permute-start
  250.1 1.6 copy.37
  251.7 4.9 slice.158
  256.6 0.6 stack.40.gains_ref
  257.2 6.5 copy.40.weight_ref
  263.7 1.6 fusion.64.third_left
  265.3 0.7 constant_dynamic-update-slice_fusion.8
  266.1 0.7 constant_dynamic-update-slice_fusion.7
  266.8 0.7 constant_dynamic-update-slice_fusion.6
  267.5 0.7 constant_dynamic-update-slice_fusion.5
  268.2 15.7 %collective-permute-done = bf16[384,2048]{0,1:T(8,128)(2,1)} collective-permute-done((bf16[384,2048]{0,1:T(8,128)(2,1)}, bf16[384,2048]{0,1:T(8,128)(2,1)}, u32[]{:S(2)}, u32[]{:S(2)}) %collective-permute-start) | collective-permute-done | bytes 1572896 | tf_op jit(solution)/shard_map/ppermute | solution.py:44
  283.9 4.9 fusion.54
  288.9 3.6 copy.39.attended_ref
  292.5 2.4 multiply_reduce_fusion
  294.9 0.5 copy-done.4
  295.5 1.5 multiply_convert_fusion
  297.0 1.7 copy.38.mid_ref
  298.7 3.5 fusion.73.first_left
  302.2 48.7 %all-gather.5.cloned.1.call-done.gate_ref.up_ref.down_ref.feed_ref = bf16[2048,8448]{1,0:T(8,128)(2,1)} async-done(((bf16[128,8448]{1,0:T(8,128)(2,1)}), bf16[2048,8448]{1,0:T(8,128)(2,1)}) %all-gather.5.cloned.1.call-update) | async-done | bytes 34603024 | tf_op jit(solution)/shard_map/all_gather | solution.py:973
  350.9 20.5 %shard_map.238.right_ref = bf16[3,384,2816]{2,1,0:T(8,128)(2,1)S(1)} custom-call(bf16[384,2048]{1,0:T(8,128)(2,1)S(1)} %copy.38.mid_ref, bf16[384,2048]{1,0:T(8,128)(2,1)S(1)} %copy-done.1, bf16[2048,8448]{1,0:T(8,128)(2,1)} %all-gather.5.cloned.1.call-done.gate_ref.up_ref.down_ref.feed_ref, ...), custom_call_target="tpu_custom_call" | custom-call | flops 13287555072 | bytes 34603008 | tf_op jit(solution)/shard_map/pallas_call | solution.py:871
  371.4 9.9 %fusion = f32[384,2048]{1,0:T(8,128)S(1)} fusion(bf16[2048,8448]{1,0:T(8,128)(2,1)} %all-gather.5.cloned.1.call-done.gate_ref.up_ref.down_ref.feed_ref, bf16[3,384,2816]{2,1,0:T(8,128)(2,1)S(1)} %shard_map.238.right_ref), kind=kOutput, calls=%fused_computation | convolution fusion | flops 4429185024 | bytes 16842752 | tf_op jit(solution)/shard_map/dot_general | solution.py:31
  381.3 10.1 %add_convert_fusion.1.mid = bf16[384,2048]{1,0:T(8,128)(2,1)} fusion(f32[384,2048]{1,0:T(8,128)S(1)} %fusion, bf16[2048,8448]{1,0:T(8,128)(2,1)} %all-gather.5.cloned.1.call-done.gate_ref.up_ref.down_ref.feed_ref, bf16[3,384,2816]{2,1,0:T(8,128)(2,1)S(1)} %shard_map.238.right_ref), kind=kOutput, calls=%fused_computation.36 | convolution fusion | flops 4430757888 | bytes 18415616 | tf_op jit(solution)/shard_map/dot_general | solution.py:31
  391.4 254.5 %shard_map.239 = (f32[128,8448]{1,0:T(8,128)}, f32[384,2048]{1,0:T(8,128)}, f32[1,2048]{1,0:T(1,128)}, bf16[384,3072]{1,0:T(8,128)(2,1)}, bf16[384,2048]{1,0:T(8,128)(2,1)}) custom-call(s32[4]{0:T(128)} %bitcast.63, bf16[2048,384]{1,0:T(8,128)(2,1)} %fusion.73.first_left, bf16[2048,384]{1,0:T(8,128)(2,1)} %bitcast.64, bf16[3,384,2816]{2,1,0:T(8,128)(2,1)} %copy-done, ...), custom_call_target="tpu_custom_call" | custom-call | flops 13287555072 | bytes 138412032 | tf_op jit(solution)/shard_map/pallas_call | solution.py:649
  645.9 4.4 fusion.8
  650.3 5.2 fusion.30.normed_part
  655.5 5.3 add_convert_fusion.memory_part
  661.0 1.7 copy-done.21
  662.6 1.2 copy-done.13
  663.8 1.7 copy.41
  665.4 111.6 %shard_map.240 = (f32[128,4096]{1,0:T(8,128)}, f32[384,2048]{1,0:T(8,128)}, f32[384,2048]{1,0:T(8,128)}, f32[8,128]{1,0:T(8,128)}) custom-call(bf16[2048,384]{1,0:T(8,128)(2,1)} %bitcast.65, bf16[2048,384]{1,0:T(8,128)(2,1)} %get-tuple-element.34.second_left, bf16[2048,384]{1,0:T(8,128)(2,1)} %fusion.64.third_left, bf16[1,384,4096]{2,1,0:T(8,128)(2,1)} %bitcast.73, ...), custom_call_target="tpu_custom_call" | custom-call | flops 6442450944 | bytes 67108864 | tf_op jit(solution)/shard_map/pallas_call | solution.py:824
  777.1 2.9 fusion.68
  780.0 1.3 slice_bitcast_fusion.8
  781.3 3.6 fusion.67
  784.9 2.9 copy.42
  787.8 1.5 copy.43
  789.3 1.5 copy.44
  790.9 1.1 copy.57
  792.0 1.3 copy-done.12
  793.3 1.7 copy.58
  795.0 1.4 copy-done.11
  796.3 1.7 copy.59
  (68 shorter events, 1.8 us)
Async XLA Ops:
  7.2 4.8 copy-start.24
  7.2 4.8 copy-start.23
  7.2 4.8 copy-start.22
  7.2 5.9 copy-start.18
  7.2 105.6 %all-gather.3.cloned.1.call-start = ((), (), s32[]{:S(2)}) async-start(), calls=%async_computation.2 | async-start | bytes 18382848 | tf_op jit(solution)/shard_map/all_gather | solution.py:963
  12.0 1.0 copy-start.15
  13.1 337.8 %all-gather.5.cloned.1.call-start = ((), (), s32[]{:S(2)}) async-start(), calls=%async_computation.3 | async-start | bytes 36765696 | tf_op jit(solution)/shard_map/all_gather | solution.py:973
  17.6 95.2 %copy-start.16 = (bf16[384,2048]{1,0:T(8,128)(2,1)S(1)}, bf16[384,2048]{1,0:T(8,128)(2,1)}, u32[]{:S(2)}) copy-start(bf16[384,2048]{1,0:T(8,128)(2,1)} %memory_ref.1) | copy-start | bytes 4718596
  113.7 8.6 %copy-start.5 = (bf16[384,2048]{0,1:T(8,128)(2,1)}, bf16[384,2048]{0,1:T(8,128)(2,1)S(1)}, u32[]{:S(2)}) copy-start(bf16[384,2048]{0,1:T(8,128)(2,1)S(1)} %copy.35) | copy-start | bytes 4718596
  116.2 10.9 %copy-start.7 = (bf16[384,2048]{0,1:T(8,128)(2,1)}, bf16[384,2048]{0,1:T(8,128)(2,1)S(1)}, u32[]{:S(2)}) copy-start(bf16[384,2048]{0,1:T(8,128)(2,1)S(1)} %copy.27) | copy-start | bytes 4718596
  117.8 180.9 %copy-start.19 = (f32[1,2048]{1,0:T(1,128)}, f32[1,2048]{1,0:T(1,128)S(1)}, u32[]{:S(2)}) copy-start(f32[1,2048]{1,0:T(1,128)S(1)} %get-tuple-element.81.gain_ref) | copy-start | bytes 24580
  133.6 5.0 copy-start.25
  133.6 72.7 %all-to-all-start = ((bf16[4,384,768]{2,1,0:T(8,128)(2,1)}), bf16[4,384,768]{2,1,0:T(8,128)(2,1)S(1)}, u32[]{:S(2)}, u32[]{:S(2)}) async-start(bf16[4,384,768]{2,1,0:T(8,128)(2,1)} %pad_maximum_fusion), calls=%async_computation | async-start | bytes 4718592 | tf_op jit(solution)/shard_map/all_to_all | solution.py:336
  138.8 75.1 %copy-start.3 = (s32[4,1]{0,1:T(1,128)}, s32[4,1]{0,1:T(1,128)S(1)}, u32[]{:S(2)}) copy-start(s32[4,1]{0,1:T(1,128)S(1)} %reduce-window.9) | copy-start | bytes 52
  206.3 7.6 copy-start.2
  241.9 0.9 copy-start.9
  242.7 7.4 copy-start.1
  248.6 35.3 %collective-permute-start = (bf16[384,2048]{0,1:T(8,128)(2,1)}, bf16[384,2048]{0,1:T(8,128)(2,1)}, u32[]{:S(2)}, u32[]{:S(2)}) collective-permute-start(bf16[384,2048]{0,1:T(8,128)(2,1)} %convolution_convert_fusion), channel_id=1, source_target_pairs={{0,1},{1,0},{2,3},{3,2},{4,5},{5,4},{6,7},{7,6},{8,9},{9,8},{10,11... | collective-permute-start | bytes 4718600 | tf_op jit(solution)/shard_map/ppermute | solution.py:44
  257.2 6.5 copy-start.6
  263.7 1.6 copy-start.10
  263.7 20.2 %copy-start.8 = (bf16[384,2048]{0,1:T(8,128)(2,1)S(1)}, bf16[384,2048]{0,1:T(8,128)(2,1)}, u32[]{:S(2)}) copy-start(bf16[384,2048]{0,1:T(8,128)(2,1)} %copy-done.7) | copy-start | bytes 4718596
  292.5 3.0 copy-start.4
  371.4 9.9 %copy-start = (bf16[3,384,2816]{2,1,0:T(8,128)(2,1)}, bf16[3,384,2816]{2,1,0:T(8,128)(2,1)S(1)}, u32[]{:S(2)}) copy-start(bf16[3,384,2816]{2,1,0:T(8,128)(2,1)S(1)} %shard_map.238.right_ref) | copy-start | bytes 19464196
  645.9 4.4 copy-start.14
  655.5 5.3 copy-start.20
  660.8 3.0 copy-start.13
  661.0 1.7 copy-start.21
  789.3 1.5 copy-start.17
  790.9 2.5 copy-start.12
  793.3 3.0 copy-start.11
Sparse Core Ops, SparseCore 0:
  13.2 99.6 all-gather.2
  114.4 236.4 all-gather.4

commit v5 on v4

--- a/solution.py
+++ b/solution.py
@@ -851,16 +851,29 @@
     return unstacked(groups, folded), hidden_grad, memory_grad, gain_grads
 
 
-def feed_kernel(mid_ref, cot_ref, gate_ref, up_ref, down_ref, out_ref):
+def feed_kernel(mid_ref, cot_ref, gate_ref, up_ref, down_ref, out_ref, grad_ref, total):
     gate = plain_dot(mid_ref[...], gate_ref[...])
     upward = plain_dot(mid_ref[...], up_ref[...])
     act_grad = plain_dot(cot_ref[...], down_ref[...])
     sigma = jax.nn.sigmoid(gate)
     silu_gate = gate * sigma
     gate_grad = act_grad * upward * sigma * (1.0 + gate * (1.0 - sigma))
-    out_ref[0] = gate_grad.astype(jnp.bfloat16)
-    out_ref[1] = (act_grad * silu_gate).astype(jnp.bfloat16)
+    gate_low = gate_grad.astype(jnp.bfloat16)
+    up_low = (act_grad * silu_gate).astype(jnp.bfloat16)
+    out_ref[0] = gate_low
+    out_ref[1] = up_low
     out_ref[2] = (silu_gate * upward).astype(jnp.bfloat16)
+    step = pl.program_id(0)
+
+    @pl.when(step == 0)
+    def _():
+        total[...] = jnp.zeros_like(total)
+
+    total[...] += dot_rows(gate_low, gate_ref[...]) + dot_rows(up_low, up_ref[...])
+
+    @pl.when(step == pl.num_programs(0) - 1)
+    def _():
+        grad_ref[...] = total[...].astype(jnp.bfloat16)
 
 
 def feed(mid, cot, full, width=256):
@@ -871,16 +884,20 @@
     return pl.pallas_call(
         feed_kernel,
         grid=(steps,),
-        out_shape=jax.ShapeDtypeStruct((3, rows, units), jnp.bfloat16),
+        out_shape=(
+            jax.ShapeDtypeStruct((3, rows, units), jnp.bfloat16),
+            jax.ShapeDtypeStruct((rows, features), jnp.bfloat16),
+        ),
         in_specs=[whole, whole]
         + [
             pl.BlockSpec((features, width), lambda i, number=number: (0, number * steps + i))
             for number in range(3)
         ],
-        out_specs=pl.BlockSpec((3, rows, width), lambda i: (0, 0, i)),
+        out_specs=(pl.BlockSpec((3, rows, width), lambda i: (0, 0, i)), whole),
+        scratch_shapes=[pltpu.VMEM((rows, features), jnp.float32)],
         compiler_params=pltpu.CompilerParams(vmem_limit_bytes=40 * 1024 * 1024),
         cost_estimate=pl.CostEstimate(
-            flops=6 * rows * features * units,
+            flops=10 * rows * features * units,
             bytes_accessed=6 * features * units,
             transcendentals=rows * units,
         ),
@@ -1002,10 +1019,8 @@
     )
     mid_low = rms_scale(attended, mid_gain).astype(jnp.bfloat16)
 
-    rights = feed(mid_low, cotangent, ffn_full)
-    full_gate, full_up, full_down = (ffn_full[:, i * padded : (i + 1) * padded] for i in range(3))
-    mid_part = dot_rows(rights[0], full_gate) + dot_rows(rights[1], full_up)
-    mid_part = mid_part.astype(jnp.bfloat16)
+    rights, mid_part = feed(mid_low, cotangent, ffn_full)
+    full_down = ffn_full[:, 2 * padded :]
     if spread:
         shares, attended_grad, mid_gain_grad, moved, output = middle(
             (mid_low.T, cot_turned),

time: 814 us -> 824 us (1.012)
  Pallas kernels: 394 us -> 421 us
  matrix products: 54.3 us -> 34.3 us
    pallas_call x1, Pallas kernels: 20.5 us -> 47.4 us  [feed(): pl.pallas_call(feed_kernel, grid=(steps,), out_shape=(jax.ShapeDtypeStruc...]
    dot_general x6 -> x4, matrix products: 40.6 us -> 20.7 us  [dot_rows(): lax.dot_general(left, right, (((1,), (1,)), ((), ())), preferred_element_...]
    unnamed x76 -> x78, local copies, waits for them, and re-layouts: 33.8 us -> 37.5 us
where the time goes in v5:
time: 824 us; the launch traced here: 815 us
  Pallas kernels  421 us (51%)
  waiting for transfers between devices  227 us (28%)
  local copies, waits for them, and re-layouts  64.8 us (8%)
  matrix products  34.3 us (4%)
  blocking collectives  27.8 us (3%)
  other arithmetic  19.2 us (2%)
  between operations  14.9 us (2%)
    pallas_call x1, Pallas kernels, middle(): pl.pallas_call(functools.partial(middle_kernel, fold, marks, tile, 1.0 /...  255 us
    pallas_call x1, Pallas kernels, last(): pl.pallas_call(functools.partial(last_kernel, fold, marks), out_shape=(sh...  111 us
    all_gather x1, waiting for transfers between devices, local(): attn_full = lax.all_gather(attn_mine, ('dp', 'blk'), axis=0, tiled=True)  95.2 us
    all_to_all x1, waiting for transfers between devices, to_heads(): moved = lax.all_to_all(packed, 'blk', 0, 0)  67.4 us
    all_gather x1, waiting for transfers between devices, local(): ffn_full = lax.all_gather(ffn_mine, ('dp', 'blk'), axis=0, tiled=True)  48.8 us
    pallas_call x1, Pallas kernels, feed(): pl.pallas_call(feed_kernel, grid=(steps,), out_shape=(jax.ShapeDtypeStruc...  47.4 us
    unnamed x78, local copies, waits for them, and re-layouts  37.5 us
    all_to_all x1, blocking collectives, swap_blocks(): lax.all_to_all(packed.reshape(blocks, length // blocks, columns), 'blk',...  27.8 us
  transfers between devices with their start and end apart: 4, of which 4 were waited for; matrix products, arithmetic and copies ran while one was open for 8% of the time, Pallas kernels for 1%

profile of v5, /device:TPU:0, one launch (start us, length us, event | category | flops | bytes accessed | tf_op | source)
XLA Modules:
  0.0 815.4 jit_solution(9032921660200746583)
XLA Ops:
  7.3 1.1 copy.31
  8.4 1.2 copy.32
  9.6 1.1 copy.33
  10.7 1.1 copy.34
  12.1 1.0 copy-done.16
  13.4 1.4 copy.29
  14.8 1.4 copy.30
  16.2 1.5 fusion.28
  17.6 95.2 %all-gather.3.cloned.1.call-done = bf16[2048,4224]{0,1:T(8,128)(2,1)} async-done(((bf16[128,4224]{0,1:T(8,128)(2,1)}), bf16[2048,4224]{0,1:T(8,128)(2,1)}) %all-gather.3.cloned.1.call-update) | async-done | bytes 17301520 | tf_op jit(solution)/shard_map/all_gather | solution.py:980
  112.9 0.9 copy.35
  113.7 2.4 copy.27
  116.2 0.4 fusion.16
  117.1 0.8 convert_bitcast_fusion.1
  117.9 4.4 fusion.32
  122.4 4.6 fusion.35
  127.1 4.5 fusion.29
  131.8 1.7 pad_maximum_fusion
  133.5 5.1 all-to-all-start
  138.8 67.4 %all-to-all-done = bf16[4,384,768]{2,1,0:T(8,128)(2,1)S(1)} async-done(((bf16[4,384,768]{2,1,0:T(8,128)(2,1)}), bf16[4,384,768]{2,1,0:T(8,128)(2,1)S(1)}, u32[]{:S(2)}, u32[]{:S(2)}) %all-to-all-start) | async-done | bytes 2359328 | tf_op jit(solution)/shard_map/all_to_all | solution.py:336
  206.3 7.6 shard_map.237
  213.9 27.8 %all_to_all.10 = bf16[4,384,256]{2,1,0:T(8,128)(2,1)S(1)} all-to-all(bf16[4,384,256]{2,1,0:T(8,128)(2,1)S(1)} %bitcast.55), channel_id=1, replica_groups=mesh['dp'=4,'blk'=4,'heads'=2] {'blk'}, dimensions={0} | all-to-all | bytes 1572864 | tf_op jit(solution)/shard_map/all_to_all | solution.py:342
  241.8 0.8 copy-done.10
  242.7 5.9 convolution_convert_fusion
  248.5 1.5 collective-permute-start
  250.1 1.6 copy.37
  251.7 4.9 slice.146
  256.5 0.6 stack.40.gains_ref
  257.1 6.5 copy.40.weight_ref
  263.7 1.6 fusion.58.third_left
  265.3 0.7 constant_dynamic-update-slice_fusion.8
  266.0 0.7 constant_dynamic-update-slice_fusion.7
  266.7 0.7 constant_dynamic-update-slice_fusion.6
  267.5 0.7 constant_dynamic-update-slice_fusion.5
  268.2 15.7 %collective-permute-done = bf16[384,2048]{0,1:T(8,128)(2,1)} collective-permute-done((bf16[384,2048]{0,1:T(8,128)(2,1)}, bf16[384,2048]{0,1:T(8,128)(2,1)}, u32[]{:S(2)}, u32[]{:S(2)}) %collective-permute-start) | collective-permute-done | bytes 1572896 | tf_op jit(solution)/shard_map/ppermute | solution.py:44
  283.8 5.0 fusion.48
  288.8 3.6 copy.39.attended_ref
  292.4 2.4 multiply_reduce_fusion
  294.9 0.5 copy-done.5
  295.4 1.5 multiply_convert_fusion
  296.9 1.7 copy.38.mid_ref
  298.7 3.5 fusion.67.first_left
  302.1 48.8 %all-gather.5.cloned.1.call-done.gate_ref.up_ref.down_ref.feed_ref = bf16[2048,8448]{1,0:T(8,128)(2,1)} async-done(((bf16[128,8448]{1,0:T(8,128)(2,1)}), bf16[2048,8448]{1,0:T(8,128)(2,1)}) %all-gather.5.cloned.1.call-update) | async-done | bytes 34603024 | tf_op jit(solution)/shard_map/all_gather | solution.py:990
  350.9 47.4 %shard_map.238 = (bf16[3,384,2816]{2,1,0:T(8,128)(2,1)S(1)}, bf16[384,2048]{1,0:T(8,128)(2,1)S(1)}) custom-call(bf16[384,2048]{1,0:T(8,128)(2,1)S(1)} %copy.38.mid_ref, bf16[384,2048]{1,0:T(8,128)(2,1)S(1)} %copy-done, bf16[2048,8448]{1,0:T(8,128)(2,1)} %all-gather.5.cloned.1.call-done.gate_ref.up_ref.down_ref.feed_ref, ...), custom_call_target="tpu_custom_call" | custom-call | flops 22145925120 | bytes 34603008 | tf_op jit(solution)/shard_map/pallas_call | solution.py:884
  398.3 2.6 copy-done.2
  400.9 1.1 copy-done.3
  402.1 254.7 %shard_map.239 = (f32[128,8448]{1,0:T(8,128)}, f32[384,2048]{1,0:T(8,128)}, f32[1,2048]{1,0:T(1,128)}, bf16[384,3072]{1,0:T(8,128)(2,1)}, bf16[384,2048]{1,0:T(8,128)(2,1)}) custom-call(s32[4]{0:T(128)} %bitcast.57, bf16[2048,384]{1,0:T(8,128)(2,1)} %fusion.67.first_left, bf16[2048,384]{1,0:T(8,128)(2,1)} %bitcast.58, bf16[3,384,2816]{2,1,0:T(8,128)(2,1)} %copy-done.2, ...), custom_call_target="tpu_custom_call" | custom-call | flops 13287555072 | bytes 138412032 | tf_op jit(solution)/shard_map/pallas_call | solution.py:649
  656.8 4.4 fusion.4
  661.2 5.2 fusion.24.normed_part
  666.4 5.3 add_convert_fusion.memory_part
  671.9 1.7 copy-done.22
  673.5 1.2 copy-done.14
  674.7 1.7 copy.41
  676.4 110.9 %shard_map.240 = (f32[128,4096]{1,0:T(8,128)}, f32[384,2048]{1,0:T(8,128)}, f32[384,2048]{1,0:T(8,128)}, f32[8,128]{1,0:T(8,128)}) custom-call(bf16[2048,384]{1,0:T(8,128)(2,1)} %bitcast.59, bf16[2048,384]{1,0:T(8,128)(2,1)} %get-tuple-element.38.second_left, bf16[2048,384]{1,0:T(8,128)(2,1)} %fusion.58.third_left, bf16[1,384,4096]{2,1,0:T(8,128)(2,1)} %bitcast.67, ...), custom_call_target="tpu_custom_call" | custom-call | flops 6442450944 | bytes 67108864 | tf_op jit(solution)/shard_map/pallas_call | solution.py:824
  787.3 2.9 fusion.62
  790.2 1.3 slice_bitcast_fusion.4
  791.5 3.6 fusion.61
  795.1 2.9 copy.42
  798.0 1.5 copy.43
  799.5 1.5 copy.44
  801.1 1.1 copy.57
  802.2 1.3 copy-done.13
  803.5 1.7 copy.58
  805.2 1.4 copy-done.12
  806.5 1.7 copy.59
  (68 shorter events, 1.8 us)
Async XLA Ops:
  7.2 4.8 copy-start.25
  7.2 4.8 copy-start.24
  7.2 4.8 copy-start.23
  7.2 105.6 %all-gather.3.cloned.1.call-start = ((), (), s32[]{:S(2)}) async-start(), calls=%async_computation.2 | async-start | bytes 18382848 | tf_op jit(solution)/shard_map/all_gather | solution.py:980
  8.4 4.7 copy-start.19
  12.0 1.0 copy-start.16
  13.1 337.8 %all-gather.5.cloned.1.call-start = ((), (), s32[]{:S(2)}) async-start(), calls=%async_computation.3 | async-start | bytes 36765696 | tf_op jit(solution)/shard_map/all_gather | solution.py:990
  17.6 95.2 %copy-start.17 = (bf16[384,2048]{1,0:T(8,128)(2,1)S(1)}, bf16[384,2048]{1,0:T(8,128)(2,1)}, u32[]{:S(2)}) copy-start(bf16[384,2048]{1,0:T(8,128)(2,1)} %memory_ref.1) | copy-start | bytes 4718596
  113.7 8.6 %copy-start.6 = (bf16[384,2048]{0,1:T(8,128)(2,1)}, bf16[384,2048]{0,1:T(8,128)(2,1)S(1)}, u32[]{:S(2)}) copy-start(bf16[384,2048]{0,1:T(8,128)(2,1)S(1)} %copy.35) | copy-start | bytes 4718596
  116.2 10.8 %copy-start.8 = (bf16[384,2048]{0,1:T(8,128)(2,1)}, bf16[384,2048]{0,1:T(8,128)(2,1)S(1)}, u32[]{:S(2)}) copy-start(bf16[384,2048]{0,1:T(8,128)(2,1)S(1)} %copy.27) | copy-start | bytes 4718596
  117.8 180.8 %copy-start.20 = (f32[1,2048]{1,0:T(1,128)}, f32[1,2048]{1,0:T(1,128)S(1)}, u32[]{:S(2)}) copy-start(f32[1,2048]{1,0:T(1,128)S(1)} %get-tuple-element.85.gain_ref) | copy-start | bytes 24580
  133.5 5.1 copy-start.26
  133.5 72.8 %all-to-all-start = ((bf16[4,384,768]{2,1,0:T(8,128)(2,1)}), bf16[4,384,768]{2,1,0:T(8,128)(2,1)S(1)}, u32[]{:S(2)}, u32[]{:S(2)}) async-start(bf16[4,384,768]{2,1,0:T(8,128)(2,1)} %pad_maximum_fusion), calls=%async_computation | async-start | bytes 4718592 | tf_op jit(solution)/shard_map/all_to_all | solution.py:336
  138.8 75.1 %copy-start.4 = (s32[4,1]{0,1:T(1,128)}, s32[4,1]{0,1:T(1,128)S(1)}, u32[]{:S(2)}) copy-start(s32[4,1]{0,1:T(1,128)S(1)} %reduce-window.9) | copy-start | bytes 52
  206.3 7.6 copy-start.1
  241.8 0.9 copy-start.10
  242.7 7.4 copy-start
  248.5 35.3 %collective-permute-start = (bf16[384,2048]{0,1:T(8,128)(2,1)}, bf16[384,2048]{0,1:T(8,128)(2,1)}, u32[]{:S(2)}, u32[]{:S(2)}) collective-permute-start(bf16[384,2048]{0,1:T(8,128)(2,1)} %convolution_convert_fusion), channel_id=1, source_target_pairs={{0,1},{1,0},{2,3},{3,2},{4,5},{5,4},{6,7},{7,6},{8,9},{9,8},{10,11... | collective-permute-start | bytes 4718600 | tf_op jit(solution)/shard_map/ppermute | solution.py:44
  257.1 6.5 copy-start.7
  263.7 1.6 copy-start.11
  263.7 20.1 %copy-start.9 = (bf16[384,2048]{0,1:T(8,128)(2,1)S(1)}, bf16[384,2048]{0,1:T(8,128)(2,1)}, u32[]{:S(2)}) copy-start(bf16[384,2048]{0,1:T(8,128)(2,1)} %copy-done.8) | copy-start | bytes 4718596
  292.4 3.0 copy-start.5
  398.3 2.7 copy-start.2
  400.9 1.1 copy-start.3
  656.8 4.4 copy-start.15
  666.4 5.3 copy-start.21
  671.7 3.0 copy-start.14
  671.9 1.7 copy-start.22
  799.5 1.5 copy-start.18
  801.1 2.5 copy-start.13
  803.5 3.0 copy-start.12
Sparse Core Ops, SparseCore 0:
  13.2 99.6 all-gather.2
  114.4 236.4 all-gather.4
